TPU v7x, 32 devices: a whole 2x2x4 slice. The times are simulated.
32 devices in a mesh: grp: 2 (over x), blk: 16 (over z, y, core).
Axes of the slice: x: 2, y: 2, z: 4, core: 2. Of those that a mesh axis runs over, the one named last changes fastest.
Arguments:
- theta: bfloat16 [32, 1024, 128], P(('grp', 'blk')), parts along dimension 0, may hold values from -6 to 6
- trial: bfloat16 [2048, 128], P('grp'), parts along dimension 0, may hold values from -0.5 to 0.5
- chol: bfloat16 [64, 128, 16384], P(('grp', 'blk')), parts along dimension 0, may hold values from -0.009765625 to 0.009765625
- fields: float32 [32, 128], P(('grp', 'blk')), parts along dimension 0, may hold values from -6 to 6
- tile_info: int32 [6, 32], P('grp'), parts along dimension 0, may hold values from 0 to 7, as said below
- tile_count: int32 [32], P('grp'), parts along dimension 0, may hold values from 0 to 2
- block_size: int32 [16], P('grp'), parts along dimension 0, may hold values from 96 to 128
Outputs:
- propagated: bfloat16 [32, 1024, 128], P(('grp', 'blk')), parts along dimension 0
- force_bias: float32 [32, 128], P(('grp', 'blk')), parts along dimension 0
There are 2 independent parts, one for each index of `grp`. A program takes and returns all parts, laid end to end along the dimension named above; each array names one. Nothing has to cross between parts.
Inputs may be any that keep to these rules, and one draw needn't show every extreme that they name: `tile_info`: every pair of blocks (P, Q) with |P - Q| <= 1 and every vector range below 1 stand in exactly one live slot; live slots of an owner come first; unused slots hold zeros.
All inputs are finite; a program needn't handle non-finite values.
Results may differ from a plain program's by a relative error of at most 0.0045.
Values may be sent and summed in bfloat16 or wider, within the bound.
No kernel may reach another device: no remote copies, remote signals or barrier semaphores. Data moves between devices by JAX's collectives and lax.ppermute only.
A program may use at most 128 MiB of HBM per device.

v0:
```python
import jax
import jax.numpy as jnp
from jax import lax
from jax.sharding import PartitionSpec as P

BS = 128
NBLOCK = 8
NOCC = 128
GS = 128
TMAX = 2


step_root = 0.25


def per_device(theta, trial, chol, fields, tile_info, tile_count, block_size):
    owners = lax.axis_size("blk")
    owner_index = lax.axis_index("blk")
    walk_local = theta.shape[0]
    walkers = walk_local * owners
    slot_total = owners * TMAX
    nchol = fields.shape[1]
    zero_index = jnp.zeros((), jnp.int32)
    rows_valid = (jnp.arange(BS, dtype=jnp.int32)[None, :] < block_size[:, None]).astype(
        jnp.float32
    )
    slot_ids = jnp.arange(slot_total, dtype=jnp.int32)
    slot_live = (slot_ids % TMAX < tile_count[slot_ids // TMAX]).astype(jnp.float32)
    theta_blocks = theta.reshape(walk_local, NBLOCK, BS * NOCC)
    outgoing = jnp.take(theta_blocks, tile_info[1], axis=1).reshape(
        walk_local, owners, TMAX, BS * NOCC
    )
    received = lax.all_to_all(outgoing, "blk", split_axis=1, concat_axis=0, tiled=True).reshape(
        walkers, TMAX, BS, NOCC
    )
    own_info = lax.dynamic_slice(tile_info, (zero_index, owner_index * TMAX), (3, TMAX))
    own_live = lax.dynamic_slice(slot_live, (owner_index * TMAX,), (TMAX,))
    bias_local = jnp.zeros((walkers, nchol), jnp.float32)
    slot_masks = []
    for slot_index in range(TMAX):
        row_block = own_info[0, slot_index]
        col_block = own_info[1, slot_index]
        slab_index = own_info[2, slot_index]
        trial_rows = lax.dynamic_slice(trial, (row_block * BS, zero_index), (BS, NOCC))
        valid_mask = (
            rows_valid[row_block][:, None] * rows_valid[col_block][None, :] * own_live[slot_index]
        )
        green_block = (
            jnp.einsum(
                "pk,wqk->wpq",
                trial_rows,
                received[:, slot_index],
                preferred_element_type=jnp.float32,
            )
            * valid_mask
        ).astype(jnp.bfloat16)
        bias_term = jnp.einsum(
            "wf,gf->wg",
            green_block.reshape(walkers, BS * BS),
            chol[slot_index],
            preferred_element_type=jnp.float32,
        )
        current = lax.dynamic_slice(bias_local, (zero_index, slab_index * GS), (walkers, GS))
        bias_local = lax.dynamic_update_slice(
            bias_local, current + bias_term, (zero_index, slab_index * GS)
        )
        slot_masks.append(valid_mask)
    bias_all = lax.psum(bias_local, "blk")
    fields_all = lax.all_gather(fields, "blk", axis=0, tiled=True)
    shifted_all = (fields_all - bias_all).astype(jnp.bfloat16)
    own_bias = lax.dynamic_slice(
        bias_all, (owner_index * walk_local, zero_index), (walk_local, nchol)
    )
    operator_list = []
    for slot_index in range(TMAX):
        slab_index = own_info[2, slot_index]
        field_slab = lax.dynamic_slice(shifted_all, (zero_index, slab_index * GS), (walkers, GS))
        operator_block = (
            (
                jnp.dot(field_slab, chol[slot_index], preferred_element_type=jnp.float32)
                * step_root
            ).reshape(walkers, BS, BS)
            * slot_masks[slot_index]
        ).astype(jnp.bfloat16)
        operator_list.append(operator_block)
    stacked = jnp.stack(operator_list).reshape(TMAX, walkers, BS * BS)
    arrived = lax.all_to_all(stacked, "blk", split_axis=1, concat_axis=0, tiled=True).reshape(
        slot_total, walk_local, BS, BS
    )
    selected = jnp.take(theta.reshape(walk_local, NBLOCK, BS, NOCC), tile_info[1], axis=1)
    returned = jnp.einsum(
        "swpq,wsqk->swpk", arrived, selected, preferred_element_type=jnp.float32
    ).reshape(slot_total, walk_local, BS * NOCC)
    placement = (tile_info[0][:, None] == jnp.arange(NBLOCK, dtype=jnp.int32)[None, :]).astype(
        jnp.float32
    ) * slot_live[:, None]
    update = jnp.einsum("sb,swf->wbf", placement, returned, precision=lax.Precision.HIGHEST)
    propagated = (theta.astype(jnp.float32) + update.reshape(walk_local, NBLOCK * BS, NOCC)).astype(
        jnp.bfloat16
    )
    return (propagated, own_bias)


def solution(mesh):
    placed = (
        P(("grp", "blk"), None, None),
        P("grp", None),
        P(("grp", "blk"), None, None),
        P(("grp", "blk"), None),
        P("grp", None),
        P("grp"),
        P("grp"),
    )
    return jax.shard_map(
        per_device,
        mesh=mesh,
        in_specs=placed,
        out_specs=(P(("grp", "blk"), None, None), P(("grp", "blk"), None)),
        check_vma=False,
    )
```

profile of v0, /device:TPU:1, one launch (start us, length us, event | category | flops | bytes accessed | tf_op | source)
XLA Modules:
  0.0 134.1 jit_solution(1629129252744959464)
XLA Ops:
  0.6 0.7 fusion.46
  1.4 0.8 slice_bitcast_fusion.4
  2.3 1.1 reshape.252
  3.3 1.2 gather_fusion
  4.6 0.7 gather.16
  5.3 2.0 %broadcast_select_fusion = bf16[1,16,2,16384]{3,2,0,1:T(2,128)(2,1)} fusion(pred[16,2]{1,0:T(8,128)(4,1)S(1)} %compare_and_fusion, bf16[1,16,2,16384]{3,2,1,0:T(2,128)(2,1)S(1)} %gather.16), kind=kLoop, calls=%fused_computation.22 | loop fusion | flops 524288 | bytes 2097184 | tf_op jit(solution)/shard_map/jit(_take)/select_n | solution.py:30
  7.3 7.3 %all-to-all-start = ((bf16[1,16,2,16384]{3,2,0,1:T(2,128)(2,1)}), bf16[1,16,2,16384]{3,2,0,1:T(2,128)(2,1)S(1)}, u32[]{:S(2)}, u32[]{:S(2)}) async-start(bf16[1,16,2,16384]{3,2,0,1:T(2,128)(2,1)} %broadcast_select_fusion), calls=%async_computation | async-start | bytes 2097152 | tf_op jit(solution)/shard_map/all_to_all | solution.py:33
  25.6 0.7 multiply_multiply_fusion.1
  26.4 0.7 multiply_multiply_fusion
  27.3 21.5 %all-gather = f32[16,1,128]{2,1,0:T(1,128)S(1)} all-gather(f32[1,1,128]{2,1,0:T(1,128)S(1)} %bitcast.121), channel_id=1, replica_groups=mesh['grp'=2,'blk'=16] {'blk'}, dimensions={0}, use_global_device_ids=true | all-gather | bytes 8704 | tf_op jit(solution)/shard_map/all_gather | solution.py:69
  50.5 0.8 reshape.288
  52.6 3.4 %fusion.5 = f32[16,128]{1,0:T(8,128)S(1)} fusion(bf16[2,128,16384]{2,1,0:T(8,128)(2,1)} %param.9, bf16[2,8,128,128]{3,2,1,0:T(8,128)(2,1)S(1)} %bitcast.116), kind=kOutput, calls=%fused_computation.11 | convolution fusion | flops 67108864 | bytes 4726784 | tf_op jit(solution)/shard_map/wf,gf->wg/dot_general | solution.py:57
  55.9 3.4 %fusion.20 = f32[16,128]{1,0:T(8,128)S(1)} fusion(f32[16,128]{1,0:T(8,128)S(1)} %fusion.5, bf16[2,128,16384]{2,1,0:T(8,128)(2,1)} %param.9, bf16[2,8,128,128]{3,2,1,0:T(8,128)(2,1)S(1)} %bitcast.117), kind=kOutput, calls=%fused_computation.29 | convolution fusion | flops 67110912 | bytes 4734976 | tf_op jit(solution)/shard_map/wf,gf->wg/dot_general | solution.py:57
  59.3 29.5 %psum.7 = f32[16,128]{1,0:T(8,128)S(1)} all-reduce(f32[16,128]{1,0:T(8,128)S(1)} %fusion.20), channel_id=1, replica_groups=mesh['grp'=2,'blk'=16] {'blk'}, use_global_device_ids=true, to_apply=%region_0.1 | all-reduce | flops 2048 | bytes 16384 | tf_op jit(solution)/shard_map/psum | solution.py:68
  88.9 2.9 %fusion.2 = bf16[1,16,16384]{2,1,0:T(8,128)(2,1)S(1)} fusion(bf16[16,128]{1,0:T(8,128)(2,1)S(1)} %subtract_convert_fusion, bf16[2,128,16384]{2,1,0:T(8,128)(2,1)} %param.9, f32[16384]{0:T(1024)S(1)} %fusion.32), kind=kOutput, calls=%fused_computation.7 | convolution fusion | flops 67633152 | bytes 4788224 | tf_op jit(solution)/shard_map/dot_general | solution.py:80
  91.7 2.9 %fusion.3 = bf16[1,16,16384]{2,1,0:T(8,128)(2,1)S(1)} fusion(bf16[16,128]{1,0:T(8,128)(2,1)S(1)} %subtract_convert_fusion, bf16[2,128,16384]{2,1,0:T(8,128)(2,1)} %param.9, f32[16384]{0:T(1024)S(1)} %fusion.34), kind=kOutput, calls=%fused_computation.8 | convolution fusion | flops 67633152 | bytes 4788224 | tf_op jit(solution)/shard_map/dot_general | solution.py:80
  94.7 2.1 %copy.26 = bf16[2,16,16384]{2,0,1:T(2,128)(2,1)} copy(bf16[2,16,16384]{2,1,0:T(8,128)(2,1)S(1)} %pad_maximum_fusion) | data formatting | bytes 2097152 | tf_op jit(solution)/shard_map/stack | solution.py:86
  96.8 7.6 %all-to-all-start.1 = ((bf16[2,16,16384]{2,0,1:T(2,128)(2,1)}), bf16[2,16,16384]{2,0,1:T(2,128)(2,1)S(1)}, u32[]{:S(2)}, u32[]{:S(2)}) async-start(bf16[2,16,16384]{2,0,1:T(2,128)(2,1)} %copy.26), calls=%async_computation.1 | async-start | bytes 2097152 | tf_op jit(solution)/shard_map/all_to_all | solution.py:87
  104.4 0.7 gather_fusion.2
  105.7 21.9 %all-to-all-done.1 = bf16[2,16,16384]{2,0,1:T(2,128)(2,1)S(1)} async-done(((bf16[2,16,16384]{2,0,1:T(2,128)(2,1)}), bf16[2,16,16384]{2,0,1:T(2,128)(2,1)S(1)}, u32[]{:S(2)}, u32[]{:S(2)}) %all-to-all-start.1) | async-done | bytes 1048608 | tf_op jit(solution)/shard_map/all_to_all | solution.py:87
  127.5 1.0 copy-done.3
  128.5 1.8 %reshape.248 = bf16[32,128,128]{2,1,0:T(8,128)(2,1)S(1)} reshape(bf16[16,2,1,16384]{3,1,0,2:T(2,128)(2,1)} %bitcast.115) | data formatting | bytes 2097152 | tf_op jit(solution)/shard_map/reshape.6
  130.9 2.4 %convolution_bitcast_fusion = f32[1,8,16384]{2,1,0:T(8,128)S(1)} fusion(f32[4,8,128,128]{3,2,1,0:T(8,128)S(1)} %bitcast.114, f32[32]{0:T(128)S(1)} %compare_convert_fusion, s32[32]{0:T(128)S(1)} %get-tuple-element.6), kind=kOutput, calls=%fused_computation.9 | convolution fusion | flops 50332160 | bytes 2621696 | tf_op jit(solution)/shard_map/sb,swf->wbf/dot_general | solution.py:97
  133.4 0.8 add_convert_fusion
  (42 shorter events, 6.6 us)
Async XLA Ops:
  0.6 50.7 %copy-start = (bf16[1024,128]{1,0:T(8,128)(2,1)S(1)}, bf16[1024,128]{1,0:T(8,128)(2,1)}, u32[]{:S(2)}) copy-start(bf16[1024,128]{1,0:T(8,128)(2,1)} %param.8) | copy-start | bytes 786436
  4.5 10.1 %copy-start.4 = (s32[3,32]{1,0:T(4,128)S(1)}, s32[3,32]{1,0:T(4,128)}, u32[]{:S(2)}) copy-start(s32[3,32]{1,0:T(4,128)} %param.11) | copy-start | bytes 1156
  4.6 17.1 %copy-start.1 = (s32[16]{0:T(128)S(1)}, s32[16]{0:T(128)}, u32[]{:S(2)}) copy-start(s32[16]{0:T(128)} %param.12) | copy-start | bytes 196
  4.6 20.4 %copy-start.5 = (s32[8]{0:T(128)S(1)}, s32[8]{0:T(128)}, u32[]{:S(2)}) copy-start(s32[8]{0:T(128)} %param.13) | copy-start | bytes 100
  4.6 22.7 %copy-start.6 = (f32[1,128]{1,0:T(1,128)S(1)}, f32[1,128]{1,0:T(1,128)}, u32[]{:S(2)}) copy-start(f32[1,128]{1,0:T(1,128)} %param.10) | copy-start | bytes 1540
  7.3 43.3 %all-to-all-start = ((bf16[1,16,2,16384]{3,2,0,1:T(2,128)(2,1)}), bf16[1,16,2,16384]{3,2,0,1:T(2,128)(2,1)S(1)}, u32[]{:S(2)}, u32[]{:S(2)}) async-start(bf16[1,16,2,16384]{3,2,0,1:T(2,128)(2,1)} %broadcast_select_fusion), calls=%async_computation | async-start | bytes 2097152 | tf_op jit(solution)/shard_map/all_to_all | solution.py:33
  94.6 9.8 %copy-start.2 = (bf16[1,1024,128]{2,1,0:T(8,128)(2,1)S(1)}, bf16[1,1024,128]{2,1,0:T(8,128)(2,1)}, u32[]{:S(2)}) copy-start(bf16[1,1024,128]{2,1,0:T(8,128)(2,1)} %param.7) | copy-start | bytes 786436
  96.8 30.8 %all-to-all-start.1 = ((bf16[2,16,16384]{2,0,1:T(2,128)(2,1)}), bf16[2,16,16384]{2,0,1:T(2,128)(2,1)S(1)}, u32[]{:S(2)}, u32[]{:S(2)}) async-start(bf16[2,16,16384]{2,0,1:T(2,128)(2,1)} %copy.26), calls=%async_computation.1 | async-start | bytes 2097152 | tf_op jit(solution)/shard_map/all_to_all | solution.py:87
  127.5 1.0 copy-start.3
where the time goes:
time: 136 us; the launch traced here: 134 us
  blocking collectives  51 us (38%)
  waiting for transfers between devices  21.9 us (16%)
  matrix products  16 us (12%)
  starting transfers between devices  14.9 us (11%)
  local copies, waits for them, and re-layouts  14.1 us (10%)
  between operations  9.73 us (7%)
  other arithmetic  6.45 us (5%)
    psum x1, blocking collectives, per_device(): bias_all = lax.psum(bias_local, 'blk')  29.5 us
    all_to_all x1, waiting for transfers between devices, per_device(): lax.all_to_all(stacked, 'blk', split_axis=1, concat_axis=0, tiled=True)  21.9 us
    all_gather x1, blocking collectives, per_device(): fields_all = lax.all_gather(fields, 'blk', axis=0, tiled=True)  21.5 us
    all_to_all x1, starting transfers between devices, per_device(): lax.all_to_all(stacked, 'blk', split_axis=1, concat_axis=0, tiled=True)  7.59 us
    all_to_all x1, starting transfers between devices, per_device(): lax.all_to_all(outgoing, 'blk', split_axis=1, concat_axis=0, tiled=True)  7.35 us
    dot_general x2, matrix products, per_device(): jnp.einsum('wf,gf->wg', green_block.reshape(walkers, BS * BS), chol[slot_...  6.77 us
    dot_general x2, matrix products, per_device(): jnp.dot(field_slab, chol[slot_index], preferred_element_type=jnp.float32)  5.71 us
  transfers between devices with their start and end apart: 2, of which 1 were waited for; matrix products, arithmetic and copies ran while one was open for 5% of the time, Pallas kernels for 0%

commit v1 on v0

v1 whole, which is shorter than its diff:
```python
import functools

import jax
import jax.numpy as jnp
from jax import lax
from jax.experimental import pallas as pl
from jax.experimental.pallas import tpu as pltpu
from jax.sharding import PartitionSpec as P

STEP_ROOT = 0.25
PIECES = 8
F32 = jnp.float32
BF16 = jnp.bfloat16
LIMIT = 48 * 1024 * 1024
VMEM = pl.BlockSpec(memory_space=pltpu.VMEM)
SMEM = pl.BlockSpec(memory_space=pltpu.SMEM)
ANY = pl.BlockSpec(memory_space=pl.ANY)
NT = (((1,), (1,)), ((), ()))


def pick_kernel(info_ref, theta_ref, out_ref, sem):
    owners, walk, slots = out_ref.shape[:3]
    for o in range(owners):
        for j in range(slots):
            block = info_ref[1, o * slots + j]
            for w in range(walk):
                pltpu.make_async_copy(theta_ref.at[w, block], out_ref.at[o, w, j], sem).start()
    pltpu.make_async_copy(out_ref, out_ref, sem).wait()


def tile_pieces(chol_ref, tile_ref, sems, slot):
    width = chol_ref.shape[2] // PIECES
    return [
        pltpu.make_async_copy(
            chol_ref.at[slot, :, pl.ds(c * width, width)],
            tile_ref.at[slot, :, pl.ds(c * width, width)],
            sems.at[slot, c],
        )
        for c in range(PIECES)
    ]


def start_tiles(chol_ref, tile_ref, sems, live):
    for slot in range(chol_ref.shape[0]):

        @pl.when(slot < live)
        def _():
            for copy in tile_pieces(chol_ref, tile_ref, sems, slot):
                copy.start()


def block_mask(size_ref, row_block, col_block, bs):
    rows = lax.broadcasted_iota(jnp.int32, (bs, bs), 0) < size_ref[row_block]
    cols = lax.broadcasted_iota(jnp.int32, (bs, bs), 1) < size_ref[col_block]
    return rows & cols


def bias_kernel(
    spread, info_ref, count_ref, size_ref, recv_ref, trial_ref, fields_ref, chol_ref,
    out_ref, tile_ref, green_ref, bias_ref, sems,
):
    owners, walk, slots, bs, _ = recv_ref.shape
    walkers = owners * walk
    me = lax.axis_index("blk")
    live = count_ref[me]
    start_tiles(chol_ref, tile_ref, sems, live)
    bias_ref[...] = jnp.zeros_like(bias_ref)
    for slot in range(slots):

        @pl.when(slot < live)
        def _(slot=slot):
            row_block = info_ref[0, me * slots + slot]
            col_block = info_ref[1, me * slots + slot]
            trial_rows = trial_ref[pl.ds(pl.multiple_of(row_block * bs, bs), bs), :]
            mask = block_mask(size_ref, row_block, col_block, bs)

            def one(w, carry):
                block = recv_ref[w // walk, w % walk, slot]
                green = lax.dot_general(trial_rows, block, NT, preferred_element_type=F32)
                green_ref[pl.ds(w, bs, stride=walkers), :] = jnp.where(mask, green, 0.0)
                return carry

            lax.fori_loop(0, walkers, one, 0, unroll=min(walkers, 16))
            per = bs // PIECES
            for c, copy in enumerate(tile_pieces(chol_ref, tile_ref, sems, slot)):
                copy.wait()
                base = c * per * walkers
                left = jnp.concatenate(
                    [
                        green_ref[pl.ds(base + p * walkers, walkers), :].astype(BF16)
                        for p in range(per)
                    ],
                    axis=1,
                )
                right = tile_ref[slot, :, pl.ds(c * per * bs, per * bs)]
                bias_ref[slot] += lax.dot_general(left, right, NT, preferred_element_type=F32)

    if spread:
        total = sum(bias_ref[slot] for slot in range(slots))
        for o in range(owners):
            out_ref[o, :walkers, :] = total
            out_ref[o, pl.ds(walkers, 8), :] = jnp.broadcast_to(fields_ref[...], (8, fields_ref.shape[1]))
    else:
        out_ref[...] = bias_ref[...]


def operator_kernel(
    spread, info_ref, count_ref, size_ref, bias_ref, fields_ref, chol_ref,
    out_ref, own_ref, tile_ref, shifted_ref, oper_ref, sems,
):
    owners, walk, slots, bs, _ = out_ref.shape
    walkers = owners * walk
    gs = chol_ref.shape[1]
    me = lax.axis_index("blk")
    live = count_ref[me]
    start_tiles(chol_ref, tile_ref, sems, live)
    if spread:
        rows = walkers + 8
        bias = sum(bias_ref[pl.ds(o * rows, walkers), :] for o in range(owners))
        fields = bias_ref[pl.ds(walkers, owners, stride=rows), :]
        shifted_ref[...] = bias
        own_ref[...] = shifted_ref[pl.ds(me, 1), :]
    else:
        bias = bias_ref[...]
        fields = fields_ref[...]
        own_ref[...] = bias_ref[pl.ds(me * walk, walk), :]
    shifted_ref[...] = (fields - bias)
    for slot in range(slots):

        @pl.when(slot < live)
        def _(slot=slot):
            row_block = info_ref[0, me * slots + slot]
            col_block = info_ref[1, me * slots + slot]
            slab = info_ref[2, me * slots + slot]
            mask = block_mask(size_ref, row_block, col_block, bs)
            left = shifted_ref[:, pl.ds(pl.multiple_of(slab * gs, gs), gs)].astype(BF16)
            per = bs // PIECES
            for c, copy in enumerate(tile_pieces(chol_ref, tile_ref, sems, slot)):
                copy.wait()
                right = tile_ref[slot, :, pl.ds(c * per * bs, per * bs)]
                oper = jnp.dot(left, right, preferred_element_type=F32) * STEP_ROOT
                for p in range(per):
                    oper_ref[pl.ds(c * per + p, walkers, stride=bs), :] = oper[:, p * bs : (p + 1) * bs]

            def one(w, carry):
                block = oper_ref[pl.ds(pl.multiple_of(w * bs, bs), bs), :]
                out_ref[w // walk, w % walk, slot] = jnp.where(mask, block, 0.0).astype(BF16)
                return carry

            lax.fori_loop(0, walkers, one, 0, unroll=min(walkers, 16))

        @pl.when(slot >= live)
        def _(slot=slot):
            def one(w, carry):
                out_ref[w // walk, w % walk, slot] = jnp.zeros((bs, bs), BF16)
                return carry

            lax.fori_loop(0, walkers, one, 0, unroll=min(walkers, 16))


def update_kernel(info_ref, count_ref, theta_ref, oper_ref, out_ref, where_ref):
    owners, walk, slots, bs, _ = oper_ref.shape
    blocks = theta_ref.shape[1]
    slabs = where_ref.shape[0] // (3 * blocks)
    for o in range(owners):
        live = count_ref[o]
        for j in range(slots):

            @pl.when(j < live)
            def _(s=o * slots + j):
                row_block = info_ref[0, s]
                side = info_ref[1, s] - row_block + 1
                where_ref[(info_ref[2, s] * blocks + row_block) * 3 + side] = jnp.int32(s)

    for w in range(walk):
        for row_block in range(blocks):
            total = theta_ref[w, row_block].astype(F32)
            for col_block in range(max(row_block - 1, 0), min(row_block + 2, blocks)):
                for slab in range(slabs):
                    s = where_ref[(slab * blocks + row_block) * 3 + col_block - row_block + 1]
                    total += jnp.dot(
                        oper_ref[s // slots, w, s % slots], theta_ref[w, col_block],
                        preferred_element_type=F32,
                    )
            out_ref[w, row_block] = total.astype(BF16)


def per_device(theta, trial, chol, fields, tile_info, tile_count, block_size):
    owners = lax.axis_size("blk")
    walk, norb, nocc = theta.shape
    walkers = walk * owners
    slots, gs, _ = chol.shape
    nchol = fields.shape[1]
    blocks = block_size.shape[0]
    bs = norb // blocks
    slabs = nchol // gs
    spread = slabs == 1 and walk == 1
    params = pltpu.CompilerParams(vmem_limit_bytes=LIMIT)
    theta_blocks = theta.reshape(walk, blocks, bs, nocc)

    outgoing = pl.pallas_call(
        pick_kernel,
        out_shape=jax.ShapeDtypeStruct((owners, walk, slots, bs, nocc), BF16),
        in_specs=[SMEM, ANY],
        out_specs=ANY,
        scratch_shapes=[pltpu.SemaphoreType.DMA],
        name="pick",
    )(tile_info, theta_blocks)
    received = lax.all_to_all(outgoing, "blk", split_axis=0, concat_axis=0, tiled=True)

    part_shape = (owners, walkers + 8, gs) if spread else (slots, walkers, gs)
    part = pl.pallas_call(
        functools.partial(bias_kernel, spread),
        out_shape=jax.ShapeDtypeStruct(part_shape, F32),
        in_specs=[SMEM, SMEM, SMEM, VMEM, VMEM, VMEM, ANY],
        out_specs=VMEM,
        scratch_shapes=[
            pltpu.VMEM(chol.shape, BF16),
            pltpu.VMEM((bs * walkers, bs), F32),
            pltpu.VMEM((slots, walkers, gs), F32),
            pltpu.SemaphoreType.DMA((slots, PIECES)),
        ],
        compiler_params=params,
        name="bias",
    )(tile_info, tile_count, block_size, received, trial, fields, chol)

    if spread:
        bias_in = lax.all_to_all(part, "blk", split_axis=0, concat_axis=0, tiled=True)
        bias_in = bias_in.reshape(owners * (walkers + 8), gs)
        fields_in = fields
    else:
        me = lax.axis_index("blk")
        local = jnp.zeros((walkers, nchol), F32)
        for slot in range(slots):
            start = (0, tile_info[2, me * slots + slot] * gs)
            old = lax.dynamic_slice(local, start, (walkers, gs))
            local = lax.dynamic_update_slice(local, old + part[slot], start)
        bias_in = lax.psum(local, "blk")
        fields_in = lax.all_gather(fields, "blk", axis=0, tiled=True)

    operators, own_bias = pl.pallas_call(
        functools.partial(operator_kernel, spread),
        out_shape=(
            jax.ShapeDtypeStruct((owners, walk, slots, bs, bs), BF16),
            jax.ShapeDtypeStruct((walk, nchol), F32),
        ),
        in_specs=[SMEM, SMEM, SMEM, VMEM, VMEM, ANY],
        out_specs=(VMEM, VMEM),
        scratch_shapes=[
            pltpu.VMEM(chol.shape, BF16),
            pltpu.VMEM((walkers, nchol), F32),
            pltpu.VMEM((walkers * bs, bs), F32),
            pltpu.SemaphoreType.DMA((slots, PIECES)),
        ],
        compiler_params=params,
        name="operator",
    )(tile_info, tile_count, block_size, bias_in, fields_in, chol)
    arrived = lax.all_to_all(operators, "blk", split_axis=0, concat_axis=0, tiled=True)

    propagated = pl.pallas_call(
        update_kernel,
        out_shape=jax.ShapeDtypeStruct(theta_blocks.shape, BF16),
        in_specs=[SMEM, SMEM, VMEM, VMEM],
        out_specs=VMEM,
        scratch_shapes=[pltpu.SMEM((slabs * blocks * 3,), jnp.int32)],
        compiler_params=params,
        name="update",
    )(tile_info, tile_count, theta_blocks, arrived)
    return propagated.reshape(theta.shape), own_bias


def solution(mesh):
    placed = (
        P(("grp", "blk"), None, None),
        P("grp", None),
        P(("grp", "blk"), None, None),
        P(("grp", "blk"), None),
        P("grp", None),
        P("grp"),
        P("grp"),
    )
    return jax.shard_map(
        per_device,
        mesh=mesh,
        in_specs=placed,
        out_specs=(P(("grp", "blk"), None, None), P(("grp", "blk"), None)),
        check_vma=False,
    )
```

time: 136 us -> 127 us (0.934); the launches traced: 134 us -> 127 us
  Pallas kernels: 0 us -> 43.8 us
  blocking collectives: 51 us -> 78.7 us
  waiting for transfers between devices: 21.9 us -> 0 us
  matrix products: 16 us -> 0 us
  starting transfers between devices: 14.9 us -> 0 us
  local copies, waits for them, and re-layouts: 14.1 us -> 3.61 us
  between operations: 9.73 us -> 0.67 us
  other arithmetic: 6.45 us -> 0 us
    all_to_all x0 -> x3, blocking collectives: none -> 78.7 us  [the longest x1 32.6 us: per_device(): lax.all_to_all(outgoing, 'blk', split_axis=0, concat_axis=0, tiled=True)]
    pallas_call x0 -> x4, Pallas kernels: none -> 43.8 us  [the longest x1 33.7 us: per_device(): pl.pallas_call(pick_kernel, out_shape=jax.ShapeDtypeStruct((owners, walk,...]
    psum x1 -> x0, blocking collectives: 29.5 us -> none  [per_device(): bias_all = lax.psum(bias_local, 'blk')]
    all_to_all x2 -> x0, waiting for transfers between devices: 21.9 us -> none  [the longest x1 21.9 us: per_device(): lax.all_to_all(stacked, 'blk', split_axis=1, concat_axis=0, tiled=True)]
    all_gather x1 -> x0, blocking collectives: 21.5 us -> none  [per_device(): fields_all = lax.all_gather(fields, 'blk', axis=0, tiled=True)]
    dot_general x8 -> x0, matrix products: 16 us -> none  [the longest x2 6.77 us: per_device(): jnp.einsum('wf,gf->wg', green_block.reshape(walkers, BS * BS), chol[slot_...]
    all_to_all x2 -> x0, starting transfers between devices: 14.9 us -> none  [the longest x1 7.59 us: per_device(): lax.all_to_all(stacked, 'blk', split_axis=1, concat_axis=0, tiled=True)]
    another operation x2 -> x0, local copies, waits for them, and re-layouts: 3.91 us -> none  [the longest x1 2.06 us: per_device(): stacked = jnp.stack(operator_list).reshape(TMAX, walkers, BS * BS)]
  transfers between devices with their start and end apart: 2 -> 0, of which waited for: 1 -> 0; matrix products, arithmetic and copies ran while one was open for 5% -> 0% of each run, Pallas kernels for 0% -> 0%
where the time goes in v1:
time: 127 us
  blocking collectives  78.7 us (62%)
  Pallas kernels  43.8 us (34%)
  local copies, waits for them, and re-layouts  3.61 us (3%)
    pallas_call x1, Pallas kernels, per_device(): pl.pallas_call(pick_kernel, out_shape=jax.ShapeDtypeStruct((owners, walk,...  33.7 us
    all_to_all x1, blocking collectives, per_device(): lax.all_to_all(outgoing, 'blk', split_axis=0, concat_axis=0, tiled=True)  32.6 us
    all_to_all x1, blocking collectives, per_device(): lax.all_to_all(operators, 'blk', split_axis=0, concat_axis=0, tiled=True)  30.2 us
    all_to_all x1, blocking collectives, per_device(): lax.all_to_all(part, 'blk', split_axis=0, concat_axis=0, tiled=True)  16 us
    pallas_call x1, Pallas kernels, per_device(): pl.pallas_call(functools.partial(bias_kernel, spread), out_shape=jax.Shap...  4.2 us
    pallas_call x1, Pallas kernels, per_device(): pl.pallas_call(functools.partial(operator_kernel, spread), out_shape=(jax...  4.11 us
    unnamed x14, local copies, waits for them, and re-layouts  3.61 us

profile of v1, /device:TPU:1, one launch (start us, length us, event | category | flops | bytes accessed | tf_op | source)
XLA Modules:
  0.0 126.7 jit_solution(4346949513196301213)
XLA Ops:
  0.6 0.0 copy-start.6
  0.6 33.7 %pick.1 = bf16[16,1,2,128,128]{4,3,2,1,0:T(8,128)(2,1)} custom-call(s32[3,32]{1,0:T(4,128)} %info_ref.7, bf16[1,8,128,128]{3,2,1,0:T(8,128)(2,1)} %bitcast.3), custom_call_target="tpu_custom_call" | custom-call | tf_op jit(solution)/shard_map/pick/pallas_call | solution.py:201
  34.3 32.6 %all_to_all.15.recv_ref = bf16[16,1,2,128,128]{4,3,2,1,0:T(8,128)(2,1)S(1)} all-to-all(bf16[16,1,2,128,128]{4,3,2,1,0:T(8,128)(2,1)} %pick.1), channel_id=1, replica_groups=mesh['grp'=2,'blk'=16] {'blk'}, dimensions={0} | all-to-all | bytes 2097152 | tf_op jit(solution)/shard_map/all_to_all | solution.py:209
  66.9 0.0 copy-start.1
  66.9 0.9 copy-done.1
  67.9 0.0 copy-start.2
  67.9 0.7 copy-done.2
  68.5 0.0 copy-start.3
  68.5 0.7 copy-done.3
  69.2 0.0 copy-start.4
  69.2 0.7 copy-done.4
  69.9 0.0 copy-start.5
  69.9 0.7 copy-done.5
  70.5 0.0 copy-start
  70.5 4.2 %bias.1 = f32[16,24,128]{2,1,0:T(8,128)S(1)} custom-call(s32[3,32]{1,0:T(4,128)S(1)} %copy-done.2, s32[16]{0:T(128)S(1)} %copy-done.3, s32[8]{0:T(128)S(1)} %copy-done.4, bf16[16,1,2,128,128]{4,3,2,1,0:T(8,128)(2,1)S(1)} %all_to_all.15.recv_ref, bf16[1024,128]{1,0:T(8,128)(2,1)S(1)} %copy-done.1, f32[1,128]{1,0:T(1,128)S(1)} %copy-done.5, ...), custom_call_target="tpu_custom_call" | custom-call | tf_op jit(solution)/shard_map/bias/pallas_call | solution.py:212
  74.7 16.0 %all_to_all.16 = f32[16,24,128]{2,1,0:T(8,128)S(1)} all-to-all(f32[16,24,128]{2,1,0:T(8,128)S(1)} %bias.1), channel_id=1, replica_groups=mesh['grp'=2,'blk'=16] {'blk'}, dimensions={0} | all-to-all | bytes 393216 | tf_op jit(solution)/shard_map/all_to_all | solution.py:228
  90.7 0.0 copy-done.6
  90.7 4.1 %operator.1 = (bf16[16,1,2,128,128]{4,3,2,1,0:T(8,128)(2,1)S(1)}, f32[1,128]{1,0:T(1,128)}) custom-call(s32[3,32]{1,0:T(4,128)S(1)} %copy-done.2, s32[16]{0:T(128)S(1)} %copy-done.3, s32[8]{0:T(128)S(1)} %copy-done.4, f32[384,128]{1,0:T(8,128)S(1)} %bitcast.5, f32[1,128]{1,0:T(1,128)S(1)} %copy-done.6, bf16[2,128,16384]{2,1,0:T(8,128)(2,1)} %chol_ref.3), custom_call_target="tpu_custom_call" | custom-call | tf_op jit(solution)/shard_map/operator/pallas_call | solution.py:241
  94.8 30.2 %all_to_all.17.oper_ref = bf16[16,1,2,128,128]{4,3,2,1,0:T(8,128)(2,1)S(1)} all-to-all(bf16[16,1,2,128,128]{4,3,2,1,0:T(8,128)(2,1)S(1)} %get-tuple-element.4), channel_id=1, replica_groups=mesh['grp'=2,'blk'=16] {'blk'}, dimensions={0} | all-to-all | bytes 2097152 | tf_op jit(solution)/shard_map/all_to_all | solution.py:258
  125.0 0.0 copy-done
  125.0 1.7 %update.1 = bf16[1,8,128,128]{3,2,1,0:T(8,128)(2,1)} custom-call(s32[3,32]{1,0:T(4,128)S(1)} %copy-done.2, s32[16]{0:T(128)S(1)} %copy-done.3, bf16[1,8,128,128]{3,2,1,0:T(8,128)(2,1)S(1)} %bitcast.4, bf16[16,1,2,128,128]{4,3,2,1,0:T(8,128)(2,1)S(1)} %all_to_all.17.oper_ref), custom_call_target="tpu_custom_call" | custom-call | tf_op jit(solution)/shard_map/update/pallas_call | solution.py:260
Async XLA Ops:
  0.6 90.1 %copy-start.6 = (f32[1,128]{1,0:T(1,128)S(1)}, f32[1,128]{1,0:T(1,128)}, u32[]{:S(2)}) copy-start(f32[1,128]{1,0:T(1,128)} %fields_ref.3) | copy-start | bytes 1540
  66.9 1.0 copy-start.1
  67.9 0.7 copy-start.2
  68.5 0.7 copy-start.3
  69.2 0.7 copy-start.4
  69.9 0.7 copy-start.5
  70.5 54.5 %copy-start = (bf16[1,1024,128]{2,1,0:T(8,128)(2,1)S(1)}, bf16[1,1024,128]{2,1,0:T(8,128)(2,1)}, u32[]{:S(2)}) copy-start(bf16[1,1024,128]{2,1,0:T(8,128)(2,1)} %param.7) | copy-start | bytes 786436

commit v2 on v1

v2 whole, which is shorter than its diff:
```python
import functools

import jax
import jax.numpy as jnp
from jax import lax
from jax.experimental import pallas as pl
from jax.experimental.pallas import tpu as pltpu
from jax.sharding import PartitionSpec as P

STEP_ROOT = 0.25
PIECES = 8
F32 = jnp.float32
BF16 = jnp.bfloat16
LIMIT = 24 * 1024 * 1024
VMEM = pl.BlockSpec(memory_space=pltpu.VMEM)
SMEM = pl.BlockSpec(memory_space=pltpu.SMEM)
HBM = pl.BlockSpec(memory_space=pltpu.HBM)
NT = (((1,), (1,)), ((), ()))


def pick_kernel(
    info_hbm, count_hbm, size_hbm, fields_hbm, theta_ref, trial_ref,
    out_ref, rows_ref, mask_ref, draws_ref, where_ref, info_ref, count_ref, size_ref, fields_ref, sems,
):
    owners, walk, slots, bs, _ = out_ref.shape
    blocks = theta_ref.shape[1]
    small = [
        pltpu.make_async_copy(source, target, sems.at[2 + n])
        for n, (source, target) in enumerate(
            [(info_hbm, info_ref), (count_hbm, count_ref), (size_hbm, size_ref), (fields_hbm, fields_ref)]
        )
    ]
    for copy in small:
        copy.start()
    small[0].wait()
    copies = []
    for o in range(owners):
        for j in range(slots):
            block = info_ref[1, o * slots + j]
            for w in range(walk):
                copies.append(pltpu.make_async_copy(theta_ref.at[w, block], out_ref.at[o, w, j], sems.at[0]))
    me = lax.axis_index("blk")
    for j in range(slots):
        block = info_ref[0, me * slots + j]
        copies.append(
            pltpu.make_async_copy(
                trial_ref.at[pl.ds(pl.multiple_of(block * bs, bs), bs), :], rows_ref.at[j], sems.at[1]
            )
        )
    for copy in copies:
        copy.start()
    for copy in small[1:]:
        copy.wait()
    live = count_ref[me]
    for j in range(slots):
        row_size = jnp.where(j < live, size_ref[info_ref[0, me * slots + j]], 0)
        col_size = size_ref[info_ref[1, me * slots + j]]
        rows = lax.broadcasted_iota(jnp.int32, (bs, bs), 0) < row_size
        cols = lax.broadcasted_iota(jnp.int32, (bs, bs), 1) < col_size
        mask_ref[j] = jnp.where(rows & cols, 1.0, 0.0)
    draws_ref[...] = jnp.broadcast_to(fields_ref[0:1, :], draws_ref.shape)
    for o in range(owners):
        for j in range(slots):

            @pl.when(j < count_ref[o])
            def _(s=o * slots + j):
                row_block = info_ref[0, s]
                side = info_ref[1, s] - row_block + 1
                where_ref[(info_ref[2, s] * blocks + row_block) * 3 + side] = jnp.int32(s)

    pltpu.make_async_copy(out_ref, out_ref, sems.at[0]).wait()
    pltpu.make_async_copy(rows_ref, rows_ref, sems.at[1]).wait()


def tile_pieces(chol_ref, tile_ref, sems, slot):
    width = chol_ref.shape[2] // PIECES
    return [
        pltpu.make_async_copy(
            chol_ref.at[slot, :, pl.ds(c * width, width)],
            tile_ref.at[slot, :, pl.ds(c * width, width)],
            sems.at[slot, c],
        )
        for c in range(PIECES)
    ]


def bias_kernel(
    spread, recv_ref, rows_ref, mask_ref, draws_ref, chol_ref, out_ref, tile_ref, green_ref, bias_ref, sems
):
    owners, walk, slots, bs, _ = recv_ref.shape
    walkers = owners * walk
    for slot in range(slots):
        for copy in tile_pieces(chol_ref, tile_ref, sems, slot):
            copy.start()
    for slot in range(slots):

        def one(w, carry, slot=slot):
            block = recv_ref[w // walk, w % walk, slot]
            green = lax.dot_general(rows_ref[slot], block, NT, preferred_element_type=F32)
            green_ref[slot, pl.ds(w, bs, stride=walkers), :] = green * mask_ref[slot]
            return carry

        lax.fori_loop(0, walkers, one, 0, unroll=min(walkers, 16))
    per = bs // PIECES
    for slot in range(slots):
        bias = jnp.zeros((walkers, chol_ref.shape[1]), F32)
        for c, copy in enumerate(tile_pieces(chol_ref, tile_ref, sems, slot)):
            copy.wait()
            base = c * per * walkers
            left = jnp.concatenate(
                [green_ref[slot, pl.ds(base + p * walkers, walkers), :].astype(BF16) for p in range(per)],
                axis=1,
            )
            right = tile_ref[slot, :, pl.ds(c * per * bs, per * bs)]
            bias += lax.dot_general(left, right, NT, preferred_element_type=F32)
        bias_ref[slot] = bias

    if spread:
        total = sum(bias_ref[slot] for slot in range(slots))
        for o in range(owners):
            out_ref[o, :walkers, :] = total
            out_ref[o, pl.ds(walkers, 8), :] = draws_ref[...]
    else:
        out_ref[...] = bias_ref[...]


def operator_kernel(spread, *refs):
    if spread:
        bias_ref, mask_ref, chol_ref, out_ref, own_ref, shifted_ref, oper_ref = refs
    else:
        info_ref, bias_ref, fields_ref, mask_ref, chol_ref, out_ref, own_ref, shifted_ref, oper_ref = refs
    owners, walk, slots, bs, _ = out_ref.shape
    walkers = owners * walk
    gs = chol_ref.shape[1]
    me = lax.axis_index("blk")
    if spread:
        rows = walkers + 8
        bias = sum(bias_ref[pl.ds(o * rows, walkers), :] for o in range(owners))
        fields = bias_ref[pl.ds(walkers, owners, stride=rows), :]
        shifted_ref[...] = bias
        own_ref[...] = shifted_ref[pl.ds(me, 1), :]
    else:
        bias = bias_ref[...]
        fields = fields_ref[...]
        own_ref[...] = bias_ref[pl.ds(me * walk, walk), :]
    shifted_ref[...] = fields - bias
    for slot in range(slots):
        slab = 0 if spread else pl.multiple_of(info_ref[2, me * slots + slot] * gs, gs)
        left = shifted_ref[:, pl.ds(slab, gs)].astype(BF16)
        per = bs // PIECES
        for c in range(PIECES):
            right = chol_ref[slot, :, pl.ds(c * per * bs, per * bs)]
            oper = jnp.dot(left, right, preferred_element_type=F32) * STEP_ROOT
            for p in range(per):
                oper_ref[pl.ds(c * per + p, walkers, stride=bs), :] = oper[:, p * bs : (p + 1) * bs]

        def one(w, carry, slot=slot):
            block = oper_ref[pl.ds(pl.multiple_of(w * bs, bs), bs), :]
            out_ref[w // walk, w % walk, slot] = (block * mask_ref[slot]).astype(BF16)
            return carry

        lax.fori_loop(0, walkers, one, 0, unroll=min(walkers, 16))


def update_kernel(where_ref, theta_ref, oper_ref, out_ref):
    owners, walk, slots, bs, _ = oper_ref.shape
    blocks = theta_ref.shape[1]
    slabs = where_ref.shape[0] // (3 * blocks)
    for w in range(walk):
        for row_block in range(blocks):
            total = theta_ref[w, row_block].astype(F32)
            for col_block in range(max(row_block - 1, 0), min(row_block + 2, blocks)):
                for slab in range(slabs):
                    s = where_ref[(slab * blocks + row_block) * 3 + col_block - row_block + 1]
                    total += jnp.dot(
                        oper_ref[s // slots, w, s % slots], theta_ref[w, col_block],
                        preferred_element_type=F32,
                    )
            out_ref[w, row_block] = total.astype(BF16)


def per_device(theta, trial, chol, fields, tile_info, tile_count, block_size):
    owners = lax.axis_size("blk")
    walk, norb, nocc = theta.shape
    walkers = walk * owners
    slots, gs, _ = chol.shape
    nchol = fields.shape[1]
    blocks = block_size.shape[0]
    bs = norb // blocks
    slabs = nchol // gs
    spread = slabs == 1 and walk == 1
    params = pltpu.CompilerParams(vmem_limit_bytes=LIMIT)
    theta_blocks = theta.reshape(walk, blocks, bs, nocc)

    outgoing, rows, mask, draws, where = pl.pallas_call(
        pick_kernel,
        out_shape=(
            jax.ShapeDtypeStruct((owners, walk, slots, bs, nocc), BF16),
            jax.ShapeDtypeStruct((slots, bs, nocc), BF16),
            jax.ShapeDtypeStruct((slots, bs, bs), F32),
            jax.ShapeDtypeStruct((8, nchol), F32),
            jax.ShapeDtypeStruct((slabs * blocks * 3,), jnp.int32),
        ),
        in_specs=[HBM] * 6,
        out_specs=(VMEM, VMEM, VMEM, VMEM, SMEM),
        scratch_shapes=[
            pltpu.SMEM(tile_info.shape, jnp.int32),
            pltpu.SMEM(tile_count.shape, jnp.int32),
            pltpu.SMEM(block_size.shape, jnp.int32),
            pltpu.VMEM(fields.shape, F32),
            pltpu.SemaphoreType.DMA((6,)),
        ],
        compiler_params=params,
        name="pick",
    )(*(pltpu.with_memory_space_constraint(x, pltpu.HBM)
        for x in (tile_info, tile_count, block_size, fields, theta_blocks, trial)))
    received = lax.all_to_all(outgoing, "blk", split_axis=0, concat_axis=0, tiled=True)

    part_shape = (owners, walkers + 8, gs) if spread else (slots, walkers, gs)
    part, tiles = pl.pallas_call(
        functools.partial(bias_kernel, spread),
        out_shape=(jax.ShapeDtypeStruct(part_shape, F32), jax.ShapeDtypeStruct(chol.shape, BF16)),
        in_specs=[VMEM, VMEM, VMEM, VMEM, HBM],
        out_specs=(VMEM, VMEM),
        scratch_shapes=[
            pltpu.VMEM((slots, bs * walkers, bs), F32),
            pltpu.VMEM((slots, walkers, gs), F32),
            pltpu.SemaphoreType.DMA((slots, PIECES)),
        ],
        compiler_params=params,
        name="bias",
    )(received, rows, mask, draws, pltpu.with_memory_space_constraint(chol, pltpu.HBM))

    if spread:
        bias_in = lax.all_to_all(part, "blk", split_axis=0, concat_axis=0, tiled=True)
        inputs = (bias_in.reshape(owners * (walkers + 8), gs),)
    else:
        me = lax.axis_index("blk")
        local = jnp.zeros((walkers, nchol), F32)
        for slot in range(slots):
            start = (0, tile_info[2, me * slots + slot] * gs)
            old = lax.dynamic_slice(local, start, (walkers, gs))
            local = lax.dynamic_update_slice(local, old + part[slot], start)
        inputs = (tile_info, lax.psum(local, "blk"), lax.all_gather(fields, "blk", axis=0, tiled=True))

    operators, own_bias = pl.pallas_call(
        functools.partial(operator_kernel, spread),
        out_shape=(
            jax.ShapeDtypeStruct((owners, walk, slots, bs, bs), BF16),
            jax.ShapeDtypeStruct((walk, nchol), F32),
        ),
        in_specs=([VMEM] if spread else [SMEM, VMEM, VMEM]) + [VMEM, VMEM],
        out_specs=(VMEM, VMEM),
        scratch_shapes=[
            pltpu.VMEM((walkers, nchol), F32),
            pltpu.VMEM((walkers * bs, bs), F32),
        ],
        compiler_params=params,
        name="operator",
    )(*inputs, mask, tiles)
    arrived = lax.all_to_all(operators, "blk", split_axis=0, concat_axis=0, tiled=True)

    propagated = pl.pallas_call(
        update_kernel,
        out_shape=jax.ShapeDtypeStruct(theta_blocks.shape, BF16),
        in_specs=[SMEM, VMEM, VMEM],
        out_specs=VMEM,
        compiler_params=params,
        name="update",
    )(where, theta_blocks, arrived)
    return propagated.reshape(theta.shape), own_bias


def solution(mesh):
    placed = (
        P(("grp", "blk"), None, None),
        P("grp", None),
        P(("grp", "blk"), None, None),
        P(("grp", "blk"), None),
        P("grp", None),
        P("grp"),
        P("grp"),
    )
    return jax.shard_map(
        per_device,
        mesh=mesh,
        in_specs=placed,
        out_specs=(P(("grp", "blk"), None, None), P(("grp", "blk"), None)),
        check_vma=False,
    )
```

time: 127 us -> 87.4 us (0.69)
  Pallas kernels: 43.8 us -> 12.8 us
  blocking collectives: 78.7 us -> 73.6 us
  local copies, waits for them, and re-layouts: 3.61 us -> 0.01 us
    pallas_call x2, Pallas kernels: 37.9 us -> 9.44 us  [the longest x1 6.55 us: per_device(): pl.pallas_call(functools.partial(bias_kernel, spread), out_shape=(jax.Sha...]
    unnamed x14 -> x2, local copies, waits for them, and re-layouts: 3.61 us -> 0.01 us
    all_to_all x1, blocking collectives: 16 us -> 12.8 us  [per_device(): lax.all_to_all(part, 'blk', split_axis=0, concat_axis=0, tiled=True)]
    pallas_call x1, Pallas kernels: 4.11 us -> 1.8 us  [per_device(): pl.pallas_call(functools.partial(operator_kernel, spread), out_shape=(jax...]
    all_to_all x1, blocking collectives: 30.2 us -> 28.5 us  [per_device(): lax.all_to_all(operators, 'blk', split_axis=0, concat_axis=0, tiled=True)]
where the time goes in v2:
time: 87.4 us; the launch traced here: 87.1 us
  blocking collectives  73.6 us (84%)
  Pallas kernels  12.8 us (15%)
    all_to_all x1, blocking collectives, per_device(): lax.all_to_all(outgoing, 'blk', split_axis=0, concat_axis=0, tiled=True)  32.4 us
    all_to_all x1, blocking collectives, per_device(): lax.all_to_all(operators, 'blk', split_axis=0, concat_axis=0, tiled=True)  28.5 us
    all_to_all x1, blocking collectives, per_device(): lax.all_to_all(part, 'blk', split_axis=0, concat_axis=0, tiled=True)  12.8 us
    pallas_call x1, Pallas kernels, per_device(): pl.pallas_call(functools.partial(bias_kernel, spread), out_shape=(jax.Sha...  6.55 us
    pallas_call x1, Pallas kernels, per_device(): pl.pallas_call(pick_kernel, out_shape=(jax.ShapeDtypeStruct((owners, walk...  2.89 us
    pallas_call x1, Pallas kernels, per_device(): pl.pallas_call(functools.partial(operator_kernel, spread), out_shape=(jax...  1.8 us

profile of v2, /device:TPU:1, one launch (start us, length us, event | category | flops | bytes accessed | tf_op | source)
XLA Modules:
  0.0 87.1 jit_solution(11937650191576331834)
XLA Ops:
  0.6 2.9 %pick.1 = (bf16[16,1,2,128,128]{4,3,2,1,0:T(8,128)(2,1)S(1)}, bf16[2,128,128]{2,1,0:T(8,128)(2,1)S(1)}, f32[2,128,128]{2,1,0:T(8,128)S(1)}, f32[8,128]{1,0:T(8,128)S(1)}, s32[24]{0:T(128)S(1)}) custom-call(s32[3,32]{1,0:T(4,128)} %info_hbm.1, s32[16]{0:T(128)} %count_hbm.1, s32[8]{0:T(128)} %size_hbm.1, f32[1,128]{1,0:T(1,128)} %fields_hbm.1, ...), custom_call_target="tpu_custom_call" | custom-call | tf_op jit(solution)/shard_map/pick/pallas_call | solution.py:195
  3.5 32.4 %all_to_all.15.recv_ref = bf16[16,1,2,128,128]{4,3,2,1,0:T(8,128)(2,1)S(1)} all-to-all(bf16[16,1,2,128,128]{4,3,2,1,0:T(8,128)(2,1)S(1)} %get-tuple-element.12), channel_id=1, replica_groups=mesh['grp'=2,'blk'=16] {'blk'}, dimensions={0} | all-to-all | bytes 2097152 | tf_op jit(solution)/shard_map/all_to_all | solution.py:217
  35.9 0.0 copy-start
  35.9 6.5 %bias.1 = (f32[16,24,128]{2,1,0:T(8,128)S(1)}, bf16[2,128,16384]{2,1,0:T(8,128)(2,1)S(1)}) custom-call(bf16[16,1,2,128,128]{4,3,2,1,0:T(8,128)(2,1)S(1)} %all_to_all.15.recv_ref, bf16[2,128,128]{2,1,0:T(8,128)(2,1)S(1)} %get-tuple-element.13.rows_ref, f32[2,128,128]{2,1,0:T(8,128)S(1)} %get-tuple-element.14.mask_ref.refs_1_, ...), custom_call_target="tpu_custom_call" | custom-call | tf_op jit(solution)/shard_map/bias/pallas_call | solution.py:220
  42.4 12.8 %all_to_all.16 = f32[16,24,128]{2,1,0:T(8,128)S(1)} all-to-all(f32[16,24,128]{2,1,0:T(8,128)S(1)} %get-tuple-element.16), channel_id=1, replica_groups=mesh['grp'=2,'blk'=16] {'blk'}, dimensions={0} | all-to-all | bytes 393216 | tf_op jit(solution)/shard_map/all_to_all | solution.py:235
  55.2 1.8 %operator.1 = (bf16[16,1,2,128,128]{4,3,2,1,0:T(8,128)(2,1)S(1)}, f32[1,128]{1,0:T(1,128)}) custom-call(f32[384,128]{1,0:T(8,128)S(1)} %bitcast.5, f32[2,128,128]{2,1,0:T(8,128)S(1)} %get-tuple-element.14.mask_ref.refs_1_, bf16[2,128,16384]{2,1,0:T(8,128)(2,1)S(1)} %get-tuple-element.17.refs_2_), custom_call_target="tpu_custom_call" | custom-call | tf_op jit(solution)/shard_map/operator/pallas_call | solution.py:246
  57.0 28.5 %all_to_all.17.oper_ref = bf16[16,1,2,128,128]{4,3,2,1,0:T(8,128)(2,1)S(1)} all-to-all(bf16[16,1,2,128,128]{4,3,2,1,0:T(8,128)(2,1)S(1)} %get-tuple-element.18), channel_id=1, replica_groups=mesh['grp'=2,'blk'=16] {'blk'}, dimensions={0} | all-to-all | bytes 2097152 | tf_op jit(solution)/shard_map/all_to_all | solution.py:261
  85.5 0.0 copy-done
  85.5 1.6 %update.1 = bf16[1,8,128,128]{3,2,1,0:T(8,128)(2,1)} custom-call(s32[24]{0:T(128)S(1)} %get-tuple-element.11.where_ref, bf16[1,8,128,128]{3,2,1,0:T(8,128)(2,1)S(1)} %bitcast.4, bf16[16,1,2,128,128]{4,3,2,1,0:T(8,128)(2,1)S(1)} %all_to_all.17.oper_ref), custom_call_target="tpu_custom_call" | custom-call | tf_op jit(solution)/shard_map/update/pallas_call | solution.py:263
Async XLA Ops:
  35.9 49.6 %copy-start = (bf16[1,1024,128]{2,1,0:T(8,128)(2,1)S(1)}, bf16[1,1024,128]{2,1,0:T(8,128)(2,1)}, u32[]{:S(2)}) copy-start(bf16[1,1024,128]{2,1,0:T(8,128)(2,1)} %param.7) | copy-start | bytes 786436

commit v3 on v2

--- a/solution.py
+++ b/solution.py
@@ -18,8 +18,21 @@
 NT = (((1,), (1,)), ((), ()))
 
 
+def each(count, body):
+    if count <= 16:
+        for index in range(count):
+            body(index)
+    else:
+
+        def step(index, carry):
+            body(index)
+            return carry
+
+        lax.fori_loop(0, count, step, 0, unroll=8)
+
+
 def pick_kernel(
-    info_hbm, count_hbm, size_hbm, fields_hbm, theta_ref, trial_ref,
+    info_hbm, count_hbm, size_hbm, fields_hbm, theta_ref, trial_ref, chol_ref,
     out_ref, rows_ref, mask_ref, draws_ref, where_ref, info_ref, count_ref, size_ref, fields_ref, sems,
 ):
     owners, walk, slots, bs, _ = out_ref.shape
@@ -72,46 +85,29 @@
     pltpu.make_async_copy(rows_ref, rows_ref, sems.at[1]).wait()
 
 
-def tile_pieces(chol_ref, tile_ref, sems, slot):
-    width = chol_ref.shape[2] // PIECES
-    return [
-        pltpu.make_async_copy(
-            chol_ref.at[slot, :, pl.ds(c * width, width)],
-            tile_ref.at[slot, :, pl.ds(c * width, width)],
-            sems.at[slot, c],
-        )
-        for c in range(PIECES)
-    ]
-
-
 def bias_kernel(
-    spread, recv_ref, rows_ref, mask_ref, draws_ref, chol_ref, out_ref, tile_ref, green_ref, bias_ref, sems
+    spread, recv_ref, rows_ref, mask_ref, draws_ref, chol_ref, out_ref, green_ref, bias_ref
 ):
     owners, walk, slots, bs, _ = recv_ref.shape
     walkers = owners * walk
     for slot in range(slots):
-        for copy in tile_pieces(chol_ref, tile_ref, sems, slot):
-            copy.start()
-    for slot in range(slots):
-
-        def one(w, carry, slot=slot):
+
+        def one(w, slot=slot):
             block = recv_ref[w // walk, w % walk, slot]
             green = lax.dot_general(rows_ref[slot], block, NT, preferred_element_type=F32)
             green_ref[slot, pl.ds(w, bs, stride=walkers), :] = green * mask_ref[slot]
-            return carry
-
-        lax.fori_loop(0, walkers, one, 0, unroll=min(walkers, 16))
+
+        each(walkers, one)
     per = bs // PIECES
     for slot in range(slots):
         bias = jnp.zeros((walkers, chol_ref.shape[1]), F32)
-        for c, copy in enumerate(tile_pieces(chol_ref, tile_ref, sems, slot)):
-            copy.wait()
+        for c in range(PIECES):
             base = c * per * walkers
             left = jnp.concatenate(
                 [green_ref[slot, pl.ds(base + p * walkers, walkers), :].astype(BF16) for p in range(per)],
                 axis=1,
             )
-            right = tile_ref[slot, :, pl.ds(c * per * bs, per * bs)]
+            right = chol_ref[slot, :, pl.ds(c * per * bs, per * bs)]
             bias += lax.dot_general(left, right, NT, preferred_element_type=F32)
         bias_ref[slot] = bias
 
@@ -154,12 +150,11 @@
             for p in range(per):
                 oper_ref[pl.ds(c * per + p, walkers, stride=bs), :] = oper[:, p * bs : (p + 1) * bs]
 
-        def one(w, carry, slot=slot):
-            block = oper_ref[pl.ds(pl.multiple_of(w * bs, bs), bs), :]
+        def one(w, slot=slot):
+            block = oper_ref[pl.ds(w * bs, bs), :]
             out_ref[w // walk, w % walk, slot] = (block * mask_ref[slot]).astype(BF16)
-            return carry
-
-        lax.fori_loop(0, walkers, one, 0, unroll=min(walkers, 16))
+
+        each(walkers, one)
 
 
 def update_kernel(where_ref, theta_ref, oper_ref, out_ref):
@@ -201,7 +196,7 @@
             jax.ShapeDtypeStruct((8, nchol), F32),
             jax.ShapeDtypeStruct((slabs * blocks * 3,), jnp.int32),
         ),
-        in_specs=[HBM] * 6,
+        in_specs=[HBM] * 7,
         out_specs=(VMEM, VMEM, VMEM, VMEM, SMEM),
         scratch_shapes=[
             pltpu.SMEM(tile_info.shape, jnp.int32),
@@ -211,25 +206,25 @@
             pltpu.SemaphoreType.DMA((6,)),
         ],
         compiler_params=params,
+        cost_estimate=pl.CostEstimate(flops=0, bytes_accessed=4 * chol.size * 2, transcendentals=0),
         name="pick",
     )(*(pltpu.with_memory_space_constraint(x, pltpu.HBM)
-        for x in (tile_info, tile_count, block_size, fields, theta_blocks, trial)))
+        for x in (tile_info, tile_count, block_size, fields, theta_blocks, trial, chol)))
     received = lax.all_to_all(outgoing, "blk", split_axis=0, concat_axis=0, tiled=True)
 
     part_shape = (owners, walkers + 8, gs) if spread else (slots, walkers, gs)
-    part, tiles = pl.pallas_call(
+    part = pl.pallas_call(
         functools.partial(bias_kernel, spread),
-        out_shape=(jax.ShapeDtypeStruct(part_shape, F32), jax.ShapeDtypeStruct(chol.shape, BF16)),
-        in_specs=[VMEM, VMEM, VMEM, VMEM, HBM],
-        out_specs=(VMEM, VMEM),
+        out_shape=jax.ShapeDtypeStruct(part_shape, F32),
+        in_specs=[VMEM] * 5,
+        out_specs=VMEM,
         scratch_shapes=[
             pltpu.VMEM((slots, bs * walkers, bs), F32),
             pltpu.VMEM((slots, walkers, gs), F32),
-            pltpu.SemaphoreType.DMA((slots, PIECES)),
         ],
         compiler_params=params,
         name="bias",
-    )(received, rows, mask, draws, pltpu.with_memory_space_constraint(chol, pltpu.HBM))
+    )(received, rows, mask, draws, chol)
 
     if spread:
         bias_in = lax.all_to_all(part, "blk", split_axis=0, concat_axis=0, tiled=True)
@@ -257,7 +252,7 @@
         ],
         compiler_params=params,
         name="operator",
-    )(*inputs, mask, tiles)
+    )(*inputs, mask, chol)
     arrived = lax.all_to_all(operators, "blk", split_axis=0, concat_axis=0, tiled=True)
 
     propagated = pl.pallas_call(

time: 87.4 us -> 84.9 us (0.971)
  Pallas kernels: 12.8 us -> 10.5 us
    pallas_call x1, Pallas kernels: 6.55 us -> 4.06 us  [per_device(): pl.pallas_call(functools.partial(bias_kernel, spread), out_shape=jax.Shap...]
where the time goes in v3:
time: 84.9 us; the launch traced here: 84.7 us
  blocking collectives  73.6 us (87%)
  Pallas kernels  10.5 us (12%)
    all_to_all x1, blocking collectives, per_device(): lax.all_to_all(outgoing, 'blk', split_axis=0, concat_axis=0, tiled=True)  32.4 us
    all_to_all x1, blocking collectives, per_device(): lax.all_to_all(operators, 'blk', split_axis=0, concat_axis=0, tiled=True)  28.5 us
    all_to_all x1, blocking collectives, per_device(): lax.all_to_all(part, 'blk', split_axis=0, concat_axis=0, tiled=True)  12.8 us
    pallas_call x1, Pallas kernels, per_device(): pl.pallas_call(functools.partial(bias_kernel, spread), out_shape=jax.Shap...  4.06 us
    pallas_call x1, Pallas kernels, per_device(): pl.pallas_call(pick_kernel, out_shape=(jax.ShapeDtypeStruct((owners, walk...  3.01 us
    pallas_call x1, Pallas kernels, per_device(): pl.pallas_call(functools.partial(operator_kernel, spread), out_shape=(jax...  1.82 us

profile of v3, /device:TPU:1, one launch (start us, length us, event | category | flops | bytes accessed | tf_op | source)
XLA Modules:
  0.0 84.7 jit_solution(9398058873669549025)
XLA Ops:
  0.6 0.0 copy-start
  0.6 3.0 %pick.1 = (bf16[16,1,2,128,128]{4,3,2,1,0:T(8,128)(2,1)S(1)}, bf16[2,128,128]{2,1,0:T(8,128)(2,1)S(1)}, f32[2,128,128]{2,1,0:T(8,128)S(1)}, f32[8,128]{1,0:T(8,128)S(1)}, s32[24]{0:T(128)S(1)}) custom-call(s32[3,32]{1,0:T(4,128)} %info_hbm.1, s32[16]{0:T(128)} %count_hbm.1, s32[8]{0:T(128)} %size_hbm.1, f32[1,128]{1,0:T(1,128)} %fields_hbm.1, ...), custom_call_target="tpu_custom_call" | custom-call | bytes 33554432 | tf_op jit(solution)/shard_map/pick/pallas_call | solution.py:190
  3.7 32.4 %all_to_all.15.recv_ref = bf16[16,1,2,128,128]{4,3,2,1,0:T(8,128)(2,1)S(1)} all-to-all(bf16[16,1,2,128,128]{4,3,2,1,0:T(8,128)(2,1)S(1)} %get-tuple-element.10), channel_id=1, replica_groups=mesh['grp'=2,'blk'=16] {'blk'}, dimensions={0} | all-to-all | bytes 2097152 | tf_op jit(solution)/shard_map/all_to_all | solution.py:213
  36.0 0.0 copy-done
  36.0 0.0 copy-start.1
  36.0 4.1 %bias.1 = f32[16,24,128]{2,1,0:T(8,128)S(1)} custom-call(bf16[16,1,2,128,128]{4,3,2,1,0:T(8,128)(2,1)S(1)} %all_to_all.15.recv_ref, bf16[2,128,128]{2,1,0:T(8,128)(2,1)S(1)} %get-tuple-element.11.rows_ref, f32[2,128,128]{2,1,0:T(8,128)S(1)} %get-tuple-element.12.mask_ref.refs_1_, f32[8,128]{1,0:T(8,128)S(1)} %get-tuple-element.13.draws_ref, ...), custom_call_target="tpu_custom_call" | custom-call | tf_op jit(solution)/shard_map/bias/pallas_call | solution.py:216
  40.1 12.8 %all_to_all.16 = f32[16,24,128]{2,1,0:T(8,128)S(1)} all-to-all(f32[16,24,128]{2,1,0:T(8,128)S(1)} %bias.1), channel_id=1, replica_groups=mesh['grp'=2,'blk'=16] {'blk'}, dimensions={0} | all-to-all | bytes 393216 | tf_op jit(solution)/shard_map/all_to_all | solution.py:230
  52.8 1.8 %operator.1 = (bf16[16,1,2,128,128]{4,3,2,1,0:T(8,128)(2,1)S(1)}, f32[1,128]{1,0:T(1,128)}) custom-call(f32[384,128]{1,0:T(8,128)S(1)} %bitcast.5, f32[2,128,128]{2,1,0:T(8,128)S(1)} %get-tuple-element.12.mask_ref.refs_1_, bf16[2,128,16384]{2,1,0:T(8,128)(2,1)S(1)} %copy-done), custom_call_target="tpu_custom_call" | custom-call | tf_op jit(solution)/shard_map/operator/pallas_call | solution.py:241
  54.7 28.5 %all_to_all.17.oper_ref = bf16[16,1,2,128,128]{4,3,2,1,0:T(8,128)(2,1)S(1)} all-to-all(bf16[16,1,2,128,128]{4,3,2,1,0:T(8,128)(2,1)S(1)} %get-tuple-element.14), channel_id=1, replica_groups=mesh['grp'=2,'blk'=16] {'blk'}, dimensions={0} | all-to-all | bytes 2097152 | tf_op jit(solution)/shard_map/all_to_all | solution.py:256
  83.1 0.0 copy-done.1
  83.1 1.6 %update.1 = bf16[1,8,128,128]{3,2,1,0:T(8,128)(2,1)} custom-call(s32[24]{0:T(128)S(1)} %get-tuple-element.9.where_ref, bf16[1,8,128,128]{3,2,1,0:T(8,128)(2,1)S(1)} %bitcast.4, bf16[16,1,2,128,128]{4,3,2,1,0:T(8,128)(2,1)S(1)} %all_to_all.17.oper_ref), custom_call_target="tpu_custom_call" | custom-call | tf_op jit(solution)/shard_map/update/pallas_call | solution.py:258
Async XLA Ops:
  0.6 35.4 %copy-start = (bf16[2,128,16384]{2,1,0:T(8,128)(2,1)S(1)}, bf16[2,128,16384]{2,1,0:T(8,128)(2,1)}, u32[]{:S(2)}) copy-start(bf16[2,128,16384]{2,1,0:T(8,128)(2,1)} %refs_2_.1) | copy-start | bytes 25165828
  36.0 47.1 %copy-start.1 = (bf16[1,1024,128]{2,1,0:T(8,128)(2,1)S(1)}, bf16[1,1024,128]{2,1,0:T(8,128)(2,1)}, u32[]{:S(2)}) copy-start(bf16[1,1024,128]{2,1,0:T(8,128)(2,1)} %param.7) | copy-start | bytes 786436

commit v4 on v3

--- a/solution.py
+++ b/solution.py
@@ -15,6 +15,7 @@
 VMEM = pl.BlockSpec(memory_space=pltpu.VMEM)
 SMEM = pl.BlockSpec(memory_space=pltpu.SMEM)
 HBM = pl.BlockSpec(memory_space=pltpu.HBM)
+ANY = pl.BlockSpec(memory_space=pl.ANY)
 NT = (((1,), (1,)), ((), ()))
 
 
@@ -174,7 +175,7 @@
             out_ref[w, row_block] = total.astype(BF16)
 
 
-def per_device(theta, trial, chol, fields, tile_info, tile_count, block_size):
+def long_axis(theta, trial, chol, fields, tile_info, tile_count, block_size):
     owners = lax.axis_size("blk")
     walk, norb, nocc = theta.shape
     walkers = walk * owners
@@ -266,6 +267,241 @@
     return propagated.reshape(theta.shape), own_bias
 
 
+def pick_pair_kernel(*refs):
+    info_hbm, count_hbm, size_hbm, fields_hbm, theta_ref, other_ref, trial_ref, _ = refs[:8]
+    rows_ref, mask_ref, draws_ref, where_ref, cols_ref = refs[8:13]
+    info_ref, count_ref, size_ref, fields_ref, sems, send_sems = refs[-6:]
+    pair_refs = refs[13:-6]
+    slots, bs, _ = rows_ref.shape
+    owners = count_ref.shape[0]
+    blocks = theta_ref.shape[1]
+    small = [
+        pltpu.make_async_copy(source, target, sems.at[n])
+        for n, (source, target) in enumerate(
+            [(info_hbm, info_ref), (count_hbm, count_ref), (size_hbm, size_ref), (fields_hbm, fields_ref)]
+        )
+    ]
+    for copy in small:
+        copy.start()
+    me = lax.axis_index("blk")
+    core = me % 2
+    small[0].wait()
+    for r, ref in enumerate(pair_refs):
+        for j in range(slots):
+            block = info_ref[1, (me ^ (2 * r)) * slots + j]
+            pltpu.make_async_copy(theta_ref.at[0, block], ref.at[core, j], send_sems.at[r]).start()
+            pltpu.make_async_copy(other_ref.at[0, block], ref.at[1 - core, j], send_sems.at[r]).start()
+    first = me // (owners // 2) * (owners // 2) * slots
+    for n in range(owners // 2 * slots):
+        cols_ref[n] = info_ref[1, first + n]
+    trial = []
+    for j in range(slots):
+        block = info_ref[0, me * slots + j]
+        trial.append(
+            pltpu.make_async_copy(
+                trial_ref.at[pl.ds(pl.multiple_of(block * bs, bs), bs), :], rows_ref.at[j], sems.at[4 + j]
+            )
+        )
+        trial[-1].start()
+    for copy in small[1:]:
+        copy.wait()
+    live = count_ref[me]
+    for j in range(slots):
+        row_size = jnp.where(j < live, size_ref[info_ref[0, me * slots + j]], 0)
+        col_size = size_ref[info_ref[1, me * slots + j]]
+        rows = lax.broadcasted_iota(jnp.int32, (bs, bs), 0) < row_size
+        cols = lax.broadcasted_iota(jnp.int32, (bs, bs), 1) < col_size
+        mask_ref[j] = jnp.where(rows & cols, 1.0, 0.0)
+    draws_ref[...] = jnp.broadcast_to(fields_ref[0:1, :], draws_ref.shape)
+    for o in range(owners):
+        for j in range(slots):
+
+            @pl.when(j < count_ref[o])
+            def _(s=o * slots + j):
+                row_block = info_ref[0, s]
+                where_ref[row_block * 3 + info_ref[1, s] - row_block + 1] = jnp.int32(s)
+
+    for r, ref in enumerate(pair_refs):
+        pltpu.make_async_copy(ref, ref, send_sems.at[r]).wait()
+    for copy in trial:
+        copy.wait()
+
+
+def spread_far_kernel(cols_ref, theta_ref, _, out_ref):
+    slots = out_ref.shape[1]
+    for k in range(out_ref.shape[0]):
+        for j in range(slots):
+            out_ref[k, j] = theta_ref[0, cols_ref[k * slots + j]]
+
+
+def bias_pair_kernel(step, rows_ref, mask_ref, draws_ref, chol_ref, far_ref, *refs):
+    pair_refs = refs[:-3]
+    out_ref, green_ref, total_ref = refs[-3:]
+    half, slots, bs, nocc = far_ref.shape
+    walkers = 2 * half
+    me = lax.axis_index("blk")
+    first = me // half * half
+    for slot in range(slots):
+        mask = mask_ref[slot]
+        for blocks, start in [(ref[:, slot], 2 * r) for r, ref in enumerate(pair_refs)] + [(far_ref[:, slot], half)]:
+            count = blocks.shape[0]
+            green = lax.dot_general(
+                rows_ref[slot], blocks.reshape(count * bs, nocc), NT, preferred_element_type=F32
+            )
+            for n in range(count):
+                green_ref[slot, pl.ds(start + n, bs, stride=walkers), :] = green[:, n * bs : (n + 1) * bs] * mask
+    per = bs // PIECES
+    tall = jnp.zeros((chol_ref.shape[1], walkers), F32)
+    wide = jnp.zeros((walkers, chol_ref.shape[1]), F32)
+    for c in range(PIECES):
+        for slot in range(slots):
+            green = jnp.concatenate(
+                [green_ref[slot, pl.ds((c * per + p) * walkers, walkers), :].astype(BF16) for p in range(per)],
+                axis=1,
+            )
+            tile = chol_ref[slot, :, pl.ds(c * per * bs, per * bs)]
+            if slot % 2:
+                wide += lax.dot_general(green, tile, NT, preferred_element_type=F32)
+            else:
+                tall += lax.dot_general(tile, green, NT, preferred_element_type=F32)
+    total = -(tall.T + wide)
+    for n in range(walkers):
+        walker = (me // 2 ^ (n // 2)) * 2 + n % 2 if n < half else (first + n - half) ^ step
+        total_ref[pl.ds(walker, 1), :] = total[n : n + 1, :]
+    total = total_ref[...]
+    own = total_ref[pl.ds(me, 1), :]
+    for o in range(walkers):
+        out_ref[o] = total
+        out_ref[o, pl.ds(me, 1), :] = jnp.where(o == me, own, own + draws_ref[0:1, :])
+
+
+def operator_pair_kernel(shift_ref, fields_ref, mask_ref, chol_ref, out_ref, own_ref, total_ref, oper_ref):
+    walkers, _, slots, bs, _ = out_ref.shape
+    me = lax.axis_index("blk")
+    total_ref[...] = sum(shift_ref[o] for o in range(walkers))
+    own = total_ref[pl.ds(me, 1), :]
+    own_ref[...] = -own
+    total_ref[pl.ds(me, 1), :] = own + fields_ref[0:1, :]
+    left = total_ref[...].astype(BF16)
+    per = bs // PIECES
+    for slot in range(slots):
+        for c in range(PIECES):
+            right = chol_ref[slot, :, pl.ds(c * per * bs, per * bs)]
+            oper = jnp.dot(left, right, preferred_element_type=F32) * STEP_ROOT
+            for p in range(per):
+                oper_ref[slot, pl.ds(c * per + p, walkers, stride=bs), :] = oper[:, p * bs : (p + 1) * bs]
+        for w in range(walkers):
+            block = oper_ref[slot, pl.ds(w * bs, bs), :]
+            out_ref[w, 0, slot] = (block * mask_ref[slot]).astype(BF16)
+
+
+def short_axis(theta, trial, chol, fields, tile_info, tile_count, block_size):
+    owners = lax.axis_size("blk")
+    _, norb, nocc = theta.shape
+    slots, gs, _ = chol.shape
+    blocks = block_size.shape[0]
+    bs = norb // blocks
+    half = owners // 2
+    step = half + half // 2
+    near = half // 2
+    params = pltpu.CompilerParams(vmem_limit_bytes=LIMIT)
+    theta_blocks = theta.reshape(1, blocks, bs, nocc)
+
+    def swap(x, step):
+        return lax.ppermute(x, "blk", [(i, i ^ step) for i in range(owners)])
+
+    def to_all(x, groups=None):
+        return lax.all_to_all(x, "blk", split_axis=0, concat_axis=0, tiled=True, axis_index_groups=groups)
+
+    def spread(pairs):
+        return [pairs[0]] + [swap(pairs[r], 2 * r) for r in range(1, near)]
+
+    hbm = functools.partial(pltpu.with_memory_space_constraint, memory_space=pltpu.HBM)
+    pair_shapes = (jax.ShapeDtypeStruct((2, slots, bs, nocc), BF16),) * near
+    partner = swap(theta_blocks, step)
+    rows, mask, draws, where, cols, *pairs = pl.pallas_call(
+        pick_pair_kernel,
+        out_shape=(
+            jax.ShapeDtypeStruct((slots, bs, nocc), BF16),
+            jax.ShapeDtypeStruct((slots, bs, bs), F32),
+            jax.ShapeDtypeStruct((8, gs), F32),
+            jax.ShapeDtypeStruct((3 * blocks,), jnp.int32),
+            jax.ShapeDtypeStruct((half * slots,), jnp.int32),
+            *pair_shapes,
+        ),
+        in_specs=[HBM] * 5 + [ANY] + [HBM] * 2,
+        out_specs=(VMEM, VMEM, VMEM, SMEM, SMEM) + (VMEM,) * near,
+        scratch_shapes=[
+            pltpu.SMEM(tile_info.shape, jnp.int32),
+            pltpu.SMEM(tile_count.shape, jnp.int32),
+            pltpu.SMEM(block_size.shape, jnp.int32),
+            pltpu.VMEM(fields.shape, F32),
+            pltpu.SemaphoreType.DMA((4 + slots,)),
+            pltpu.SemaphoreType.DMA((near,)),
+        ],
+        compiler_params=params,
+        cost_estimate=pl.CostEstimate(flops=0, bytes_accessed=8 * chol.size, transcendentals=0),
+        name="pick",
+    )(
+        *map(hbm, (tile_info, tile_count, block_size, fields, theta_blocks)),
+        swap(theta_blocks, 1),
+        *map(hbm, (trial, chol)),
+    )
+    received = spread(pairs)
+    partner, *received = lax.optimization_barrier((partner, *received))
+    far = pl.pallas_call(
+        spread_far_kernel,
+        out_shape=jax.ShapeDtypeStruct((half, slots, bs, nocc), BF16),
+        in_specs=[SMEM, VMEM, HBM],
+        out_specs=VMEM,
+        compiler_params=params,
+        cost_estimate=pl.CostEstimate(flops=0, bytes_accessed=8 * chol.size, transcendentals=0),
+        name="spread",
+    )(cols, partner, hbm(chol))
+    groups = [list(range(half)), list(range(half, owners))]
+    far = to_all(far, groups)
+
+    part = pl.pallas_call(
+        functools.partial(bias_pair_kernel, step),
+        out_shape=jax.ShapeDtypeStruct((owners, owners, gs), F32),
+        in_specs=[VMEM] * (5 + near),
+        out_specs=VMEM,
+        scratch_shapes=[pltpu.VMEM((slots, bs * owners, bs), F32), pltpu.VMEM((owners, gs), F32)],
+        compiler_params=params,
+        name="bias",
+    )(rows, mask, draws, chol, far, *received)
+
+    operators, own_bias = pl.pallas_call(
+        operator_pair_kernel,
+        out_shape=(
+            jax.ShapeDtypeStruct((owners, 1, slots, bs, bs), BF16),
+            jax.ShapeDtypeStruct((1, gs), F32),
+        ),
+        in_specs=[VMEM] * 4,
+        out_specs=(VMEM, VMEM),
+        scratch_shapes=[pltpu.VMEM((owners, gs), F32), pltpu.VMEM((slots, owners * bs, bs), F32)],
+        compiler_params=params,
+        name="operator",
+    )(to_all(part), draws, mask, chol)
+
+    propagated = pl.pallas_call(
+        update_kernel,
+        out_shape=jax.ShapeDtypeStruct(theta_blocks.shape, BF16),
+        in_specs=[SMEM, VMEM, VMEM],
+        out_specs=VMEM,
+        compiler_params=params,
+        name="update",
+    )(where, theta_blocks, to_all(operators))
+    return propagated.reshape(theta.shape), own_bias
+
+
+def per_device(theta, trial, chol, fields, tile_info, tile_count, block_size):
+    short = lax.axis_size("blk") in (8, 16)
+    one_slab = fields.shape[1] == chol.shape[1]
+    plan = short_axis if short and one_slab and theta.shape[0] == 1 else long_axis
+    return plan(theta, trial, chol, fields, tile_info, tile_count, block_size)
+
+
 def solution(mesh):
     placed = (
         P(("grp", "blk"), None, None),

time: 84.9 us -> 79.4 us (0.935)
  blocking collectives: 73.6 us -> 52.5 us
  waiting for transfers between devices: 0 us -> 8.24 us
  starting transfers between devices: 0 us -> 7.62 us
    all_to_all x3, blocking collectives: 73.6 us -> 52.5 us  [to_all(): lax.all_to_all(x, 'blk', split_axis=0, concat_axis=0, tiled=True, axis_in...]
    ppermute x0 -> x5, waiting for transfers between devices: none -> 8.24 us  [swap(): return lax.ppermute(x, 'blk', [(i, i ^ step) for i in range(owners)])]
    ppermute x0 -> x5, starting transfers between devices: none -> 7.62 us  [swap(): return lax.ppermute(x, 'blk', [(i, i ^ step) for i in range(owners)])]
    pallas_call x4 -> x5, Pallas kernels: 10.5 us -> 10 us  [the longest x1 2.95 us: short_axis(): pl.pallas_call(functools.partial(bias_pair_kernel, step), out_shape=jax.S...]
  transfers between devices with their start and end apart: 0 -> 5, of which waited for: 0 -> 4; matrix products, arithmetic and copies ran while one was open for 0% -> 0% of each run, Pallas kernels for 0% -> 3%
where the time goes in v4:
time: 79.4 us; the launch traced here: 79 us
  blocking collectives  52.5 us (66%)
  Pallas kernels  10 us (13%)
  waiting for transfers between devices  8.24 us (10%)
  starting transfers between devices  7.62 us (10%)
    all_to_all x3, blocking collectives, to_all(): lax.all_to_all(x, 'blk', split_axis=0, concat_axis=0, tiled=True, axis_in...  52.5 us
    ppermute x5, waiting for transfers between devices, swap(): return lax.ppermute(x, 'blk', [(i, i ^ step) for i in range(owners)])  8.24 us
    ppermute x5, starting transfers between devices, swap(): return lax.ppermute(x, 'blk', [(i, i ^ step) for i in range(owners)])  7.62 us
    pallas_call x1, Pallas kernels, short_axis(): pl.pallas_call(functools.partial(bias_pair_kernel, step), out_shape=jax.S...  2.95 us
    pallas_call x1, Pallas kernels, short_axis(): pl.pallas_call(pick_pair_kernel, out_shape=(jax.ShapeDtypeStruct((slots,...  2.67 us
    pallas_call x1, Pallas kernels, short_axis(): pl.pallas_call(operator_pair_kernel, out_shape=(jax.ShapeDtypeStruct((own...  2.24 us
    pallas_call x1, Pallas kernels, short_axis(): pl.pallas_call(update_kernel, out_shape=jax.ShapeDtypeStruct(theta_blocks...  1.59 us
  transfers between devices with their start and end apart: 5, of which 4 were waited for; matrix products, arithmetic and copies ran while one was open for 0% of the time, Pallas kernels for 3%

profile of v4, /device:TPU:1, one launch (start us, length us, event | category | flops | bytes accessed | tf_op | source)
XLA Modules:
  0.0 79.0 jit_solution(17969439590467880462)
XLA Ops:
  0.6 0.0 slice-start
  0.6 0.1 collective-permute-start
  0.8 4.8 %collective-permute-start.1 = (bf16[1,8,128,128]{3,2,1,0:T(8,128)(2,1)}, bf16[1,8,128,128]{3,2,1,0:T(8,128)(2,1)S(1)}, u32[]{:S(2)}, u32[]{:S(2)}) collective-permute-start(bf16[1,8,128,128]{3,2,1,0:T(8,128)(2,1)} %bitcast.5), channel_id=1, source_target_pairs={{0,12},{1,13},{2,14},{3,15},{4,8},{5,9},{6,10},{7,11},{8,4},{9,5},... | collective-permute-start | bytes 786440 | tf_op jit(solution)/shard_map/ppermute | solution.py:411
  5.6 0.0 collective-permute-done.refs_5_
  5.6 2.7 %pick.1 = (bf16[2,128,128]{2,1,0:T(8,128)(2,1)S(1)}, f32[2,128,128]{2,1,0:T(8,128)S(1)}, f32[8,128]{1,0:T(8,128)S(1)}, s32[24]{0:T(128)S(1)}, s32[16]{0:T(128)S(...) custom-call(s32[3,32]{1,0:T(4,128)} %refs_0_.1, ...), custom_call_target="tpu_custom_call" | custom-call | bytes 33554432 | tf_op jit(solution)/shard_map/pick/pallas_call | solution.py:422
  8.2 1.2 %collective-permute-start.2 = (bf16[2,2,128,128]{3,2,1,0:T(8,128)(2,1)S(1)}, bf16[2,2,128,128]{3,2,1,0:T(8,128)(2,1)S(1)}, u32[]{:S(2)}, u32[]{:S(2)}) collective-permute-start(bf16[2,2,128,128]{3,2,1,0:T(8,128)(2,1)S(1)} %get-tuple-element.24), channel_id=1, source_target_pairs={{0,2},{1,3},{2,0},{3,1},{4,6},{5,7},{6,4},{7,5},{8,10},{9,11},{10,... | collective-permute-start | bytes 393224 | tf_op jit(solution)/shard_map/ppermute | solution.py:411
  9.5 0.0 collective-permute-start.3
  9.5 1.5 %collective-permute-start.4 = (bf16[2,2,128,128]{3,2,1,0:T(8,128)(2,1)S(1)}, bf16[2,2,128,128]{3,2,1,0:T(8,128)(2,1)S(1)}, u32[]{:S(2)}, u32[]{:S(2)}) collective-permute-start(bf16[2,2,128,128]{3,2,1,0:T(8,128)(2,1)S(1)} %get-tuple-element.26), channel_id=1, source_target_pairs={{0,6},{1,7},{2,4},{3,5},{4,2},{5,3},{6,0},{7,1},{8,14},{9,15},{10,... | collective-permute-start | bytes 393224 | tf_op jit(solution)/shard_map/ppermute | solution.py:411
  10.9 1.4 %collective-permute-done.1.theta_ref = bf16[1,8,128,128]{3,2,1,0:T(8,128)(2,1)S(1)} collective-permute-done((bf16[1,8,128,128]{3,2,1,0:T(8,128)(2,1)}, bf16[1,8,128,128]{3,2,1,0:T(8,128)(2,1)S(1)}, u32[]{:S(2)}, u32[]{:S(2)}) %collective-permute-start.1) | collective-permute-done | bytes 262176 | tf_op jit(solution)/shard_map/ppermute | solution.py:411
  12.4 0.7 collective-permute-done.2.refs_1_
  13.1 1.8 %collective-permute-done.3.refs_2_ = bf16[2,2,128,128]{3,2,1,0:T(8,128)(2,1)S(1)} collective-permute-done((bf16[2,2,128,128]{3,2,1,0:T(8,128)(2,1)S(1)}, bf16[2,2,128,128]{3,2,1,0:T(8,128)(2,1)S(1)}, u32[]{:S(2)}, u32[]{:S(2)}) %collective-permute-start.3) | collective-permute-done | bytes 131104 | tf_op jit(solution)/shard_map/ppermute | solution.py:411
  14.9 4.2 %collective-permute-done.4.refs_3_ = bf16[2,2,128,128]{3,2,1,0:T(8,128)(2,1)S(1)} collective-permute-done((bf16[2,2,128,128]{3,2,1,0:T(8,128)(2,1)S(1)}, bf16[2,2,128,128]{3,2,1,0:T(8,128)(2,1)S(1)}, u32[]{:S(2)}, u32[]{:S(2)}) %collective-permute-start.4) | collective-permute-done | bytes 131104 | tf_op jit(solution)/shard_map/ppermute | solution.py:411
  19.2 0.0 slice-start.1
  19.2 0.6 spread.1
  19.8 11.6 %all_to_all.15.far_ref = bf16[8,2,128,128]{3,2,1,0:T(8,128)(2,1)S(1)} all-to-all(bf16[8,2,128,128]{3,2,1,0:T(8,128)(2,1)S(1)} %spread.1), channel_id=1, replica_groups={{0,1,2,3,4,5,6,7},{8,9,10,11,12,13,14,15},{16,17,18,19,20,21,22,23},{24..., dimensions={0} | all-to-all | bytes 1048576 | tf_op jit(solution)/shard_map/all_to_all | solution.py:414
  31.4 0.0 slice-done
  31.4 0.0 slice-done.1
  31.4 0.0 copy-start
  31.4 3.0 %bias.1 = f32[16,16,128]{2,1,0:T(8,128)S(1)} custom-call(bf16[2,128,128]{2,1,0:T(8,128)(2,1)S(1)} %get-tuple-element.19.rows_ref, f32[2,128,128]{2,1,0:T(8,128)S(1)} %get-tuple-element.20.mask_ref, f32[8,128]{1,0:T(8,128)S(1)} %get-tuple-element.21.draws_ref.fields_ref, bf16[2,128,16384]{2,1,0:T(8,128)(2,1)S(1)} %bitcast.3, ...), custom_call_target="tpu_custom_call" | custom-call | tf_op jit(solution)/shard_map/bias/pallas_call | solution.py:464
  34.3 12.0 %all_to_all.16.shift_ref = f32[16,16,128]{2,1,0:T(8,128)S(1)} all-to-all(f32[16,16,128]{2,1,0:T(8,128)S(1)} %bias.1), channel_id=1, replica_groups=mesh['grp'=2,'blk'=16] {'blk'}, dimensions={0} | all-to-all | bytes 262144 | tf_op jit(solution)/shard_map/all_to_all | solution.py:414
  46.4 2.2 %operator.1 = (bf16[16,1,2,128,128]{4,3,2,1,0:T(8,128)(2,1)S(1)}, f32[1,128]{1,0:T(1,128)}) custom-call(f32[16,16,128]{2,1,0:T(8,128)S(1)} %all_to_all.16.shift_ref, f32[8,128]{1,0:T(8,128)S(1)} %get-tuple-element.21.draws_ref.fields_ref, f32[2,128,128]{2,1,0:T(8,128)S(1)} %get-tuple-element.20.mask_ref, bf16[2,128,16384]{2,1,0:T(8,128)(2,1)S(1)} %bitcast.3), custom_call_target="tpu_custom_call" | custom-call | tf_op jit(solution)/shard_map/operator/pallas_call | solution.py:474
  48.6 28.8 %all_to_all.17.oper_ref = bf16[16,1,2,128,128]{4,3,2,1,0:T(8,128)(2,1)S(1)} all-to-all(bf16[16,1,2,128,128]{4,3,2,1,0:T(8,128)(2,1)S(1)} %get-tuple-element.32), channel_id=1, replica_groups=mesh['grp'=2,'blk'=16] {'blk'}, dimensions={0} | all-to-all | bytes 2097152 | tf_op jit(solution)/shard_map/all_to_all | solution.py:414
  77.4 0.0 copy-done
  77.4 1.6 %update.1 = bf16[1,8,128,128]{3,2,1,0:T(8,128)(2,1)} custom-call(s32[24]{0:T(128)S(1)} %get-tuple-element.18.where_ref, bf16[1,8,128,128]{3,2,1,0:T(8,128)(2,1)S(1)} %bitcast.7, bf16[16,1,2,128,128]{4,3,2,1,0:T(8,128)(2,1)S(1)} %all_to_all.17.oper_ref), custom_call_target="tpu_custom_call" | custom-call | tf_op jit(solution)/shard_map/update/pallas_call | solution.py:487
  (1 shorter events, 0.0 us)
Async XLA Ops:
  0.6 30.7 %slice-start = ((s8[8388608]{0:T(1024)(128)(4,1)}), s8[4194304]{0:T(1024)(128)(4,1)S(1)}, s32[]{:S(2)}) async-start(s8[8388608]{0:T(1024)(128)(4,1)} %bitcast.2), calls=%async_computation.3 | async-start | bytes 8388608
  0.6 4.9 %collective-permute-start = (bf16[1,8,128,128]{3,2,1,0:T(8,128)(2,1)}, bf16[1,8,128,128]{3,2,1,0:T(8,128)(2,1)S(1)}, u32[]{:S(2)}, u32[]{:S(2)}) collective-permute-start(bf16[1,8,128,128]{3,2,1,0:T(8,128)(2,1)} %bitcast.4), channel_id=1, source_target_pairs={{0,1},{1,0},{2,3},{3,2},{4,5},{5,4},{6,7},{7,6},{8,9},{9,8},{10,11... | collective-permute-start | bytes 786440 | tf_op jit(solution)/shard_map/ppermute | solution.py:411
  0.8 11.6 %collective-permute-start.1 = (bf16[1,8,128,128]{3,2,1,0:T(8,128)(2,1)}, bf16[1,8,128,128]{3,2,1,0:T(8,128)(2,1)S(1)}, u32[]{:S(2)}, u32[]{:S(2)}) collective-permute-start(bf16[1,8,128,128]{3,2,1,0:T(8,128)(2,1)} %bitcast.5), channel_id=1, source_target_pairs={{0,12},{1,13},{2,14},{3,15},{4,8},{5,9},{6,10},{7,11},{8,4},{9,5},... | collective-permute-start | bytes 786440 | tf_op jit(solution)/shard_map/ppermute | solution.py:411
  8.2 4.9 %collective-permute-start.2 = (bf16[2,2,128,128]{3,2,1,0:T(8,128)(2,1)S(1)}, bf16[2,2,128,128]{3,2,1,0:T(8,128)(2,1)S(1)}, u32[]{:S(2)}, u32[]{:S(2)}) collective-permute-start(bf16[2,2,128,128]{3,2,1,0:T(8,128)(2,1)S(1)} %get-tuple-element.24), channel_id=1, source_target_pairs={{0,2},{1,3},{2,0},{3,1},{4,6},{5,7},{6,4},{7,5},{8,10},{9,11},{10,... | collective-permute-start | bytes 393224 | tf_op jit(solution)/shard_map/ppermute | solution.py:411
  9.5 5.5 %collective-permute-start.3 = (bf16[2,2,128,128]{3,2,1,0:T(8,128)(2,1)S(1)}, bf16[2,2,128,128]{3,2,1,0:T(8,128)(2,1)S(1)}, u32[]{:S(2)}, u32[]{:S(2)}) collective-permute-start(bf16[2,2,128,128]{3,2,1,0:T(8,128)(2,1)S(1)} %get-tuple-element.25), channel_id=1, source_target_pairs={{0,4},{1,5},{2,6},{3,7},{4,0},{5,1},{6,2},{7,3},{8,12},{9,13},{10,... | collective-permute-start | bytes 393224 | tf_op jit(solution)/shard_map/ppermute | solution.py:411
  9.5 9.7 %collective-permute-start.4 = (bf16[2,2,128,128]{3,2,1,0:T(8,128)(2,1)S(1)}, bf16[2,2,128,128]{3,2,1,0:T(8,128)(2,1)S(1)}, u32[]{:S(2)}, u32[]{:S(2)}) collective-permute-start(bf16[2,2,128,128]{3,2,1,0:T(8,128)(2,1)S(1)} %get-tuple-element.26), channel_id=1, source_target_pairs={{0,6},{1,7},{2,4},{3,5},{4,2},{5,3},{6,0},{7,1},{8,14},{9,15},{10,... | collective-permute-start | bytes 393224 | tf_op jit(solution)/shard_map/ppermute | solution.py:411
  19.2 12.2 %slice-start.1 = ((s8[8388608]{0:T(1024)(128)(4,1)}), s8[4194304]{0:T(1024)(128)(4,1)S(1)}, s32[]{:S(2)}) async-start(s8[8388608]{0:T(1024)(128)(4,1)} %bitcast.2), calls=%async_computation.4 | async-start | bytes 8388608
  31.4 46.1 %copy-start = (bf16[1,1024,128]{2,1,0:T(8,128)(2,1)S(1)}, bf16[1,1024,128]{2,1,0:T(8,128)(2,1)}, u32[]{:S(2)}) copy-start(bf16[1,1024,128]{2,1,0:T(8,128)(2,1)} %param.7) | copy-start | bytes 786436

commit v5 on v4

--- a/solution.py
+++ b/solution.py
@@ -267,14 +267,33 @@
     return propagated.reshape(theta.shape), own_bias
 
 
-def pick_pair_kernel(*refs):
-    info_hbm, count_hbm, size_hbm, fields_hbm, theta_ref, other_ref, trial_ref, _ = refs[:8]
-    rows_ref, mask_ref, draws_ref, where_ref, cols_ref = refs[8:13]
-    info_ref, count_ref, size_ref, fields_ref, sems, send_sems = refs[-6:]
-    pair_refs = refs[13:-6]
+def pick_pair_kernel(info_hbm, theta_hbm, other_ref, _, *refs):
+    pair_refs = refs[:-3]
+    info_ref, theta_ref, sems = refs[-3:]
+    slots = pair_refs[0].shape[1]
+    copies = [
+        pltpu.make_async_copy(info_hbm, info_ref, sems.at[0]),
+        pltpu.make_async_copy(theta_hbm, theta_ref, sems.at[1]),
+    ]
+    for copy in copies:
+        copy.start()
+    me = lax.axis_index("blk")
+    core = me % 2
+    for copy in copies:
+        copy.wait()
+    for r, ref in enumerate(pair_refs):
+        for j in range(slots):
+            block = info_ref[1, (me ^ (2 * r)) * slots + j]
+            ref[core, j] = theta_ref[0, block]
+            ref[1 - core, j] = other_ref[0, block]
+
+
+def prepare_kernel(
+    info_hbm, count_hbm, size_hbm, fields_hbm, trial_ref,
+    rows_ref, mask_ref, draws_ref, where_ref, cols_ref, info_ref, count_ref, size_ref, fields_ref, sems,
+):
     slots, bs, _ = rows_ref.shape
     owners = count_ref.shape[0]
-    blocks = theta_ref.shape[1]
     small = [
         pltpu.make_async_copy(source, target, sems.at[n])
         for n, (source, target) in enumerate(
@@ -284,16 +303,8 @@
     for copy in small:
         copy.start()
     me = lax.axis_index("blk")
-    core = me % 2
-    small[0].wait()
-    for r, ref in enumerate(pair_refs):
-        for j in range(slots):
-            block = info_ref[1, (me ^ (2 * r)) * slots + j]
-            pltpu.make_async_copy(theta_ref.at[0, block], ref.at[core, j], send_sems.at[r]).start()
-            pltpu.make_async_copy(other_ref.at[0, block], ref.at[1 - core, j], send_sems.at[r]).start()
-    first = me // (owners // 2) * (owners // 2) * slots
-    for n in range(owners // 2 * slots):
-        cols_ref[n] = info_ref[1, first + n]
+    for copy in small:
+        copy.wait()
     trial = []
     for j in range(slots):
         block = info_ref[0, me * slots + j]
@@ -303,8 +314,9 @@
             )
         )
         trial[-1].start()
-    for copy in small[1:]:
-        copy.wait()
+    first = me // (owners // 2) * (owners // 2) * slots
+    for n in range(owners // 2 * slots):
+        cols_ref[n] = info_ref[1, first + n]
     live = count_ref[me]
     for j in range(slots):
         row_size = jnp.where(j < live, size_ref[info_ref[0, me * slots + j]], 0)
@@ -321,8 +333,6 @@
                 row_block = info_ref[0, s]
                 where_ref[row_block * 3 + info_ref[1, s] - row_block + 1] = jnp.int32(s)
 
-    for r, ref in enumerate(pair_refs):
-        pltpu.make_async_copy(ref, ref, send_sems.at[r]).wait()
     for copy in trial:
         copy.wait()
 
@@ -341,6 +351,7 @@
     walkers = 2 * half
     me = lax.axis_index("blk")
     first = me // half * half
+    pitch = walkers + 1
     for slot in range(slots):
         mask = mask_ref[slot]
         for blocks, start in [(ref[:, slot], 2 * r) for r, ref in enumerate(pair_refs)] + [(far_ref[:, slot], half)]:
@@ -349,14 +360,14 @@
                 rows_ref[slot], blocks.reshape(count * bs, nocc), NT, preferred_element_type=F32
             )
             for n in range(count):
-                green_ref[slot, pl.ds(start + n, bs, stride=walkers), :] = green[:, n * bs : (n + 1) * bs] * mask
+                green_ref[slot, pl.ds(start + n, bs, stride=pitch), :] = green[:, n * bs : (n + 1) * bs] * mask
     per = bs // PIECES
     tall = jnp.zeros((chol_ref.shape[1], walkers), F32)
     wide = jnp.zeros((walkers, chol_ref.shape[1]), F32)
     for c in range(PIECES):
         for slot in range(slots):
             green = jnp.concatenate(
-                [green_ref[slot, pl.ds((c * per + p) * walkers, walkers), :].astype(BF16) for p in range(per)],
+                [green_ref[slot, pl.ds((c * per + p) * pitch, walkers), :].astype(BF16) for p in range(per)],
                 axis=1,
             )
             tile = chol_ref[slot, :, pl.ds(c * per * bs, per * bs)]
@@ -384,14 +395,15 @@
     total_ref[pl.ds(me, 1), :] = own + fields_ref[0:1, :]
     left = total_ref[...].astype(BF16)
     per = bs // PIECES
+    pitch = bs + 8
     for slot in range(slots):
         for c in range(PIECES):
             right = chol_ref[slot, :, pl.ds(c * per * bs, per * bs)]
             oper = jnp.dot(left, right, preferred_element_type=F32) * STEP_ROOT
             for p in range(per):
-                oper_ref[slot, pl.ds(c * per + p, walkers, stride=bs), :] = oper[:, p * bs : (p + 1) * bs]
+                oper_ref[slot, pl.ds(c * per + p, walkers, stride=pitch), :] = oper[:, p * bs : (p + 1) * bs]
         for w in range(walkers):
-            block = oper_ref[slot, pl.ds(w * bs, bs), :]
+            block = oper_ref[slot, pl.ds(w * pitch, bs), :]
             out_ref[w, 0, slot] = (block * mask_ref[slot]).astype(BF16)
 
 
@@ -419,46 +431,54 @@
     hbm = functools.partial(pltpu.with_memory_space_constraint, memory_space=pltpu.HBM)
     pair_shapes = (jax.ShapeDtypeStruct((2, slots, bs, nocc), BF16),) * near
     partner = swap(theta_blocks, step)
-    rows, mask, draws, where, cols, *pairs = pl.pallas_call(
+    load = pl.CostEstimate(flops=0, bytes_accessed=8 * chol.size, transcendentals=0)
+    pairs = pl.pallas_call(
         pick_pair_kernel,
+        out_shape=pair_shapes,
+        in_specs=[HBM, HBM, VMEM, HBM],
+        out_specs=(VMEM,) * near,
+        scratch_shapes=[
+            pltpu.SMEM(tile_info.shape, jnp.int32),
+            pltpu.VMEM(theta_blocks.shape, BF16),
+            pltpu.SemaphoreType.DMA((2,)),
+        ],
+        compiler_params=params,
+        cost_estimate=load,
+        name="pick",
+    )(hbm(tile_info), hbm(theta_blocks), swap(theta_blocks, 1), hbm(chol))
+    rows, mask, draws, where, cols = pl.pallas_call(
+        prepare_kernel,
         out_shape=(
             jax.ShapeDtypeStruct((slots, bs, nocc), BF16),
             jax.ShapeDtypeStruct((slots, bs, bs), F32),
             jax.ShapeDtypeStruct((8, gs), F32),
             jax.ShapeDtypeStruct((3 * blocks,), jnp.int32),
             jax.ShapeDtypeStruct((half * slots,), jnp.int32),
-            *pair_shapes,
         ),
-        in_specs=[HBM] * 5 + [ANY] + [HBM] * 2,
-        out_specs=(VMEM, VMEM, VMEM, SMEM, SMEM) + (VMEM,) * near,
+        in_specs=[HBM] * 5,
+        out_specs=(VMEM, VMEM, VMEM, SMEM, SMEM),
         scratch_shapes=[
             pltpu.SMEM(tile_info.shape, jnp.int32),
             pltpu.SMEM(tile_count.shape, jnp.int32),
             pltpu.SMEM(block_size.shape, jnp.int32),
             pltpu.VMEM(fields.shape, F32),
             pltpu.SemaphoreType.DMA((4 + slots,)),
-            pltpu.SemaphoreType.DMA((near,)),
         ],
         compiler_params=params,
-        cost_estimate=pl.CostEstimate(flops=0, bytes_accessed=8 * chol.size, transcendentals=0),
-        name="pick",
-    )(
-        *map(hbm, (tile_info, tile_count, block_size, fields, theta_blocks)),
-        swap(theta_blocks, 1),
-        *map(hbm, (trial, chol)),
-    )
+        name="prepare",
+    )(*map(hbm, (tile_info, tile_count, block_size, fields, trial)))
     received = spread(pairs)
-    partner, *received = lax.optimization_barrier((partner, *received))
     far = pl.pallas_call(
         spread_far_kernel,
         out_shape=jax.ShapeDtypeStruct((half, slots, bs, nocc), BF16),
         in_specs=[SMEM, VMEM, HBM],
         out_specs=VMEM,
         compiler_params=params,
-        cost_estimate=pl.CostEstimate(flops=0, bytes_accessed=8 * chol.size, transcendentals=0),
+        cost_estimate=load,
         name="spread",
     )(cols, partner, hbm(chol))
     groups = [list(range(half)), list(range(half, owners))]
+    far, *received = lax.optimization_barrier((far, *received))
     far = to_all(far, groups)
 
     part = pl.pallas_call(
@@ -466,7 +486,7 @@
         out_shape=jax.ShapeDtypeStruct((owners, owners, gs), F32),
         in_specs=[VMEM] * (5 + near),
         out_specs=VMEM,
-        scratch_shapes=[pltpu.VMEM((slots, bs * owners, bs), F32), pltpu.VMEM((owners, gs), F32)],
+        scratch_shapes=[pltpu.VMEM((slots, (bs + 1) * (owners + 1), bs), F32), pltpu.VMEM((owners, gs), F32)],
         compiler_params=params,
         name="bias",
     )(rows, mask, draws, chol, far, *received)
@@ -479,7 +499,7 @@
         ),
         in_specs=[VMEM] * 4,
         out_specs=(VMEM, VMEM),
-        scratch_shapes=[pltpu.VMEM((owners, gs), F32), pltpu.VMEM((slots, owners * bs, bs), F32)],
+        scratch_shapes=[pltpu.VMEM((owners, gs), F32), pltpu.VMEM((slots, (owners + 1) * (bs + 8), bs), F32)],
         compiler_params=params,
         name="operator",
     )(to_all(part), draws, mask, chol)

time: 79.4 us -> 77.7 us (0.979)
  waiting for transfers between devices: 8.24 us -> 7.01 us
    ppermute x5, waiting for transfers between devices: 8.24 us -> 7.01 us  [swap(): return lax.ppermute(x, 'blk', [(i, i ^ step) for i in range(owners)])]
    pallas_call x1 -> x2, Pallas kernels: 2.67 us -> 3.3 us  [the longest x1 2.27 us: short_axis(): pl.pallas_call(prepare_kernel, out_shape=(jax.ShapeDtypeStruct((slots, bs...]
  transfers between devices with their start and end apart: 5 -> 5, of which waited for: 4 -> 3; matrix products, arithmetic and copies ran while one was open for 0% -> 0% of each run, Pallas kernels for 3% -> 5%
where the time goes in v5:
time: 77.7 us; the launch traced here: 77.4 us
  blocking collectives  52.3 us (67%)
  Pallas kernels  9.77 us (13%)
  starting transfers between devices  7.62 us (10%)
  waiting for transfers between devices  7.01 us (9%)
    all_to_all x3, blocking collectives, to_all(): lax.all_to_all(x, 'blk', split_axis=0, concat_axis=0, tiled=True, axis_in...  52.3 us
    ppermute x5, starting transfers between devices, swap(): return lax.ppermute(x, 'blk', [(i, i ^ step) for i in range(owners)])  7.62 us
    ppermute x5, waiting for transfers between devices, swap(): return lax.ppermute(x, 'blk', [(i, i ^ step) for i in range(owners)])  7.01 us
    pallas_call x1, Pallas kernels, short_axis(): pl.pallas_call(functools.partial(bias_pair_kernel, step), out_shape=jax.S...  2.55 us
    pallas_call x1, Pallas kernels, short_axis(): pl.pallas_call(prepare_kernel, out_shape=(jax.ShapeDtypeStruct((slots, bs...  2.27 us
    pallas_call x1, Pallas kernels, short_axis(): pl.pallas_call(operator_pair_kernel, out_shape=(jax.ShapeDtypeStruct((own...  1.76 us
    pallas_call x1, Pallas kernels, short_axis(): pl.pallas_call(update_kernel, out_shape=jax.ShapeDtypeStruct(theta_blocks...  1.58 us
  transfers between devices with their start and end apart: 5, of which 3 were waited for; matrix products, arithmetic and copies ran while one was open for 0% of the time, Pallas kernels for 5%

profile of v5, /device:TPU:1, one launch (start us, length us, event | category | flops | bytes accessed | tf_op | source)
XLA Modules:
  0.0 77.4 jit_solution(3448964644478962441)
XLA Ops:
  0.6 0.0 slice-start
  0.6 0.1 collective-permute-start.1
  0.8 4.8 %collective-permute-start = (bf16[1,8,128,128]{3,2,1,0:T(8,128)(2,1)}, bf16[1,8,128,128]{3,2,1,0:T(8,128)(2,1)S(1)}, u32[]{:S(2)}, u32[]{:S(2)}) collective-permute-start(bf16[1,8,128,128]{3,2,1,0:T(8,128)(2,1)} %bitcast.5), channel_id=1, source_target_pairs={{0,12},{1,13},{2,14},{3,15},{4,8},{5,9},{6,10},{7,11},{8,4},{9,5},... | collective-permute-start | bytes 786440 | tf_op jit(solution)/shard_map/ppermute | solution.py:423
  5.5 0.0 collective-permute-done.1.other_ref
  5.6 1.0 %pick.1 = (bf16[2,2,128,128]{3,2,1,0:T(8,128)(2,1)S(1)}, bf16[2,2,128,128]{3,2,1,0:T(8,128)(2,1)S(1)}, bf16[2,2,128,128]{3,2,1,0:T(8,128)(2,1)S(1)}, bf16[2,2,128,128]{3,2,1,0:T(8,128)(2,1)S(1)}) custom-call(s32[3,32]{1,0:T(4,128)} %info_hbm.3, bf16[1,8,128,128]{3,2,1,0:T(8,128)(2,1)} %bitcast.6, ...), custom_call_target="tpu_custom_call" | custom-call | bytes 33554432 | tf_op jit(solution)/shard_map/pick/pallas_call | solution.py:435
  6.6 1.3 %collective-permute-start.2 = (bf16[2,2,128,128]{3,2,1,0:T(8,128)(2,1)S(1)}, bf16[2,2,128,128]{3,2,1,0:T(8,128)(2,1)S(1)}, u32[]{:S(2)}, u32[]{:S(2)}) collective-permute-start(bf16[2,2,128,128]{3,2,1,0:T(8,128)(2,1)S(1)} %get-tuple-element.24), channel_id=1, source_target_pairs={{0,2},{1,3},{2,0},{3,1},{4,6},{5,7},{6,4},{7,5},{8,10},{9,11},{10,... | collective-permute-start | bytes 393224 | tf_op jit(solution)/shard_map/ppermute | solution.py:423
  7.9 0.0 collective-permute-start.3
  7.9 1.4 %collective-permute-start.4 = (bf16[2,2,128,128]{3,2,1,0:T(8,128)(2,1)S(1)}, bf16[2,2,128,128]{3,2,1,0:T(8,128)(2,1)S(1)}, u32[]{:S(2)}, u32[]{:S(2)}) collective-permute-start(bf16[2,2,128,128]{3,2,1,0:T(8,128)(2,1)S(1)} %get-tuple-element.26), channel_id=1, source_target_pairs={{0,6},{1,7},{2,4},{3,5},{4,2},{5,3},{6,0},{7,1},{8,14},{9,15},{10,... | collective-permute-start | bytes 393224 | tf_op jit(solution)/shard_map/ppermute | solution.py:423
  9.3 2.3 %prepare.1 = (bf16[2,128,128]{2,1,0:T(8,128)(2,1)S(1)}, f32[2,128,128]{2,1,0:T(8,128)S(1)}, f32[8,128]{1,0:T(8,128)S(1)}, s32[24]{0:T(128)S(1)}, s32[16]{0:T(128)S(1)}) custom-call(s32[3,32]{1,0:T(4,128)} %info_hbm.3, s32[16]{0:T(128)} %count_hbm.1, s32[8]{0:T(128)} %size_hbm.1, f32[1,128]{1,0:T(1,128)} %fields_hbm.1, bf16[1024,128]{1,0:T(8,128)(2,1)} %trial_ref.1), custom_call_target="tpu_custom_call" | custom-call | tf_op jit(solution)/shard_map/prepare/pallas_call | solution.py:449
  11.6 0.8 %collective-permute-done.theta_ref = bf16[1,8,128,128]{3,2,1,0:T(8,128)(2,1)S(1)} collective-permute-done((bf16[1,8,128,128]{3,2,1,0:T(8,128)(2,1)}, bf16[1,8,128,128]{3,2,1,0:T(8,128)(2,1)S(1)}, u32[]{:S(2)}, u32[]{:S(2)}) %collective-permute-start) | collective-permute-done | bytes 262176 | tf_op jit(solution)/shard_map/ppermute | solution.py:423
  12.4 0.0 slice-start.1
  12.4 0.6 spread.1
  13.0 0.0 collective-permute-done.2.refs_1_
  13.0 2.4 %collective-permute-done.3.refs_2_ = bf16[2,2,128,128]{3,2,1,0:T(8,128)(2,1)S(1)} collective-permute-done((bf16[2,2,128,128]{3,2,1,0:T(8,128)(2,1)S(1)}, bf16[2,2,128,128]{3,2,1,0:T(8,128)(2,1)S(1)}, u32[]{:S(2)}, u32[]{:S(2)}) %collective-permute-start.3) | collective-permute-done | bytes 131104 | tf_op jit(solution)/shard_map/ppermute | solution.py:423
  15.4 3.8 %collective-permute-done.4.refs_3_ = bf16[2,2,128,128]{3,2,1,0:T(8,128)(2,1)S(1)} collective-permute-done((bf16[2,2,128,128]{3,2,1,0:T(8,128)(2,1)S(1)}, bf16[2,2,128,128]{3,2,1,0:T(8,128)(2,1)S(1)}, u32[]{:S(2)}, u32[]{:S(2)}) %collective-permute-start.4) | collective-permute-done | bytes 131104 | tf_op jit(solution)/shard_map/ppermute | solution.py:423
  19.2 11.4 %all_to_all.15.far_ref = bf16[8,2,128,128]{3,2,1,0:T(8,128)(2,1)S(1)} all-to-all(bf16[8,2,128,128]{3,2,1,0:T(8,128)(2,1)S(1)} %spread.1), channel_id=1, replica_groups={{0,1,2,3,4,5,6,7},{8,9,10,11,12,13,14,15},{16,17,18,19,20,21,22,23},{24..., dimensions={0} | all-to-all | bytes 1048576 | tf_op jit(solution)/shard_map/all_to_all | solution.py:426
  30.6 0.0 slice-done
  30.6 0.0 slice-done.1
  30.6 2.5 %bias.1 = f32[16,16,128]{2,1,0:T(8,128)S(1)} custom-call(bf16[2,128,128]{2,1,0:T(8,128)(2,1)S(1)} %get-tuple-element.19.rows_ref, f32[2,128,128]{2,1,0:T(8,128)S(1)} %get-tuple-element.20.mask_ref, f32[8,128]{1,0:T(8,128)S(1)} %get-tuple-element.21.draws_ref.fields_ref, bf16[2,128,16384]{2,1,0:T(8,128)(2,1)S(1)} %bitcast.3, ...), custom_call_target="tpu_custom_call" | custom-call | tf_op jit(solution)/shard_map/bias/pallas_call | solution.py:484
  33.2 12.0 %all_to_all.16.shift_ref = f32[16,16,128]{2,1,0:T(8,128)S(1)} all-to-all(f32[16,16,128]{2,1,0:T(8,128)S(1)} %bias.1), channel_id=1, replica_groups=mesh['grp'=2,'blk'=16] {'blk'}, dimensions={0} | all-to-all | bytes 262144 | tf_op jit(solution)/shard_map/all_to_all | solution.py:426
  45.2 1.8 %operator.1 = (bf16[16,1,2,128,128]{4,3,2,1,0:T(8,128)(2,1)S(1)}, f32[1,128]{1,0:T(1,128)}) custom-call(f32[16,16,128]{2,1,0:T(8,128)S(1)} %all_to_all.16.shift_ref, f32[8,128]{1,0:T(8,128)S(1)} %get-tuple-element.21.draws_ref.fields_ref, f32[2,128,128]{2,1,0:T(8,128)S(1)} %get-tuple-element.20.mask_ref, bf16[2,128,16384]{2,1,0:T(8,128)(2,1)S(1)} %bitcast.3), custom_call_target="tpu_custom_call" | custom-call | tf_op jit(solution)/shard_map/operator/pallas_call | solution.py:494
  47.0 28.8 %all_to_all.17.oper_ref = bf16[16,1,2,128,128]{4,3,2,1,0:T(8,128)(2,1)S(1)} all-to-all(bf16[16,1,2,128,128]{4,3,2,1,0:T(8,128)(2,1)S(1)} %get-tuple-element.32), channel_id=1, replica_groups=mesh['grp'=2,'blk'=16] {'blk'}, dimensions={0} | all-to-all | bytes 2097152 | tf_op jit(solution)/shard_map/all_to_all | solution.py:426
  75.8 0.0 copy-done
  75.8 1.6 %update.1 = bf16[1,8,128,128]{3,2,1,0:T(8,128)(2,1)} custom-call(s32[24]{0:T(128)S(1)} %get-tuple-element.18.where_ref, bf16[1,8,128,128]{3,2,1,0:T(8,128)(2,1)S(1)} %bitcast.7, bf16[16,1,2,128,128]{4,3,2,1,0:T(8,128)(2,1)S(1)} %all_to_all.17.oper_ref), custom_call_target="tpu_custom_call" | custom-call | tf_op jit(solution)/shard_map/update/pallas_call | solution.py:507
  (2 shorter events, 0.0 us)
Async XLA Ops:
  0.6 30.0 %slice-start = ((s8[8388608]{0:T(1024)(128)(4,1)}), s8[4194304]{0:T(1024)(128)(4,1)S(1)}, s32[]{:S(2)}) async-start(s8[8388608]{0:T(1024)(128)(4,1)} %bitcast.2), calls=%async_computation.3 | async-start | bytes 8388608
  0.6 4.9 %collective-permute-start.1 = (bf16[1,8,128,128]{3,2,1,0:T(8,128)(2,1)}, bf16[1,8,128,128]{3,2,1,0:T(8,128)(2,1)S(1)}, u32[]{:S(2)}, u32[]{:S(2)}) collective-permute-start(bf16[1,8,128,128]{3,2,1,0:T(8,128)(2,1)} %bitcast.4), channel_id=1, source_target_pairs={{0,1},{1,0},{2,3},{3,2},{4,5},{5,4},{6,7},{7,6},{8,9},{9,8},{10,11... | collective-permute-start | bytes 786440 | tf_op jit(solution)/shard_map/ppermute | solution.py:423
  0.8 11.6 %collective-permute-start = (bf16[1,8,128,128]{3,2,1,0:T(8,128)(2,1)}, bf16[1,8,128,128]{3,2,1,0:T(8,128)(2,1)S(1)}, u32[]{:S(2)}, u32[]{:S(2)}) collective-permute-start(bf16[1,8,128,128]{3,2,1,0:T(8,128)(2,1)} %bitcast.5), channel_id=1, source_target_pairs={{0,12},{1,13},{2,14},{3,15},{4,8},{5,9},{6,10},{7,11},{8,4},{9,5},... | collective-permute-start | bytes 786440 | tf_op jit(solution)/shard_map/ppermute | solution.py:423
  6.6 6.4 %collective-permute-start.2 = (bf16[2,2,128,128]{3,2,1,0:T(8,128)(2,1)S(1)}, bf16[2,2,128,128]{3,2,1,0:T(8,128)(2,1)S(1)}, u32[]{:S(2)}, u32[]{:S(2)}) collective-permute-start(bf16[2,2,128,128]{3,2,1,0:T(8,128)(2,1)S(1)} %get-tuple-element.24), channel_id=1, source_target_pairs={{0,2},{1,3},{2,0},{3,1},{4,6},{5,7},{6,4},{7,5},{8,10},{9,11},{10,... | collective-permute-start | bytes 393224 | tf_op jit(solution)/shard_map/ppermute | solution.py:423
  7.9 7.5 %collective-permute-start.3 = (bf16[2,2,128,128]{3,2,1,0:T(8,128)(2,1)S(1)}, bf16[2,2,128,128]{3,2,1,0:T(8,128)(2,1)S(1)}, u32[]{:S(2)}, u32[]{:S(2)}) collective-permute-start(bf16[2,2,128,128]{3,2,1,0:T(8,128)(2,1)S(1)} %get-tuple-element.25), channel_id=1, source_target_pairs={{0,4},{1,5},{2,6},{3,7},{4,0},{5,1},{6,2},{7,3},{8,12},{9,13},{10,... | collective-permute-start | bytes 393224 | tf_op jit(solution)/shard_map/ppermute | solution.py:423
  7.9 11.3 %collective-permute-start.4 = (bf16[2,2,128,128]{3,2,1,0:T(8,128)(2,1)S(1)}, bf16[2,2,128,128]{3,2,1,0:T(8,128)(2,1)S(1)}, u32[]{:S(2)}, u32[]{:S(2)}) collective-permute-start(bf16[2,2,128,128]{3,2,1,0:T(8,128)(2,1)S(1)} %get-tuple-element.26), channel_id=1, source_target_pairs={{0,6},{1,7},{2,4},{3,5},{4,2},{5,3},{6,0},{7,1},{8,14},{9,15},{10,... | collective-permute-start | bytes 393224 | tf_op jit(solution)/shard_map/ppermute | solution.py:423
  12.4 18.2 %slice-start.1 = ((s8[8388608]{0:T(1024)(128)(4,1)}), s8[4194304]{0:T(1024)(128)(4,1)S(1)}, s32[]{:S(2)}) async-start(s8[8388608]{0:T(1024)(128)(4,1)} %bitcast.2), calls=%async_computation.4 | async-start | bytes 8388608
  30.6 45.2 %copy-start = (bf16[1,1024,128]{2,1,0:T(8,128)(2,1)S(1)}, bf16[1,1024,128]{2,1,0:T(8,128)(2,1)}, u32[]{:S(2)}) copy-start(bf16[1,1024,128]{2,1,0:T(8,128)(2,1)} %param.7) | copy-start | bytes 786436

commit v6 on v5

--- a/solution.py
+++ b/solution.py
@@ -289,7 +289,7 @@
 
 
 def prepare_kernel(
-    info_hbm, count_hbm, size_hbm, fields_hbm, trial_ref,
+    place, near_ring, info_hbm, count_hbm, size_hbm, fields_hbm, trial_ref,
     rows_ref, mask_ref, draws_ref, where_ref, cols_ref, info_ref, count_ref, size_ref, fields_ref, sems,
 ):
     slots, bs, _ = rows_ref.shape
@@ -314,9 +314,10 @@
             )
         )
         trial[-1].start()
-    first = me // (owners // 2) * (owners // 2) * slots
-    for n in range(owners // 2 * slots):
-        cols_ref[n] = info_ref[1, first + n]
+    first = me // len(near_ring) * len(near_ring)
+    for n, k in enumerate(near_ring):
+        for j in range(slots):
+            cols_ref[n * slots + j] = info_ref[1, (first + k) * slots + j]
     live = count_ref[me]
     for j in range(slots):
         row_size = jnp.where(j < live, size_ref[info_ref[0, me * slots + j]], 0)
@@ -329,9 +330,9 @@
         for j in range(slots):
 
             @pl.when(j < count_ref[o])
-            def _(s=o * slots + j):
+            def _(s=o * slots + j, n=place[o] * slots + j):
                 row_block = info_ref[0, s]
-                where_ref[row_block * 3 + info_ref[1, s] - row_block + 1] = jnp.int32(s)
+                where_ref[row_block * 3 + info_ref[1, s] - row_block + 1] = jnp.int32(n)
 
     for copy in trial:
         copy.wait()
@@ -344,7 +345,7 @@
             out_ref[k, j] = theta_ref[0, cols_ref[k * slots + j]]
 
 
-def bias_pair_kernel(step, rows_ref, mask_ref, draws_ref, chol_ref, far_ref, *refs):
+def bias_pair_kernel(step, ring, near_ring, rows_ref, mask_ref, draws_ref, chol_ref, far_ref, *refs):
     pair_refs = refs[:-3]
     out_ref, green_ref, total_ref = refs[-3:]
     half, slots, bs, nocc = far_ref.shape
@@ -377,16 +378,16 @@
                 tall += lax.dot_general(tile, green, NT, preferred_element_type=F32)
     total = -(tall.T + wide)
     for n in range(walkers):
-        walker = (me // 2 ^ (n // 2)) * 2 + n % 2 if n < half else (first + n - half) ^ step
+        walker = (me // 2 ^ (n // 2)) * 2 + n % 2 if n < half else (first + near_ring[n - half]) ^ step
         total_ref[pl.ds(walker, 1), :] = total[n : n + 1, :]
     total = total_ref[...]
     own = total_ref[pl.ds(me, 1), :]
-    for o in range(walkers):
-        out_ref[o] = total
-        out_ref[o, pl.ds(me, 1), :] = jnp.where(o == me, own, own + draws_ref[0:1, :])
-
-
-def operator_pair_kernel(shift_ref, fields_ref, mask_ref, chol_ref, out_ref, own_ref, total_ref, oper_ref):
+    for n, o in enumerate(ring):
+        out_ref[n] = total
+        out_ref[n, pl.ds(me, 1), :] = jnp.where(o == me, own, own + draws_ref[0:1, :])
+
+
+def operator_pair_kernel(place, shift_ref, fields_ref, mask_ref, chol_ref, out_ref, own_ref, total_ref, oper_ref):
     walkers, _, slots, bs, _ = out_ref.shape
     me = lax.axis_index("blk")
     total_ref[...] = sum(shift_ref[o] for o in range(walkers))
@@ -404,7 +405,7 @@
                 oper_ref[slot, pl.ds(c * per + p, walkers, stride=pitch), :] = oper[:, p * bs : (p + 1) * bs]
         for w in range(walkers):
             block = oper_ref[slot, pl.ds(w * pitch, bs), :]
-            out_ref[w, 0, slot] = (block * mask_ref[slot]).astype(BF16)
+            out_ref[place[w], 0, slot] = (block * mask_ref[slot]).astype(BF16)
 
 
 def short_axis(theta, trial, chol, fields, tile_info, tile_count, block_size):
@@ -416,6 +417,10 @@
     half = owners // 2
     step = half + half // 2
     near = half // 2
+    chips = [*range(1, half, 2), *range(0, half, 2)[::-1]]
+    ring = [2 * chip + core for chip in chips for core in (1, 0)]
+    place = [ring.index(o) for o in range(owners)]
+    near_ring = [2 * chip + core for chip in range(near) for core in (1, 0)]
     params = pltpu.CompilerParams(vmem_limit_bytes=LIMIT)
     theta_blocks = theta.reshape(1, blocks, bs, nocc)
 
@@ -447,7 +452,7 @@
         name="pick",
     )(hbm(tile_info), hbm(theta_blocks), swap(theta_blocks, 1), hbm(chol))
     rows, mask, draws, where, cols = pl.pallas_call(
-        prepare_kernel,
+        functools.partial(prepare_kernel, place, near_ring),
         out_shape=(
             jax.ShapeDtypeStruct((slots, bs, nocc), BF16),
             jax.ShapeDtypeStruct((slots, bs, bs), F32),
@@ -477,12 +482,12 @@
         cost_estimate=load,
         name="spread",
     )(cols, partner, hbm(chol))
-    groups = [list(range(half)), list(range(half, owners))]
+    groups = [near_ring, [half + k for k in near_ring]]
     far, *received = lax.optimization_barrier((far, *received))
     far = to_all(far, groups)
 
     part = pl.pallas_call(
-        functools.partial(bias_pair_kernel, step),
+        functools.partial(bias_pair_kernel, step, ring, near_ring),
         out_shape=jax.ShapeDtypeStruct((owners, owners, gs), F32),
         in_specs=[VMEM] * (5 + near),
         out_specs=VMEM,
@@ -492,7 +497,7 @@
     )(rows, mask, draws, chol, far, *received)
 
     operators, own_bias = pl.pallas_call(
-        operator_pair_kernel,
+        functools.partial(operator_pair_kernel, place),
         out_shape=(
             jax.ShapeDtypeStruct((owners, 1, slots, bs, bs), BF16),
             jax.ShapeDtypeStruct((1, gs), F32),
@@ -502,7 +507,7 @@
         scratch_shapes=[pltpu.VMEM((owners, gs), F32), pltpu.VMEM((slots, (owners + 1) * (bs + 8), bs), F32)],
         compiler_params=params,
         name="operator",
-    )(to_all(part), draws, mask, chol)
+    )(to_all(part, [ring]), draws, mask, chol)
 
     propagated = pl.pallas_call(
         update_kernel,
@@ -511,7 +516,7 @@
         out_specs=VMEM,
         compiler_params=params,
         name="update",
-    )(where, theta_blocks, to_all(operators))
+    )(where, theta_blocks, to_all(operators, [ring]))
     return propagated.reshape(theta.shape), own_bias
 
 

time: 77.7 us -> 76.3 us (0.982)
  blocking collectives: 52.3 us -> 50.9 us
    all_to_all x3, blocking collectives: 52.3 us -> 50.9 us  [to_all(): lax.all_to_all(x, 'blk', split_axis=0, concat_axis=0, tiled=True, axis_in...]
where the time goes in v6:
time: 76.3 us; the launch traced here: 76 us
  blocking collectives  50.9 us (67%)
  Pallas kernels  9.83 us (13%)
  starting transfers between devices  7.62 us (10%)
  waiting for transfers between devices  6.95 us (9%)
    all_to_all x3, blocking collectives, to_all(): lax.all_to_all(x, 'blk', split_axis=0, concat_axis=0, tiled=True, axis_in...  50.9 us
    ppermute x5, starting transfers between devices, swap(): return lax.ppermute(x, 'blk', [(i, i ^ step) for i in range(owners)])  7.62 us
    ppermute x5, waiting for transfers between devices, swap(): return lax.ppermute(x, 'blk', [(i, i ^ step) for i in range(owners)])  6.95 us
    pallas_call x1, Pallas kernels, short_axis(): pl.pallas_call(functools.partial(bias_pair_kernel, step, ring, near_ring)...  2.55 us
    pallas_call x1, Pallas kernels, short_axis(): pl.pallas_call(functools.partial(prepare_kernel, place, near_ring), out_s...  2.32 us
    pallas_call x1, Pallas kernels, short_axis(): pl.pallas_call(functools.partial(operator_pair_kernel, place), out_shape=...  1.76 us
    pallas_call x1, Pallas kernels, short_axis(): pl.pallas_call(update_kernel, out_shape=jax.ShapeDtypeStruct(theta_blocks...  1.58 us
  transfers between devices with their start and end apart: 5, of which 3 were waited for; matrix products, arithmetic and copies ran while one was open for 0% of the time, Pallas kernels for 5%

profile of v6, /device:TPU:1, one launch (start us, length us, event | category | flops | bytes accessed | tf_op | source)
XLA Modules:
  0.0 76.0 jit_solution(8246525769042047593)
XLA Ops:
  0.6 0.0 slice-start
  0.6 0.1 collective-permute-start.1
  0.8 4.8 %collective-permute-start = (bf16[1,8,128,128]{3,2,1,0:T(8,128)(2,1)}, bf16[1,8,128,128]{3,2,1,0:T(8,128)(2,1)S(1)}, u32[]{:S(2)}, u32[]{:S(2)}) collective-permute-start(bf16[1,8,128,128]{3,2,1,0:T(8,128)(2,1)} %bitcast.5), channel_id=1, source_target_pairs={{0,12},{1,13},{2,14},{3,15},{4,8},{5,9},{6,10},{7,11},{8,4},{9,5},... | collective-permute-start | bytes 786440 | tf_op jit(solution)/shard_map/ppermute | solution.py:428
  5.5 0.0 collective-permute-done.1.other_ref
  5.6 1.0 %pick.1 = (bf16[2,2,128,128]{3,2,1,0:T(8,128)(2,1)S(1)}, bf16[2,2,128,128]{3,2,1,0:T(8,128)(2,1)S(1)}, bf16[2,2,128,128]{3,2,1,0:T(8,128)(2,1)S(1)}, bf16[2,2,128,128]{3,2,1,0:T(8,128)(2,1)S(1)}) custom-call(s32[3,32]{1,0:T(4,128)} %info_hbm.3, bf16[1,8,128,128]{3,2,1,0:T(8,128)(2,1)} %bitcast.6, ...), custom_call_target="tpu_custom_call" | custom-call | bytes 33554432 | tf_op jit(solution)/shard_map/pick/pallas_call | solution.py:440
  6.6 1.3 %collective-permute-start.2 = (bf16[2,2,128,128]{3,2,1,0:T(8,128)(2,1)S(1)}, bf16[2,2,128,128]{3,2,1,0:T(8,128)(2,1)S(1)}, u32[]{:S(2)}, u32[]{:S(2)}) collective-permute-start(bf16[2,2,128,128]{3,2,1,0:T(8,128)(2,1)S(1)} %get-tuple-element.24), channel_id=1, source_target_pairs={{0,2},{1,3},{2,0},{3,1},{4,6},{5,7},{6,4},{7,5},{8,10},{9,11},{10,... | collective-permute-start | bytes 393224 | tf_op jit(solution)/shard_map/ppermute | solution.py:428
  7.9 0.0 collective-permute-start.3
  7.9 1.4 %collective-permute-start.4 = (bf16[2,2,128,128]{3,2,1,0:T(8,128)(2,1)S(1)}, bf16[2,2,128,128]{3,2,1,0:T(8,128)(2,1)S(1)}, u32[]{:S(2)}, u32[]{:S(2)}) collective-permute-start(bf16[2,2,128,128]{3,2,1,0:T(8,128)(2,1)S(1)} %get-tuple-element.26), channel_id=1, source_target_pairs={{0,6},{1,7},{2,4},{3,5},{4,2},{5,3},{6,0},{7,1},{8,14},{9,15},{10,... | collective-permute-start | bytes 393224 | tf_op jit(solution)/shard_map/ppermute | solution.py:428
  9.3 2.3 %prepare.1 = (bf16[2,128,128]{2,1,0:T(8,128)(2,1)S(1)}, f32[2,128,128]{2,1,0:T(8,128)S(1)}, f32[8,128]{1,0:T(8,128)S(1)}, s32[24]{0:T(128)S(1)}, s32[16]{0:T(128)S(1)}) custom-call(s32[3,32]{1,0:T(4,128)} %info_hbm.3, s32[16]{0:T(128)} %count_hbm.1, s32[8]{0:T(128)} %size_hbm.1, f32[1,128]{1,0:T(1,128)} %fields_hbm.1, bf16[1024,128]{1,0:T(8,128)(2,1)} %trial_ref.1), custom_call_target="tpu_custom_call" | custom-call | tf_op jit(solution)/shard_map/prepare/pallas_call | solution.py:454
  11.6 0.7 collective-permute-done.theta_ref
  12.4 0.0 slice-start.1
  12.4 0.6 spread.1
  13.0 0.0 collective-permute-done.2.refs_1_
  13.0 2.4 %collective-permute-done.3.refs_2_ = bf16[2,2,128,128]{3,2,1,0:T(8,128)(2,1)S(1)} collective-permute-done((bf16[2,2,128,128]{3,2,1,0:T(8,128)(2,1)S(1)}, bf16[2,2,128,128]{3,2,1,0:T(8,128)(2,1)S(1)}, u32[]{:S(2)}, u32[]{:S(2)}) %collective-permute-start.3) | collective-permute-done | bytes 131104 | tf_op jit(solution)/shard_map/ppermute | solution.py:428
  15.4 3.8 %collective-permute-done.4.refs_3_ = bf16[2,2,128,128]{3,2,1,0:T(8,128)(2,1)S(1)} collective-permute-done((bf16[2,2,128,128]{3,2,1,0:T(8,128)(2,1)S(1)}, bf16[2,2,128,128]{3,2,1,0:T(8,128)(2,1)S(1)}, u32[]{:S(2)}, u32[]{:S(2)}) %collective-permute-start.4) | collective-permute-done | bytes 131104 | tf_op jit(solution)/shard_map/ppermute | solution.py:428
  19.2 11.7 %all_to_all.15.far_ref = bf16[8,2,128,128]{3,2,1,0:T(8,128)(2,1)S(1)} all-to-all(bf16[8,2,128,128]{3,2,1,0:T(8,128)(2,1)S(1)} %spread.1), channel_id=1, replica_groups={{1,0,3,2,5,4,7,6},{9,8,11,10,13,12,15,14},{17,16,19,18,21,20,23,22},{25..., dimensions={0} | all-to-all | bytes 1048576 | tf_op jit(solution)/shard_map/all_to_all | solution.py:431
  30.9 0.0 slice-done
  30.9 0.0 slice-done.1
  30.9 2.5 %bias.1 = f32[16,16,128]{2,1,0:T(8,128)S(1)} custom-call(bf16[2,128,128]{2,1,0:T(8,128)(2,1)S(1)} %get-tuple-element.19.rows_ref, f32[2,128,128]{2,1,0:T(8,128)S(1)} %get-tuple-element.20.mask_ref, f32[8,128]{1,0:T(8,128)S(1)} %get-tuple-element.21.draws_ref.fields_ref, bf16[2,128,16384]{2,1,0:T(8,128)(2,1)S(1)} %bitcast.3, ...), custom_call_target="tpu_custom_call" | custom-call | tf_op jit(solution)/shard_map/bias/pallas_call | solution.py:489
  33.4 10.7 %all_to_all.16.shift_ref = f32[16,16,128]{2,1,0:T(8,128)S(1)} all-to-all(f32[16,16,128]{2,1,0:T(8,128)S(1)} %bias.1), channel_id=1, replica_groups={{3,2,7,6,11,10,15,14,13,12,9,8,5,4,1,0},{19,18,23,22,27,26,31,30,29,28,..., dimensions={0} | all-to-all | bytes 262144 | tf_op jit(solution)/shard_map/all_to_all | solution.py:431
  44.1 1.8 %operator.1 = (bf16[16,1,2,128,128]{4,3,2,1,0:T(8,128)(2,1)S(1)}, f32[1,128]{1,0:T(1,128)}) custom-call(f32[16,16,128]{2,1,0:T(8,128)S(1)} %all_to_all.16.shift_ref, f32[8,128]{1,0:T(8,128)S(1)} %get-tuple-element.21.draws_ref.fields_ref, f32[2,128,128]{2,1,0:T(8,128)S(1)} %get-tuple-element.20.mask_ref, bf16[2,128,16384]{2,1,0:T(8,128)(2,1)S(1)} %bitcast.3), custom_call_target="tpu_custom_call" | custom-call | tf_op jit(solution)/shard_map/operator/pallas_call | solution.py:499
  45.9 28.5 %all_to_all.17.oper_ref = bf16[16,1,2,128,128]{4,3,2,1,0:T(8,128)(2,1)S(1)} all-to-all(bf16[16,1,2,128,128]{4,3,2,1,0:T(8,128)(2,1)S(1)} %get-tuple-element.32), channel_id=1, replica_groups={{3,2,7,6,11,10,15,14,13,12,9,8,5,4,1,0},{19,18,23,22,27,26,31,30,29,28,..., dimensions={0} | all-to-all | bytes 2097152 | tf_op jit(solution)/shard_map/all_to_all | solution.py:431
  74.4 0.0 copy-done
  74.4 1.6 %update.1 = bf16[1,8,128,128]{3,2,1,0:T(8,128)(2,1)} custom-call(s32[24]{0:T(128)S(1)} %get-tuple-element.18.where_ref, bf16[1,8,128,128]{3,2,1,0:T(8,128)(2,1)S(1)} %bitcast.7, bf16[16,1,2,128,128]{4,3,2,1,0:T(8,128)(2,1)S(1)} %all_to_all.17.oper_ref), custom_call_target="tpu_custom_call" | custom-call | tf_op jit(solution)/shard_map/update/pallas_call | solution.py:512
  (2 shorter events, 0.0 us)
Async XLA Ops:
  0.6 30.2 %slice-start = ((s8[8388608]{0:T(1024)(128)(4,1)}), s8[4194304]{0:T(1024)(128)(4,1)S(1)}, s32[]{:S(2)}) async-start(s8[8388608]{0:T(1024)(128)(4,1)} %bitcast.2), calls=%async_computation.3 | async-start | bytes 8388608
  0.6 4.9 %collective-permute-start.1 = (bf16[1,8,128,128]{3,2,1,0:T(8,128)(2,1)}, bf16[1,8,128,128]{3,2,1,0:T(8,128)(2,1)S(1)}, u32[]{:S(2)}, u32[]{:S(2)}) collective-permute-start(bf16[1,8,128,128]{3,2,1,0:T(8,128)(2,1)} %bitcast.4), channel_id=1, source_target_pairs={{0,1},{1,0},{2,3},{3,2},{4,5},{5,4},{6,7},{7,6},{8,9},{9,8},{10,11... | collective-permute-start | bytes 786440 | tf_op jit(solution)/shard_map/ppermute | solution.py:428
  0.8 11.6 %collective-permute-start = (bf16[1,8,128,128]{3,2,1,0:T(8,128)(2,1)}, bf16[1,8,128,128]{3,2,1,0:T(8,128)(2,1)S(1)}, u32[]{:S(2)}, u32[]{:S(2)}) collective-permute-start(bf16[1,8,128,128]{3,2,1,0:T(8,128)(2,1)} %bitcast.5), channel_id=1, source_target_pairs={{0,12},{1,13},{2,14},{3,15},{4,8},{5,9},{6,10},{7,11},{8,4},{9,5},... | collective-permute-start | bytes 786440 | tf_op jit(solution)/shard_map/ppermute | solution.py:428
  6.6 6.4 %collective-permute-start.2 = (bf16[2,2,128,128]{3,2,1,0:T(8,128)(2,1)S(1)}, bf16[2,2,128,128]{3,2,1,0:T(8,128)(2,1)S(1)}, u32[]{:S(2)}, u32[]{:S(2)}) collective-permute-start(bf16[2,2,128,128]{3,2,1,0:T(8,128)(2,1)S(1)} %get-tuple-element.24), channel_id=1, source_target_pairs={{0,2},{1,3},{2,0},{3,1},{4,6},{5,7},{6,4},{7,5},{8,10},{9,11},{10,... | collective-permute-start | bytes 393224 | tf_op jit(solution)/shard_map/ppermute | solution.py:428
  7.9 7.5 %collective-permute-start.3 = (bf16[2,2,128,128]{3,2,1,0:T(8,128)(2,1)S(1)}, bf16[2,2,128,128]{3,2,1,0:T(8,128)(2,1)S(1)}, u32[]{:S(2)}, u32[]{:S(2)}) collective-permute-start(bf16[2,2,128,128]{3,2,1,0:T(8,128)(2,1)S(1)} %get-tuple-element.25), channel_id=1, source_target_pairs={{0,4},{1,5},{2,6},{3,7},{4,0},{5,1},{6,2},{7,3},{8,12},{9,13},{10,... | collective-permute-start | bytes 393224 | tf_op jit(solution)/shard_map/ppermute | solution.py:428
  7.9 11.3 %collective-permute-start.4 = (bf16[2,2,128,128]{3,2,1,0:T(8,128)(2,1)S(1)}, bf16[2,2,128,128]{3,2,1,0:T(8,128)(2,1)S(1)}, u32[]{:S(2)}, u32[]{:S(2)}) collective-permute-start(bf16[2,2,128,128]{3,2,1,0:T(8,128)(2,1)S(1)} %get-tuple-element.26), channel_id=1, source_target_pairs={{0,6},{1,7},{2,4},{3,5},{4,2},{5,3},{6,0},{7,1},{8,14},{9,15},{10,... | collective-permute-start | bytes 393224 | tf_op jit(solution)/shard_map/ppermute | solution.py:428
  12.4 18.5 %slice-start.1 = ((s8[8388608]{0:T(1024)(128)(4,1)}), s8[4194304]{0:T(1024)(128)(4,1)S(1)}, s32[]{:S(2)}) async-start(s8[8388608]{0:T(1024)(128)(4,1)} %bitcast.2), calls=%async_computation.4 | async-start | bytes 8388608
  30.9 43.5 %copy-start = (bf16[1,1024,128]{2,1,0:T(8,128)(2,1)S(1)}, bf16[1,1024,128]{2,1,0:T(8,128)(2,1)}, u32[]{:S(2)}) copy-start(bf16[1,1024,128]{2,1,0:T(8,128)(2,1)} %param.7) | copy-start | bytes 786436

commit v7 on v6

--- a/solution.py
+++ b/solution.py
@@ -289,7 +289,7 @@
 
 
 def prepare_kernel(
-    place, near_ring, info_hbm, count_hbm, size_hbm, fields_hbm, trial_ref,
+    place, near_ring, info_hbm, count_hbm, size_hbm, fields_hbm, trial_ref, _,
     rows_ref, mask_ref, draws_ref, where_ref, cols_ref, info_ref, count_ref, size_ref, fields_ref, sems,
 ):
     slots, bs, _ = rows_ref.shape
@@ -437,7 +437,7 @@
     pair_shapes = (jax.ShapeDtypeStruct((2, slots, bs, nocc), BF16),) * near
     partner = swap(theta_blocks, step)
     load = pl.CostEstimate(flops=0, bytes_accessed=8 * chol.size, transcendentals=0)
-    pairs = pl.pallas_call(
+    pick = pl.pallas_call(
         pick_pair_kernel,
         out_shape=pair_shapes,
         in_specs=[HBM, HBM, VMEM, HBM],
@@ -450,7 +450,13 @@
         compiler_params=params,
         cost_estimate=load,
         name="pick",
-    )(hbm(tile_info), hbm(theta_blocks), swap(theta_blocks, 1), hbm(chol))
+    )
+    pairs = lax.cond(
+        lax.axis_index("blk") < owners,
+        lambda x: pick(hbm(tile_info), hbm(x), swap(x, 1), hbm(chol)),
+        lambda x: pick(hbm(tile_info), hbm(x), swap(swap(swap(x, 1), 1), 1), hbm(chol)),
+        theta_blocks,
+    )
     rows, mask, draws, where, cols = pl.pallas_call(
         functools.partial(prepare_kernel, place, near_ring),
         out_shape=(
@@ -460,7 +466,7 @@
             jax.ShapeDtypeStruct((3 * blocks,), jnp.int32),
             jax.ShapeDtypeStruct((half * slots,), jnp.int32),
         ),
-        in_specs=[HBM] * 5,
+        in_specs=[HBM] * 6,
         out_specs=(VMEM, VMEM, VMEM, SMEM, SMEM),
         scratch_shapes=[
             pltpu.SMEM(tile_info.shape, jnp.int32),
@@ -470,8 +476,9 @@
             pltpu.SemaphoreType.DMA((4 + slots,)),
         ],
         compiler_params=params,
+        cost_estimate=load,
         name="prepare",
-    )(*map(hbm, (tile_info, tile_count, block_size, fields, trial)))
+    )(*map(hbm, (tile_info, tile_count, block_size, fields, trial, chol)))
     received = spread(pairs)
     far = pl.pallas_call(
         spread_far_kernel,

time: 76.3 us -> 75.6 us (level)
  waiting for transfers between devices: 6.95 us -> 5.68 us
    ppermute x5, waiting for transfers between devices: 6.95 us -> 5.68 us  [swap(): return lax.ppermute(x, 'blk', [(i, i ^ step) for i in range(owners)])]
where the time goes in v7:
time: 75.6 us; the launch traced here: 75.3 us
  blocking collectives  51.3 us (68%)
  Pallas kernels  9.77 us (13%)
  starting transfers between devices  7.88 us (10%)
  waiting for transfers between devices  5.68 us (8%)
    all_to_all x3, blocking collectives, to_all(): lax.all_to_all(x, 'blk', split_axis=0, concat_axis=0, tiled=True, axis_in...  51.3 us
    ppermute x5, starting transfers between devices, swap(): return lax.ppermute(x, 'blk', [(i, i ^ step) for i in range(owners)])  7.88 us
    ppermute x5, waiting for transfers between devices, swap(): return lax.ppermute(x, 'blk', [(i, i ^ step) for i in range(owners)])  5.68 us
    pallas_call x1, Pallas kernels, short_axis(): pl.pallas_call(functools.partial(bias_pair_kernel, step, ring, near_ring)...  2.57 us
    pallas_call x1, Pallas kernels, short_axis(): pl.pallas_call(functools.partial(prepare_kernel, place, near_ring), out_s...  2.26 us
    pallas_call x1, Pallas kernels, short_axis(): pl.pallas_call(functools.partial(operator_pair_kernel, place), out_shape=...  1.77 us
    pallas_call x1, Pallas kernels, short_axis(): pl.pallas_call(update_kernel, out_shape=jax.ShapeDtypeStruct(theta_blocks...  1.58 us
  transfers between devices with their start and end apart: 5, of which 3 were waited for; matrix products, arithmetic and copies ran while one was open for 0% of the time, Pallas kernels for 5%

profile of v7, /device:TPU:1, one launch (start us, length us, event | category | flops | bytes accessed | tf_op | source)
XLA Modules:
  0.0 75.3 jit_solution(6249200746003182749)
XLA Ops:
  0.6 4.2 %collective-permute-start.4 = (bf16[1,8,128,128]{3,2,1,0:T(8,128)(2,1)}, bf16[1,8,128,128]{3,2,1,0:T(8,128)(2,1)S(1)}, u32[]{:S(2)}, u32[]{:S(2)}) collective-permute-start(bf16[1,8,128,128]{3,2,1,0:T(8,128)(2,1)} %bitcast.4), channel_id=1, source_target_pairs={{0,12},{1,13},{2,14},{3,15},{4,8},{5,9},{6,10},{7,11},{8,4},{9,5},... | collective-permute-start | bytes 786440 | tf_op jit(solution)/shard_map/ppermute | solution.py:428
  4.8 3.3 %conditional.1 = ((bf16[2,2,128,128]{3,2,1,0:T(8,128)(2,1)S(1)}, bf16[2,2,128,128]{3,2,1,0:T(8,128)(2,1)S(1)}, bf16[2,2,128,128]{3,2,1,0:T(8,128)(2,1)S(1)}, bf16[2,2,128,128]{3,2,1,0:T(8,128)(2,1)S(1)})) conditional(s32[]{:T(128)} %convert_element_type.3, (bf16[1,8,128,128]{3,2,1,0:T(8,128)(2,1)}, s32[3,32]{1,0:T(4,128)}, ...), branch_computations={%region_0.0_spmd, %region_1.0_spmd} | conditional | bytes 36700288 | solution.py:454
  4.8 1.0 %collective-permute-start.3 = (bf16[1,8,128,128]{3,2,1,0:T(8,128)(2,1)}, bf16[1,8,128,128]{3,2,1,0:T(8,128)(2,1)S(1)}, u32[]{:S(2)}, u32[]{:S(2)}) collective-permute-start(bf16[1,8,128,128]{3,2,1,0:T(8,128)(2,1)} %get-tuple-element.16.theta_hbm), channel_id=1, source_target_pairs={{0,1},{1,0},{2,3},{3,2},{4,5},{5,4},{6,7},{7,6},{8,9},{9,8},{10,11... | collective-permute-start | bytes 786440 | tf_op jit(solution)/shard_map/cond/branch_1_fun/ppermute | solution.py:428
  5.8 1.4 %collective-permute-done.3.other_ref = bf16[1,8,128,128]{3,2,1,0:T(8,128)(2,1)S(1)} collective-permute-done((bf16[1,8,128,128]{3,2,1,0:T(8,128)(2,1)}, bf16[1,8,128,128]{3,2,1,0:T(8,128)(2,1)S(1)}, u32[]{:S(2)}, u32[]{:S(2)}) %collective-permute-start.3) | collective-permute-done | bytes 262176 | tf_op jit(solution)/shard_map/cond/branch_1_fun/ppermute | solution.py:428
  7.2 1.0 %pick.3 = (bf16[2,2,128,128]{3,2,1,0:T(8,128)(2,1)S(1)}, bf16[2,2,128,128]{3,2,1,0:T(8,128)(2,1)S(1)}, bf16[2,2,128,128]{3,2,1,0:T(8,128)(2,1)S(1)}, bf16[2,2,128,128]{3,2,1,0:T(8,128)(2,1)S(1)}) custom-call(s32[3,32]{1,0:T(4,128)} %get-tuple-element.15.info_hbm, bf16[1,8,128,128]{3,2,1,0:T(8,128)(2,1)} %get-tuple-element.16.theta_hbm, ...), custom_call_target="tpu_custom_call" | custom-call | bytes 33554432 | tf_op jit(solution)/shard_map/cond/branch_1_fun/pick/pallas_call | solution.py:456
  8.2 1.3 %collective-permute-start.5 = (bf16[2,2,128,128]{3,2,1,0:T(8,128)(2,1)S(1)}, bf16[2,2,128,128]{3,2,1,0:T(8,128)(2,1)S(1)}, u32[]{:S(2)}, u32[]{:S(2)}) collective-permute-start(bf16[2,2,128,128]{3,2,1,0:T(8,128)(2,1)S(1)} %get-tuple-element.42), channel_id=1, source_target_pairs={{0,2},{1,3},{2,0},{3,1},{4,6},{5,7},{6,4},{7,5},{8,10},{9,11},{10,... | collective-permute-start | bytes 393224 | tf_op jit(solution)/shard_map/ppermute | solution.py:428
  9.5 0.0 collective-permute-start.6
  9.5 1.4 %collective-permute-start.7 = (bf16[2,2,128,128]{3,2,1,0:T(8,128)(2,1)S(1)}, bf16[2,2,128,128]{3,2,1,0:T(8,128)(2,1)S(1)}, u32[]{:S(2)}, u32[]{:S(2)}) collective-permute-start(bf16[2,2,128,128]{3,2,1,0:T(8,128)(2,1)S(1)} %get-tuple-element.44), channel_id=1, source_target_pairs={{0,6},{1,7},{2,4},{3,5},{4,2},{5,3},{6,0},{7,1},{8,14},{9,15},{10,... | collective-permute-start | bytes 393224 | tf_op jit(solution)/shard_map/ppermute | solution.py:428
  10.9 2.3 %prepare.1 = (bf16[2,128,128]{2,1,0:T(8,128)(2,1)S(1)}, f32[2,128,128]{2,1,0:T(8,128)S(1)}, f32[8,128]{1,0:T(8,128)S(1)}, s32[24]{0:T(128)S(1)}, s32[16]{0:T(128)S(1)}) custom-call(s32[3,32]{1,0:T(4,128)} %info_hbm.1, s32[16]{0:T(128)} %count_hbm.1, s32[8]{0:T(128)} %size_hbm.1, f32[1,128]{1,0:T(1,128)} %fields_hbm.1, bf16[1024,128]{1,0:T(8,128)(2,1)} %trial_ref.1, ...), custom_call_target="tpu_custom_call" | custom-call | bytes 33554432 | tf_op jit(solution)/shard_map/prepare/pallas_call | solution.py:460
  13.2 0.0 collective-permute-done.4.theta_ref
  13.2 0.0 slice-start.1
  13.2 0.6 spread.1
  13.8 0.0 collective-permute-done.5.refs_1_
  13.8 0.7 collective-permute-done.6.refs_2_
  14.5 3.6 %collective-permute-done.7.refs_3_ = bf16[2,2,128,128]{3,2,1,0:T(8,128)(2,1)S(1)} collective-permute-done((bf16[2,2,128,128]{3,2,1,0:T(8,128)(2,1)S(1)}, bf16[2,2,128,128]{3,2,1,0:T(8,128)(2,1)S(1)}, u32[]{:S(2)}, u32[]{:S(2)}) %collective-permute-start.7) | collective-permute-done | bytes 131104 | tf_op jit(solution)/shard_map/ppermute | solution.py:428
  18.1 12.1 %all_to_all.15.far_ref = bf16[8,2,128,128]{3,2,1,0:T(8,128)(2,1)S(1)} all-to-all(bf16[8,2,128,128]{3,2,1,0:T(8,128)(2,1)S(1)} %spread.1), channel_id=1, replica_groups={{1,0,3,2,5,4,7,6},{9,8,11,10,13,12,15,14},{17,16,19,18,21,20,23,22},{25..., dimensions={0} | all-to-all | bytes 1048576 | tf_op jit(solution)/shard_map/all_to_all | solution.py:431
  30.2 0.0 slice-done
  30.2 0.0 slice-done.1
  30.2 2.6 %bias.1 = f32[16,16,128]{2,1,0:T(8,128)S(1)} custom-call(bf16[2,128,128]{2,1,0:T(8,128)(2,1)S(1)} %get-tuple-element.37.rows_ref, f32[2,128,128]{2,1,0:T(8,128)S(1)} %get-tuple-element.38.mask_ref, f32[8,128]{1,0:T(8,128)S(1)} %get-tuple-element.39.draws_ref.fields_ref, bf16[2,128,16384]{2,1,0:T(8,128)(2,1)S(1)} %bitcast.3, ...), custom_call_target="tpu_custom_call" | custom-call | tf_op jit(solution)/shard_map/bias/pallas_call | solution.py:496
  32.8 10.7 %all_to_all.16.shift_ref = f32[16,16,128]{2,1,0:T(8,128)S(1)} all-to-all(f32[16,16,128]{2,1,0:T(8,128)S(1)} %bias.1), channel_id=1, replica_groups={{3,2,7,6,11,10,15,14,13,12,9,8,5,4,1,0},{19,18,23,22,27,26,31,30,29,28,..., dimensions={0} | all-to-all | bytes 262144 | tf_op jit(solution)/shard_map/all_to_all | solution.py:431
  43.4 1.8 %operator.1 = (bf16[16,1,2,128,128]{4,3,2,1,0:T(8,128)(2,1)S(1)}, f32[1,128]{1,0:T(1,128)}) custom-call(f32[16,16,128]{2,1,0:T(8,128)S(1)} %all_to_all.16.shift_ref, f32[8,128]{1,0:T(8,128)S(1)} %get-tuple-element.39.draws_ref.fields_ref, f32[2,128,128]{2,1,0:T(8,128)S(1)} %get-tuple-element.38.mask_ref, bf16[2,128,16384]{2,1,0:T(8,128)(2,1)S(1)} %bitcast.3), custom_call_target="tpu_custom_call" | custom-call | tf_op jit(solution)/shard_map/operator/pallas_call | solution.py:506
  45.2 28.5 %all_to_all.17.oper_ref = bf16[16,1,2,128,128]{4,3,2,1,0:T(8,128)(2,1)S(1)} all-to-all(bf16[16,1,2,128,128]{4,3,2,1,0:T(8,128)(2,1)S(1)} %get-tuple-element.50), channel_id=1, replica_groups={{3,2,7,6,11,10,15,14,13,12,9,8,5,4,1,0},{19,18,23,22,27,26,31,30,29,28,..., dimensions={0} | all-to-all | bytes 2097152 | tf_op jit(solution)/shard_map/all_to_all | solution.py:431
  73.7 0.0 copy-done
  73.7 1.6 %update.1 = bf16[1,8,128,128]{3,2,1,0:T(8,128)(2,1)} custom-call(s32[24]{0:T(128)S(1)} %get-tuple-element.36.where_ref, bf16[1,8,128,128]{3,2,1,0:T(8,128)(2,1)S(1)} %bitcast.7, bf16[16,1,2,128,128]{4,3,2,1,0:T(8,128)(2,1)S(1)} %all_to_all.17.oper_ref), custom_call_target="tpu_custom_call" | custom-call | tf_op jit(solution)/shard_map/update/pallas_call | solution.py:519
  (3 shorter events, 0.0 us)
Async XLA Ops:
  0.6 12.5 %collective-permute-start.4 = (bf16[1,8,128,128]{3,2,1,0:T(8,128)(2,1)}, bf16[1,8,128,128]{3,2,1,0:T(8,128)(2,1)S(1)}, u32[]{:S(2)}, u32[]{:S(2)}) collective-permute-start(bf16[1,8,128,128]{3,2,1,0:T(8,128)(2,1)} %bitcast.4), channel_id=1, source_target_pairs={{0,12},{1,13},{2,14},{3,15},{4,8},{5,9},{6,10},{7,11},{8,4},{9,5},... | collective-permute-start | bytes 786440 | tf_op jit(solution)/shard_map/ppermute | solution.py:428
  4.8 2.3 %collective-permute-start.3 = (bf16[1,8,128,128]{3,2,1,0:T(8,128)(2,1)}, bf16[1,8,128,128]{3,2,1,0:T(8,128)(2,1)S(1)}, u32[]{:S(2)}, u32[]{:S(2)}) collective-permute-start(bf16[1,8,128,128]{3,2,1,0:T(8,128)(2,1)} %get-tuple-element.16.theta_hbm), channel_id=1, source_target_pairs={{0,1},{1,0},{2,3},{3,2},{4,5},{5,4},{6,7},{7,6},{8,9},{9,8},{10,11... | collective-permute-start | bytes 786440 | tf_op jit(solution)/shard_map/cond/branch_1_fun/ppermute | solution.py:428
  8.2 5.6 %collective-permute-start.5 = (bf16[2,2,128,128]{3,2,1,0:T(8,128)(2,1)S(1)}, bf16[2,2,128,128]{3,2,1,0:T(8,128)(2,1)S(1)}, u32[]{:S(2)}, u32[]{:S(2)}) collective-permute-start(bf16[2,2,128,128]{3,2,1,0:T(8,128)(2,1)S(1)} %get-tuple-element.42), channel_id=1, source_target_pairs={{0,2},{1,3},{2,0},{3,1},{4,6},{5,7},{6,4},{7,5},{8,10},{9,11},{10,... | collective-permute-start | bytes 393224 | tf_op jit(solution)/shard_map/ppermute | solution.py:428
  9.5 5.0 %collective-permute-start.6 = (bf16[2,2,128,128]{3,2,1,0:T(8,128)(2,1)S(1)}, bf16[2,2,128,128]{3,2,1,0:T(8,128)(2,1)S(1)}, u32[]{:S(2)}, u32[]{:S(2)}) collective-permute-start(bf16[2,2,128,128]{3,2,1,0:T(8,128)(2,1)S(1)} %get-tuple-element.43), channel_id=1, source_target_pairs={{0,4},{1,5},{2,6},{3,7},{4,0},{5,1},{6,2},{7,3},{8,12},{9,13},{10,... | collective-permute-start | bytes 393224 | tf_op jit(solution)/shard_map/ppermute | solution.py:428
  9.5 20.7 %slice-start = ((s8[8388608]{0:T(1024)(128)(4,1)}), s8[4194304]{0:T(1024)(128)(4,1)S(1)}, s32[]{:S(2)}) async-start(s8[8388608]{0:T(1024)(128)(4,1)} %bitcast.2), calls=%async_computation.3 | async-start | bytes 8388608
  9.5 8.6 %collective-permute-start.7 = (bf16[2,2,128,128]{3,2,1,0:T(8,128)(2,1)S(1)}, bf16[2,2,128,128]{3,2,1,0:T(8,128)(2,1)S(1)}, u32[]{:S(2)}, u32[]{:S(2)}) collective-permute-start(bf16[2,2,128,128]{3,2,1,0:T(8,128)(2,1)S(1)} %get-tuple-element.44), channel_id=1, source_target_pairs={{0,6},{1,7},{2,4},{3,5},{4,2},{5,3},{6,0},{7,1},{8,14},{9,15},{10,... | collective-permute-start | bytes 393224 | tf_op jit(solution)/shard_map/ppermute | solution.py:428
  13.2 17.0 %slice-start.1 = ((s8[8388608]{0:T(1024)(128)(4,1)}), s8[4194304]{0:T(1024)(128)(4,1)S(1)}, s32[]{:S(2)}) async-start(s8[8388608]{0:T(1024)(128)(4,1)} %bitcast.2), calls=%async_computation.4 | async-start | bytes 8388608
  30.2 43.5 %copy-start = (bf16[1,1024,128]{2,1,0:T(8,128)(2,1)S(1)}, bf16[1,1024,128]{2,1,0:T(8,128)(2,1)}, u32[]{:S(2)}) copy-start(bf16[1,1024,128]{2,1,0:T(8,128)(2,1)} %param.9) | copy-start | bytes 786436

commit v8 on v7

--- a/solution.py
+++ b/solution.py
@@ -392,7 +392,7 @@
     me = lax.axis_index("blk")
     total_ref[...] = sum(shift_ref[o] for o in range(walkers))
     own = total_ref[pl.ds(me, 1), :]
-    own_ref[...] = -own
+    own_ref[...] = jnp.broadcast_to(-own, own_ref.shape)
     total_ref[pl.ds(me, 1), :] = own + fields_ref[0:1, :]
     left = total_ref[...].astype(BF16)
     per = bs // PIECES
@@ -406,6 +406,11 @@
         for w in range(walkers):
             block = oper_ref[slot, pl.ds(w * pitch, bs), :]
             out_ref[place[w], 0, slot] = (block * mask_ref[slot]).astype(BF16)
+
+
+def update_pair_kernel(where_ref, theta_ref, oper_ref, bias_ref, out_ref, own_ref):
+    own_ref[...] = bias_ref[0:1, :]
+    update_kernel(where_ref, theta_ref, oper_ref, out_ref)
 
 
 def short_axis(theta, trial, chol, fields, tile_info, tile_count, block_size):
@@ -507,7 +512,7 @@
         functools.partial(operator_pair_kernel, place),
         out_shape=(
             jax.ShapeDtypeStruct((owners, 1, slots, bs, bs), BF16),
-            jax.ShapeDtypeStruct((1, gs), F32),
+            jax.ShapeDtypeStruct((8, gs), F32),
         ),
         in_specs=[VMEM] * 4,
         out_specs=(VMEM, VMEM),
@@ -516,14 +521,14 @@
         name="operator",
     )(to_all(part, [ring]), draws, mask, chol)
 
-    propagated = pl.pallas_call(
-        update_kernel,
-        out_shape=jax.ShapeDtypeStruct(theta_blocks.shape, BF16),
-        in_specs=[SMEM, VMEM, VMEM],
-        out_specs=VMEM,
+    propagated, own_bias = pl.pallas_call(
+        update_pair_kernel,
+        out_shape=(jax.ShapeDtypeStruct(theta_blocks.shape, BF16), jax.ShapeDtypeStruct((1, gs), F32)),
+        in_specs=[SMEM, VMEM, VMEM, VMEM],
+        out_specs=(VMEM, VMEM),
         compiler_params=params,
         name="update",
-    )(where, theta_blocks, to_all(operators, [ring]))
+    )(where, theta_blocks, to_all(operators, [ring]), own_bias)
     return propagated.reshape(theta.shape), own_bias
 
 

time: 75.6 us -> 75.2 us (level)
  no operation moved by 1% of the time
where the time goes in v8:
time: 75.2 us; the launch traced here: 74.9 us
  blocking collectives  51.3 us (68%)
  Pallas kernels  9.38 us (12%)
  starting transfers between devices  7.88 us (10%)
  waiting for transfers between devices  5.62 us (7%)
    all_to_all x3, blocking collectives, to_all(): lax.all_to_all(x, 'blk', split_axis=0, concat_axis=0, tiled=True, axis_in...  51.3 us
    ppermute x5, starting transfers between devices, swap(): return lax.ppermute(x, 'blk', [(i, i ^ step) for i in range(owners)])  7.88 us
    ppermute x5, waiting for transfers between devices, swap(): return lax.ppermute(x, 'blk', [(i, i ^ step) for i in range(owners)])  5.62 us
    pallas_call x1, Pallas kernels, short_axis(): pl.pallas_call(functools.partial(bias_pair_kernel, step, ring, near_ring)...  2.57 us
    pallas_call x1, Pallas kernels, short_axis(): pl.pallas_call(functools.partial(prepare_kernel, place, near_ring), out_s...  2.32 us
    pallas_call x1, Pallas kernels, short_axis(): pl.pallas_call(update_pair_kernel, out_shape=(jax.ShapeDtypeStruct(theta_...  1.59 us
  transfers between devices with their start and end apart: 5, of which 3 were waited for; matrix products, arithmetic and copies ran while one was open for 0% of the time, Pallas kernels for 5%

profile of v8, /device:TPU:1, one launch (start us, length us, event | category | flops | bytes accessed | tf_op | source)
XLA Modules:
  0.0 74.9 jit_solution(2761679722584240671)
XLA Ops:
  0.6 4.2 %collective-permute-start.4 = (bf16[1,8,128,128]{3,2,1,0:T(8,128)(2,1)}, bf16[1,8,128,128]{3,2,1,0:T(8,128)(2,1)S(1)}, u32[]{:S(2)}, u32[]{:S(2)}) collective-permute-start(bf16[1,8,128,128]{3,2,1,0:T(8,128)(2,1)} %bitcast.4), channel_id=1, source_target_pairs={{0,12},{1,13},{2,14},{3,15},{4,8},{5,9},{6,10},{7,11},{8,4},{9,5},... | collective-permute-start | bytes 786440 | tf_op jit(solution)/shard_map/ppermute | solution.py:433
  4.8 3.3 %conditional.1 = ((bf16[2,2,128,128]{3,2,1,0:T(8,128)(2,1)S(1)}, bf16[2,2,128,128]{3,2,1,0:T(8,128)(2,1)S(1)}, bf16[2,2,128,128]{3,2,1,0:T(8,128)(2,1)S(1)}, bf16[2,2,128,128]{3,2,1,0:T(8,128)(2,1)S(1)})) conditional(s32[]{:T(128)} %convert_element_type.3, (bf16[1,8,128,128]{3,2,1,0:T(8,128)(2,1)}, s32[3,32]{1,0:T(4,128)}, ...), branch_computations={%region_0.0_spmd, %region_1.0_spmd} | conditional | bytes 36700288 | solution.py:459
  4.8 1.0 %collective-permute-start.3 = (bf16[1,8,128,128]{3,2,1,0:T(8,128)(2,1)}, bf16[1,8,128,128]{3,2,1,0:T(8,128)(2,1)S(1)}, u32[]{:S(2)}, u32[]{:S(2)}) collective-permute-start(bf16[1,8,128,128]{3,2,1,0:T(8,128)(2,1)} %get-tuple-element.16.theta_hbm), channel_id=1, source_target_pairs={{0,1},{1,0},{2,3},{3,2},{4,5},{5,4},{6,7},{7,6},{8,9},{9,8},{10,11... | collective-permute-start | bytes 786440 | tf_op jit(solution)/shard_map/cond/branch_1_fun/ppermute | solution.py:433
  5.8 1.4 %collective-permute-done.3.other_ref = bf16[1,8,128,128]{3,2,1,0:T(8,128)(2,1)S(1)} collective-permute-done((bf16[1,8,128,128]{3,2,1,0:T(8,128)(2,1)}, bf16[1,8,128,128]{3,2,1,0:T(8,128)(2,1)S(1)}, u32[]{:S(2)}, u32[]{:S(2)}) %collective-permute-start.3) | collective-permute-done | bytes 262176 | tf_op jit(solution)/shard_map/cond/branch_1_fun/ppermute | solution.py:433
  7.2 1.0 %pick.3 = (bf16[2,2,128,128]{3,2,1,0:T(8,128)(2,1)S(1)}, bf16[2,2,128,128]{3,2,1,0:T(8,128)(2,1)S(1)}, bf16[2,2,128,128]{3,2,1,0:T(8,128)(2,1)S(1)}, bf16[2,2,128,128]{3,2,1,0:T(8,128)(2,1)S(1)}) custom-call(s32[3,32]{1,0:T(4,128)} %get-tuple-element.15.info_hbm, bf16[1,8,128,128]{3,2,1,0:T(8,128)(2,1)} %get-tuple-element.16.theta_hbm, ...), custom_call_target="tpu_custom_call" | custom-call | bytes 33554432 | tf_op jit(solution)/shard_map/cond/branch_1_fun/pick/pallas_call | solution.py:461
  8.2 1.3 %collective-permute-start.5 = (bf16[2,2,128,128]{3,2,1,0:T(8,128)(2,1)S(1)}, bf16[2,2,128,128]{3,2,1,0:T(8,128)(2,1)S(1)}, u32[]{:S(2)}, u32[]{:S(2)}) collective-permute-start(bf16[2,2,128,128]{3,2,1,0:T(8,128)(2,1)S(1)} %get-tuple-element.44), channel_id=1, source_target_pairs={{0,2},{1,3},{2,0},{3,1},{4,6},{5,7},{6,4},{7,5},{8,10},{9,11},{10,... | collective-permute-start | bytes 393224 | tf_op jit(solution)/shard_map/ppermute | solution.py:433
  9.5 0.0 collective-permute-start.6
  9.5 1.4 %collective-permute-start.7 = (bf16[2,2,128,128]{3,2,1,0:T(8,128)(2,1)S(1)}, bf16[2,2,128,128]{3,2,1,0:T(8,128)(2,1)S(1)}, u32[]{:S(2)}, u32[]{:S(2)}) collective-permute-start(bf16[2,2,128,128]{3,2,1,0:T(8,128)(2,1)S(1)} %get-tuple-element.46), channel_id=1, source_target_pairs={{0,6},{1,7},{2,4},{3,5},{4,2},{5,3},{6,0},{7,1},{8,14},{9,15},{10,... | collective-permute-start | bytes 393224 | tf_op jit(solution)/shard_map/ppermute | solution.py:433
  10.9 2.3 %prepare.1 = (bf16[2,128,128]{2,1,0:T(8,128)(2,1)S(1)}, f32[2,128,128]{2,1,0:T(8,128)S(1)}, f32[8,128]{1,0:T(8,128)S(1)}, s32[24]{0:T(128)S(1)}, s32[16]{0:T(128)S(1)}) custom-call(s32[3,32]{1,0:T(4,128)} %info_hbm.1, s32[16]{0:T(128)} %count_hbm.1, s32[8]{0:T(128)} %size_hbm.1, f32[1,128]{1,0:T(1,128)} %fields_hbm.1, bf16[1024,128]{1,0:T(8,128)(2,1)} %trial_ref.1, ...), custom_call_target="tpu_custom_call" | custom-call | bytes 33554432 | tf_op jit(solution)/shard_map/prepare/pallas_call | solution.py:465
  13.2 0.0 collective-permute-done.4.theta_ref
  13.2 0.0 slice-start.1
  13.3 0.6 spread.1
  13.8 0.0 collective-permute-done.5.refs_1_
  13.9 0.6 collective-permute-done.6.refs_2_
  14.5 3.6 %collective-permute-done.7.refs_3_ = bf16[2,2,128,128]{3,2,1,0:T(8,128)(2,1)S(1)} collective-permute-done((bf16[2,2,128,128]{3,2,1,0:T(8,128)(2,1)S(1)}, bf16[2,2,128,128]{3,2,1,0:T(8,128)(2,1)S(1)}, u32[]{:S(2)}, u32[]{:S(2)}) %collective-permute-start.7) | collective-permute-done | bytes 131104 | tf_op jit(solution)/shard_map/ppermute | solution.py:433
  18.1 12.1 %all_to_all.15.far_ref = bf16[8,2,128,128]{3,2,1,0:T(8,128)(2,1)S(1)} all-to-all(bf16[8,2,128,128]{3,2,1,0:T(8,128)(2,1)S(1)} %spread.1), channel_id=1, replica_groups={{1,0,3,2,5,4,7,6},{9,8,11,10,13,12,15,14},{17,16,19,18,21,20,23,22},{25..., dimensions={0} | all-to-all | bytes 1048576 | tf_op jit(solution)/shard_map/all_to_all | solution.py:436
  30.2 0.0 slice-done
  30.2 0.0 slice-done.1
  30.2 2.6 %bias.1 = f32[16,16,128]{2,1,0:T(8,128)S(1)} custom-call(bf16[2,128,128]{2,1,0:T(8,128)(2,1)S(1)} %get-tuple-element.39.rows_ref, f32[2,128,128]{2,1,0:T(8,128)S(1)} %get-tuple-element.40.mask_ref, f32[8,128]{1,0:T(8,128)S(1)} %get-tuple-element.41.draws_ref.fields_ref, bf16[2,128,16384]{2,1,0:T(8,128)(2,1)S(1)} %bitcast.3, ...), custom_call_target="tpu_custom_call" | custom-call | tf_op jit(solution)/shard_map/bias/pallas_call | solution.py:501
  32.8 10.7 %all_to_all.16.shift_ref = f32[16,16,128]{2,1,0:T(8,128)S(1)} all-to-all(f32[16,16,128]{2,1,0:T(8,128)S(1)} %bias.1), channel_id=1, replica_groups={{3,2,7,6,11,10,15,14,13,12,9,8,5,4,1,0},{19,18,23,22,27,26,31,30,29,28,..., dimensions={0} | all-to-all | bytes 262144 | tf_op jit(solution)/shard_map/all_to_all | solution.py:436
  43.4 1.3 %operator.1 = (bf16[16,1,2,128,128]{4,3,2,1,0:T(8,128)(2,1)S(1)}, f32[8,128]{1,0:T(8,128)S(1)}) custom-call(f32[16,16,128]{2,1,0:T(8,128)S(1)} %all_to_all.16.shift_ref, f32[8,128]{1,0:T(8,128)S(1)} %get-tuple-element.41.draws_ref.fields_ref, f32[2,128,128]{2,1,0:T(8,128)S(1)} %get-tuple-element.40.mask_ref, bf16[2,128,16384]{2,1,0:T(8,128)(2,1)S(1)} %bitcast.3), custom_call_target="tpu_custom_call" | custom-call | tf_op jit(solution)/shard_map/operator/pallas_call | solution.py:511
  44.8 28.5 %all_to_all.17.oper_ref = bf16[16,1,2,128,128]{4,3,2,1,0:T(8,128)(2,1)S(1)} all-to-all(bf16[16,1,2,128,128]{4,3,2,1,0:T(8,128)(2,1)S(1)} %get-tuple-element.52), channel_id=1, replica_groups={{3,2,7,6,11,10,15,14,13,12,9,8,5,4,1,0},{19,18,23,22,27,26,31,30,29,28,..., dimensions={0} | all-to-all | bytes 2097152 | tf_op jit(solution)/shard_map/all_to_all | solution.py:436
  73.3 0.0 copy-done
  73.3 1.6 %update.1 = (bf16[1,8,128,128]{3,2,1,0:T(8,128)(2,1)}, f32[1,128]{1,0:T(1,128)}) custom-call(s32[24]{0:T(128)S(1)} %get-tuple-element.38.where_ref, bf16[1,8,128,128]{3,2,1,0:T(8,128)(2,1)S(1)} %bitcast.7, bf16[16,1,2,128,128]{4,3,2,1,0:T(8,128)(2,1)S(1)} %all_to_all.17.oper_ref, f32[8,128]{1,0:T(8,128)S(1)} %get-tuple-element.53.bias_ref), custom_call_target="tpu_custom_call" | custom-call | tf_op jit(solution)/shard_map/update/pallas_call | solution.py:524
  (3 shorter events, 0.0 us)
Async XLA Ops:
  0.6 12.6 %collective-permute-start.4 = (bf16[1,8,128,128]{3,2,1,0:T(8,128)(2,1)}, bf16[1,8,128,128]{3,2,1,0:T(8,128)(2,1)S(1)}, u32[]{:S(2)}, u32[]{:S(2)}) collective-permute-start(bf16[1,8,128,128]{3,2,1,0:T(8,128)(2,1)} %bitcast.4), channel_id=1, source_target_pairs={{0,12},{1,13},{2,14},{3,15},{4,8},{5,9},{6,10},{7,11},{8,4},{9,5},... | collective-permute-start | bytes 786440 | tf_op jit(solution)/shard_map/ppermute | solution.py:433
  4.8 2.3 %collective-permute-start.3 = (bf16[1,8,128,128]{3,2,1,0:T(8,128)(2,1)}, bf16[1,8,128,128]{3,2,1,0:T(8,128)(2,1)S(1)}, u32[]{:S(2)}, u32[]{:S(2)}) collective-permute-start(bf16[1,8,128,128]{3,2,1,0:T(8,128)(2,1)} %get-tuple-element.16.theta_hbm), channel_id=1, source_target_pairs={{0,1},{1,0},{2,3},{3,2},{4,5},{5,4},{6,7},{7,6},{8,9},{9,8},{10,11... | collective-permute-start | bytes 786440 | tf_op jit(solution)/shard_map/cond/branch_1_fun/ppermute | solution.py:433
  8.2 5.7 %collective-permute-start.5 = (bf16[2,2,128,128]{3,2,1,0:T(8,128)(2,1)S(1)}, bf16[2,2,128,128]{3,2,1,0:T(8,128)(2,1)S(1)}, u32[]{:S(2)}, u32[]{:S(2)}) collective-permute-start(bf16[2,2,128,128]{3,2,1,0:T(8,128)(2,1)S(1)} %get-tuple-element.44), channel_id=1, source_target_pairs={{0,2},{1,3},{2,0},{3,1},{4,6},{5,7},{6,4},{7,5},{8,10},{9,11},{10,... | collective-permute-start | bytes 393224 | tf_op jit(solution)/shard_map/ppermute | solution.py:433
  9.5 5.0 %collective-permute-start.6 = (bf16[2,2,128,128]{3,2,1,0:T(8,128)(2,1)S(1)}, bf16[2,2,128,128]{3,2,1,0:T(8,128)(2,1)S(1)}, u32[]{:S(2)}, u32[]{:S(2)}) collective-permute-start(bf16[2,2,128,128]{3,2,1,0:T(8,128)(2,1)S(1)} %get-tuple-element.45), channel_id=1, source_target_pairs={{0,4},{1,5},{2,6},{3,7},{4,0},{5,1},{6,2},{7,3},{8,12},{9,13},{10,... | collective-permute-start | bytes 393224 | tf_op jit(solution)/shard_map/ppermute | solution.py:433
  9.5 20.7 %slice-start = ((s8[8388608]{0:T(1024)(128)(4,1)}), s8[4194304]{0:T(1024)(128)(4,1)S(1)}, s32[]{:S(2)}) async-start(s8[8388608]{0:T(1024)(128)(4,1)} %bitcast.2), calls=%async_computation.3 | async-start | bytes 8388608
  9.5 8.6 %collective-permute-start.7 = (bf16[2,2,128,128]{3,2,1,0:T(8,128)(2,1)S(1)}, bf16[2,2,128,128]{3,2,1,0:T(8,128)(2,1)S(1)}, u32[]{:S(2)}, u32[]{:S(2)}) collective-permute-start(bf16[2,2,128,128]{3,2,1,0:T(8,128)(2,1)S(1)} %get-tuple-element.46), channel_id=1, source_target_pairs={{0,6},{1,7},{2,4},{3,5},{4,2},{5,3},{6,0},{7,1},{8,14},{9,15},{10,... | collective-permute-start | bytes 393224 | tf_op jit(solution)/shard_map/ppermute | solution.py:433
  13.2 16.9 %slice-start.1 = ((s8[8388608]{0:T(1024)(128)(4,1)}), s8[4194304]{0:T(1024)(128)(4,1)S(1)}, s32[]{:S(2)}) async-start(s8[8388608]{0:T(1024)(128)(4,1)} %bitcast.2), calls=%async_computation.4 | async-start | bytes 8388608
  30.2 43.1 %copy-start = (bf16[1,1024,128]{2,1,0:T(8,128)(2,1)S(1)}, bf16[1,1024,128]{2,1,0:T(8,128)(2,1)}, u32[]{:S(2)}) copy-start(bf16[1,1024,128]{2,1,0:T(8,128)(2,1)} %param.9) | copy-start | bytes 786436

commit v9 on v8

--- a/solution.py
+++ b/solution.py
@@ -424,7 +424,8 @@
     near = half // 2
     chips = [*range(1, half, 2), *range(0, half, 2)[::-1]]
     ring = [2 * chip + core for chip in chips for core in (1, 0)]
-    place = [ring.index(o) for o in range(owners)]
+    back = [o for n in range(half) for o in (2 * chips[n] + 1, 2 * chips[(n + near) % half])]
+    place = [back.index(o) for o in range(owners)]
     near_ring = [2 * chip + core for chip in range(near) for core in (1, 0)]
     params = pltpu.CompilerParams(vmem_limit_bytes=LIMIT)
     theta_blocks = theta.reshape(1, blocks, bs, nocc)
@@ -528,7 +529,7 @@
         out_specs=(VMEM, VMEM),
         compiler_params=params,
         name="update",
-    )(where, theta_blocks, to_all(operators, [ring]), own_bias)
+    )(where, theta_blocks, to_all(operators, [back]), own_bias)
     return propagated.reshape(theta.shape), own_bias
 
 

time: 75.2 us -> 74.9 us (level)
  no operation moved by 1% of the time
where the time goes in v9:
time: 74.9 us; the launch traced here: 74.2 us
  blocking collectives  50.6 us (68%)
  Pallas kernels  9.33 us (12%)
  starting transfers between devices  7.88 us (11%)
  waiting for transfers between devices  5.68 us (8%)
    all_to_all x3, blocking collectives, to_all(): lax.all_to_all(x, 'blk', split_axis=0, concat_axis=0, tiled=True, axis_in...  50.6 us
    ppermute x5, starting transfers between devices, swap(): return lax.ppermute(x, 'blk', [(i, i ^ step) for i in range(owners)])  7.88 us
    ppermute x5, waiting for transfers between devices, swap(): return lax.ppermute(x, 'blk', [(i, i ^ step) for i in range(owners)])  5.68 us
    pallas_call x1, Pallas kernels, short_axis(): pl.pallas_call(functools.partial(bias_pair_kernel, step, ring, near_ring)...  2.57 us
    pallas_call x1, Pallas kernels, short_axis(): pl.pallas_call(functools.partial(prepare_kernel, place, near_ring), out_s...  2.26 us
    pallas_call x1, Pallas kernels, short_axis(): pl.pallas_call(update_pair_kernel, out_shape=(jax.ShapeDtypeStruct(theta_...  1.59 us
  transfers between devices with their start and end apart: 5, of which 3 were waited for; matrix products, arithmetic and copies ran while one was open for 0% of the time, Pallas kernels for 5%

profile of v9, /device:TPU:1, one launch (start us, length us, event | category | flops | bytes accessed | tf_op | source)
XLA Modules:
  0.0 74.2 jit_solution(17186039551783519932)
XLA Ops:
  0.6 4.2 %collective-permute-start.4 = (bf16[1,8,128,128]{3,2,1,0:T(8,128)(2,1)}, bf16[1,8,128,128]{3,2,1,0:T(8,128)(2,1)S(1)}, u32[]{:S(2)}, u32[]{:S(2)}) collective-permute-start(bf16[1,8,128,128]{3,2,1,0:T(8,128)(2,1)} %bitcast.4), channel_id=1, source_target_pairs={{0,12},{1,13},{2,14},{3,15},{4,8},{5,9},{6,10},{7,11},{8,4},{9,5},... | collective-permute-start | bytes 786440 | tf_op jit(solution)/shard_map/ppermute | solution.py:434
  4.8 3.3 %conditional.1 = ((bf16[2,2,128,128]{3,2,1,0:T(8,128)(2,1)S(1)}, bf16[2,2,128,128]{3,2,1,0:T(8,128)(2,1)S(1)}, bf16[2,2,128,128]{3,2,1,0:T(8,128)(2,1)S(1)}, bf16[2,2,128,128]{3,2,1,0:T(8,128)(2,1)S(1)})) conditional(s32[]{:T(128)} %convert_element_type.3, (bf16[1,8,128,128]{3,2,1,0:T(8,128)(2,1)}, s32[3,32]{1,0:T(4,128)}, ...), branch_computations={%region_0.0_spmd, %region_1.0_spmd} | conditional | bytes 36700288 | solution.py:460
  4.8 1.0 %collective-permute-start.3 = (bf16[1,8,128,128]{3,2,1,0:T(8,128)(2,1)}, bf16[1,8,128,128]{3,2,1,0:T(8,128)(2,1)S(1)}, u32[]{:S(2)}, u32[]{:S(2)}) collective-permute-start(bf16[1,8,128,128]{3,2,1,0:T(8,128)(2,1)} %get-tuple-element.16.theta_hbm), channel_id=1, source_target_pairs={{0,1},{1,0},{2,3},{3,2},{4,5},{5,4},{6,7},{7,6},{8,9},{9,8},{10,11... | collective-permute-start | bytes 786440 | tf_op jit(solution)/shard_map/cond/branch_1_fun/ppermute | solution.py:434
  5.8 1.4 %collective-permute-done.3.other_ref = bf16[1,8,128,128]{3,2,1,0:T(8,128)(2,1)S(1)} collective-permute-done((bf16[1,8,128,128]{3,2,1,0:T(8,128)(2,1)}, bf16[1,8,128,128]{3,2,1,0:T(8,128)(2,1)S(1)}, u32[]{:S(2)}, u32[]{:S(2)}) %collective-permute-start.3) | collective-permute-done | bytes 262176 | tf_op jit(solution)/shard_map/cond/branch_1_fun/ppermute | solution.py:434
  7.2 1.0 %pick.3 = (bf16[2,2,128,128]{3,2,1,0:T(8,128)(2,1)S(1)}, bf16[2,2,128,128]{3,2,1,0:T(8,128)(2,1)S(1)}, bf16[2,2,128,128]{3,2,1,0:T(8,128)(2,1)S(1)}, bf16[2,2,128,128]{3,2,1,0:T(8,128)(2,1)S(1)}) custom-call(s32[3,32]{1,0:T(4,128)} %get-tuple-element.15.info_hbm, bf16[1,8,128,128]{3,2,1,0:T(8,128)(2,1)} %get-tuple-element.16.theta_hbm, ...), custom_call_target="tpu_custom_call" | custom-call | bytes 33554432 | tf_op jit(solution)/shard_map/cond/branch_1_fun/pick/pallas_call | solution.py:462
  8.2 1.3 %collective-permute-start.5 = (bf16[2,2,128,128]{3,2,1,0:T(8,128)(2,1)S(1)}, bf16[2,2,128,128]{3,2,1,0:T(8,128)(2,1)S(1)}, u32[]{:S(2)}, u32[]{:S(2)}) collective-permute-start(bf16[2,2,128,128]{3,2,1,0:T(8,128)(2,1)S(1)} %get-tuple-element.44), channel_id=1, source_target_pairs={{0,2},{1,3},{2,0},{3,1},{4,6},{5,7},{6,4},{7,5},{8,10},{9,11},{10,... | collective-permute-start | bytes 393224 | tf_op jit(solution)/shard_map/ppermute | solution.py:434
  9.5 0.0 collective-permute-start.6
  9.5 1.4 %collective-permute-start.7 = (bf16[2,2,128,128]{3,2,1,0:T(8,128)(2,1)S(1)}, bf16[2,2,128,128]{3,2,1,0:T(8,128)(2,1)S(1)}, u32[]{:S(2)}, u32[]{:S(2)}) collective-permute-start(bf16[2,2,128,128]{3,2,1,0:T(8,128)(2,1)S(1)} %get-tuple-element.46), channel_id=1, source_target_pairs={{0,6},{1,7},{2,4},{3,5},{4,2},{5,3},{6,0},{7,1},{8,14},{9,15},{10,... | collective-permute-start | bytes 393224 | tf_op jit(solution)/shard_map/ppermute | solution.py:434
  10.9 2.3 %prepare.1 = (bf16[2,128,128]{2,1,0:T(8,128)(2,1)S(1)}, f32[2,128,128]{2,1,0:T(8,128)S(1)}, f32[8,128]{1,0:T(8,128)S(1)}, s32[24]{0:T(128)S(1)}, s32[16]{0:T(128)S(1)}) custom-call(s32[3,32]{1,0:T(4,128)} %info_hbm.1, s32[16]{0:T(128)} %count_hbm.1, s32[8]{0:T(128)} %size_hbm.1, f32[1,128]{1,0:T(1,128)} %fields_hbm.1, bf16[1024,128]{1,0:T(8,128)(2,1)} %trial_ref.1, ...), custom_call_target="tpu_custom_call" | custom-call | bytes 33554432 | tf_op jit(solution)/shard_map/prepare/pallas_call | solution.py:466
  13.2 0.0 collective-permute-done.4.theta_ref
  13.2 0.0 slice-start.1
  13.2 0.6 spread.1
  13.8 0.0 collective-permute-done.5.refs_1_
  13.8 0.7 collective-permute-done.6.refs_2_
  14.5 3.6 %collective-permute-done.7.refs_3_ = bf16[2,2,128,128]{3,2,1,0:T(8,128)(2,1)S(1)} collective-permute-done((bf16[2,2,128,128]{3,2,1,0:T(8,128)(2,1)S(1)}, bf16[2,2,128,128]{3,2,1,0:T(8,128)(2,1)S(1)}, u32[]{:S(2)}, u32[]{:S(2)}) %collective-permute-start.7) | collective-permute-done | bytes 131104 | tf_op jit(solution)/shard_map/ppermute | solution.py:434
  18.1 12.1 %all_to_all.15.far_ref = bf16[8,2,128,128]{3,2,1,0:T(8,128)(2,1)S(1)} all-to-all(bf16[8,2,128,128]{3,2,1,0:T(8,128)(2,1)S(1)} %spread.1), channel_id=1, replica_groups={{1,0,3,2,5,4,7,6},{9,8,11,10,13,12,15,14},{17,16,19,18,21,20,23,22},{25..., dimensions={0} | all-to-all | bytes 1048576 | tf_op jit(solution)/shard_map/all_to_all | solution.py:437
  30.2 0.0 slice-done
  30.2 0.0 slice-done.1
  30.2 2.6 %bias.1 = f32[16,16,128]{2,1,0:T(8,128)S(1)} custom-call(bf16[2,128,128]{2,1,0:T(8,128)(2,1)S(1)} %get-tuple-element.39.rows_ref, f32[2,128,128]{2,1,0:T(8,128)S(1)} %get-tuple-element.40.mask_ref, f32[8,128]{1,0:T(8,128)S(1)} %get-tuple-element.41.draws_ref.fields_ref, bf16[2,128,16384]{2,1,0:T(8,128)(2,1)S(1)} %bitcast.3, ...), custom_call_target="tpu_custom_call" | custom-call | tf_op jit(solution)/shard_map/bias/pallas_call | solution.py:502
  32.8 10.7 %all_to_all.16.shift_ref = f32[16,16,128]{2,1,0:T(8,128)S(1)} all-to-all(f32[16,16,128]{2,1,0:T(8,128)S(1)} %bias.1), channel_id=1, replica_groups={{3,2,7,6,11,10,15,14,13,12,9,8,5,4,1,0},{19,18,23,22,27,26,31,30,29,28,..., dimensions={0} | all-to-all | bytes 262144 | tf_op jit(solution)/shard_map/all_to_all | solution.py:437
  43.4 1.3 %operator.1 = (bf16[16,1,2,128,128]{4,3,2,1,0:T(8,128)(2,1)S(1)}, f32[8,128]{1,0:T(8,128)S(1)}) custom-call(f32[16,16,128]{2,1,0:T(8,128)S(1)} %all_to_all.16.shift_ref, f32[8,128]{1,0:T(8,128)S(1)} %get-tuple-element.41.draws_ref.fields_ref, f32[2,128,128]{2,1,0:T(8,128)S(1)} %get-tuple-element.40.mask_ref, bf16[2,128,16384]{2,1,0:T(8,128)(2,1)S(1)} %bitcast.3), custom_call_target="tpu_custom_call" | custom-call | tf_op jit(solution)/shard_map/operator/pallas_call | solution.py:512
  44.8 27.8 %all_to_all.17.oper_ref = bf16[16,1,2,128,128]{4,3,2,1,0:T(8,128)(2,1)S(1)} all-to-all(bf16[16,1,2,128,128]{4,3,2,1,0:T(8,128)(2,1)S(1)} %get-tuple-element.52), channel_id=1, replica_groups={{3,12,7,8,11,4,15,0,13,2,9,6,5,10,1,14},{19,28,23,24,27,20,31,16,29,18,..., dimensions={0} | all-to-all | bytes 2097152 | tf_op jit(solution)/shard_map/all_to_all | solution.py:437
  72.6 0.0 copy-done
  72.6 1.6 %update.1 = (bf16[1,8,128,128]{3,2,1,0:T(8,128)(2,1)}, f32[1,128]{1,0:T(1,128)}) custom-call(s32[24]{0:T(128)S(1)} %get-tuple-element.38.where_ref, bf16[1,8,128,128]{3,2,1,0:T(8,128)(2,1)S(1)} %bitcast.7, bf16[16,1,2,128,128]{4,3,2,1,0:T(8,128)(2,1)S(1)} %all_to_all.17.oper_ref, f32[8,128]{1,0:T(8,128)S(1)} %get-tuple-element.53.bias_ref), custom_call_target="tpu_custom_call" | custom-call | tf_op jit(solution)/shard_map/update/pallas_call | solution.py:525
  (3 shorter events, 0.0 us)
Async XLA Ops:
  0.6 12.5 %collective-permute-start.4 = (bf16[1,8,128,128]{3,2,1,0:T(8,128)(2,1)}, bf16[1,8,128,128]{3,2,1,0:T(8,128)(2,1)S(1)}, u32[]{:S(2)}, u32[]{:S(2)}) collective-permute-start(bf16[1,8,128,128]{3,2,1,0:T(8,128)(2,1)} %bitcast.4), channel_id=1, source_target_pairs={{0,12},{1,13},{2,14},{3,15},{4,8},{5,9},{6,10},{7,11},{8,4},{9,5},... | collective-permute-start | bytes 786440 | tf_op jit(solution)/shard_map/ppermute | solution.py:434
  4.8 2.3 %collective-permute-start.3 = (bf16[1,8,128,128]{3,2,1,0:T(8,128)(2,1)}, bf16[1,8,128,128]{3,2,1,0:T(8,128)(2,1)S(1)}, u32[]{:S(2)}, u32[]{:S(2)}) collective-permute-start(bf16[1,8,128,128]{3,2,1,0:T(8,128)(2,1)} %get-tuple-element.16.theta_hbm), channel_id=1, source_target_pairs={{0,1},{1,0},{2,3},{3,2},{4,5},{5,4},{6,7},{7,6},{8,9},{9,8},{10,11... | collective-permute-start | bytes 786440 | tf_op jit(solution)/shard_map/cond/branch_1_fun/ppermute | solution.py:434
  8.2 5.6 %collective-permute-start.5 = (bf16[2,2,128,128]{3,2,1,0:T(8,128)(2,1)S(1)}, bf16[2,2,128,128]{3,2,1,0:T(8,128)(2,1)S(1)}, u32[]{:S(2)}, u32[]{:S(2)}) collective-permute-start(bf16[2,2,128,128]{3,2,1,0:T(8,128)(2,1)S(1)} %get-tuple-element.44), channel_id=1, source_target_pairs={{0,2},{1,3},{2,0},{3,1},{4,6},{5,7},{6,4},{7,5},{8,10},{9,11},{10,... | collective-permute-start | bytes 393224 | tf_op jit(solution)/shard_map/ppermute | solution.py:434
  9.5 5.0 %collective-permute-start.6 = (bf16[2,2,128,128]{3,2,1,0:T(8,128)(2,1)S(1)}, bf16[2,2,128,128]{3,2,1,0:T(8,128)(2,1)S(1)}, u32[]{:S(2)}, u32[]{:S(2)}) collective-permute-start(bf16[2,2,128,128]{3,2,1,0:T(8,128)(2,1)S(1)} %get-tuple-element.45), channel_id=1, source_target_pairs={{0,4},{1,5},{2,6},{3,7},{4,0},{5,1},{6,2},{7,3},{8,12},{9,13},{10,... | collective-permute-start | bytes 393224 | tf_op jit(solution)/shard_map/ppermute | solution.py:434
  9.5 20.7 %slice-start = ((s8[8388608]{0:T(1024)(128)(4,1)}), s8[4194304]{0:T(1024)(128)(4,1)S(1)}, s32[]{:S(2)}) async-start(s8[8388608]{0:T(1024)(128)(4,1)} %bitcast.2), calls=%async_computation.3 | async-start | bytes 8388608
  9.5 8.6 %collective-permute-start.7 = (bf16[2,2,128,128]{3,2,1,0:T(8,128)(2,1)S(1)}, bf16[2,2,128,128]{3,2,1,0:T(8,128)(2,1)S(1)}, u32[]{:S(2)}, u32[]{:S(2)}) collective-permute-start(bf16[2,2,128,128]{3,2,1,0:T(8,128)(2,1)S(1)} %get-tuple-element.46), channel_id=1, source_target_pairs={{0,6},{1,7},{2,4},{3,5},{4,2},{5,3},{6,0},{7,1},{8,14},{9,15},{10,... | collective-permute-start | bytes 393224 | tf_op jit(solution)/shard_map/ppermute | solution.py:434
  13.2 17.0 %slice-start.1 = ((s8[8388608]{0:T(1024)(128)(4,1)}), s8[4194304]{0:T(1024)(128)(4,1)S(1)}, s32[]{:S(2)}) async-start(s8[8388608]{0:T(1024)(128)(4,1)} %bitcast.2), calls=%async_computation.4 | async-start | bytes 8388608
  30.2 42.4 %copy-start = (bf16[1,1024,128]{2,1,0:T(8,128)(2,1)S(1)}, bf16[1,1024,128]{2,1,0:T(8,128)(2,1)}, u32[]{:S(2)}) copy-start(bf16[1,1024,128]{2,1,0:T(8,128)(2,1)} %param.9) | copy-start | bytes 786436

commit v10 on v9

--- a/solution.py
+++ b/solution.py
@@ -394,13 +394,13 @@
     own = total_ref[pl.ds(me, 1), :]
     own_ref[...] = jnp.broadcast_to(-own, own_ref.shape)
     total_ref[pl.ds(me, 1), :] = own + fields_ref[0:1, :]
-    left = total_ref[...].astype(BF16)
+    left = (total_ref[...] * STEP_ROOT).astype(BF16)
     per = bs // PIECES
     pitch = bs + 8
     for slot in range(slots):
         for c in range(PIECES):
             right = chol_ref[slot, :, pl.ds(c * per * bs, per * bs)]
-            oper = jnp.dot(left, right, preferred_element_type=F32) * STEP_ROOT
+            oper = jnp.dot(left, right, preferred_element_type=F32)
             for p in range(per):
                 oper_ref[slot, pl.ds(c * per + p, walkers, stride=pitch), :] = oper[:, p * bs : (p + 1) * bs]
         for w in range(walkers):

time: 74.9 us -> 74.9 us (level)
  no operation moved by 1% of the time
where the time goes in v10:
time: 74.9 us; the launch traced here: 74.2 us
  blocking collectives  50.6 us (68%)
  Pallas kernels  9.36 us (12%)
  starting transfers between devices  7.88 us (11%)
  waiting for transfers between devices  5.68 us (8%)
    all_to_all x3, blocking collectives, to_all(): lax.all_to_all(x, 'blk', split_axis=0, concat_axis=0, tiled=True, axis_in...  50.6 us
    ppermute x5, starting transfers between devices, swap(): return lax.ppermute(x, 'blk', [(i, i ^ step) for i in range(owners)])  7.88 us
    ppermute x5, waiting for transfers between devices, swap(): return lax.ppermute(x, 'blk', [(i, i ^ step) for i in range(owners)])  5.68 us
    pallas_call x1, Pallas kernels, short_axis(): pl.pallas_call(functools.partial(bias_pair_kernel, step, ring, near_ring)...  2.57 us
    pallas_call x1, Pallas kernels, short_axis(): pl.pallas_call(functools.partial(prepare_kernel, place, near_ring), out_s...  2.26 us
    pallas_call x1, Pallas kernels, short_axis(): pl.pallas_call(update_pair_kernel, out_shape=(jax.ShapeDtypeStruct(theta_...  1.59 us
  transfers between devices with their start and end apart: 5, of which 3 were waited for; matrix products, arithmetic and copies ran while one was open for 0% of the time, Pallas kernels for 5%

profile of v10, /device:TPU:1, one launch (start us, length us, event | category | flops | bytes accessed | tf_op | source)
XLA Modules:
  0.0 74.2 jit_solution(15287850104063851701)
XLA Ops:
  0.6 4.2 %collective-permute-start.4 = (bf16[1,8,128,128]{3,2,1,0:T(8,128)(2,1)}, bf16[1,8,128,128]{3,2,1,0:T(8,128)(2,1)S(1)}, u32[]{:S(2)}, u32[]{:S(2)}) collective-permute-start(bf16[1,8,128,128]{3,2,1,0:T(8,128)(2,1)} %bitcast.4), channel_id=1, source_target_pairs={{0,12},{1,13},{2,14},{3,15},{4,8},{5,9},{6,10},{7,11},{8,4},{9,5},... | collective-permute-start | bytes 786440 | tf_op jit(solution)/shard_map/ppermute | solution.py:434
  4.8 3.3 %conditional.1 = ((bf16[2,2,128,128]{3,2,1,0:T(8,128)(2,1)S(1)}, bf16[2,2,128,128]{3,2,1,0:T(8,128)(2,1)S(1)}, bf16[2,2,128,128]{3,2,1,0:T(8,128)(2,1)S(1)}, bf16[2,2,128,128]{3,2,1,0:T(8,128)(2,1)S(1)})) conditional(s32[]{:T(128)} %convert_element_type.3, (bf16[1,8,128,128]{3,2,1,0:T(8,128)(2,1)}, s32[3,32]{1,0:T(4,128)}, ...), branch_computations={%region_0.0_spmd, %region_1.0_spmd} | conditional | bytes 36700288 | solution.py:460
  4.8 1.0 %collective-permute-start.3 = (bf16[1,8,128,128]{3,2,1,0:T(8,128)(2,1)}, bf16[1,8,128,128]{3,2,1,0:T(8,128)(2,1)S(1)}, u32[]{:S(2)}, u32[]{:S(2)}) collective-permute-start(bf16[1,8,128,128]{3,2,1,0:T(8,128)(2,1)} %get-tuple-element.16.theta_hbm), channel_id=1, source_target_pairs={{0,1},{1,0},{2,3},{3,2},{4,5},{5,4},{6,7},{7,6},{8,9},{9,8},{10,11... | collective-permute-start | bytes 786440 | tf_op jit(solution)/shard_map/cond/branch_1_fun/ppermute | solution.py:434
  5.8 1.4 %collective-permute-done.3.other_ref = bf16[1,8,128,128]{3,2,1,0:T(8,128)(2,1)S(1)} collective-permute-done((bf16[1,8,128,128]{3,2,1,0:T(8,128)(2,1)}, bf16[1,8,128,128]{3,2,1,0:T(8,128)(2,1)S(1)}, u32[]{:S(2)}, u32[]{:S(2)}) %collective-permute-start.3) | collective-permute-done | bytes 262176 | tf_op jit(solution)/shard_map/cond/branch_1_fun/ppermute | solution.py:434
  7.2 1.0 %pick.3 = (bf16[2,2,128,128]{3,2,1,0:T(8,128)(2,1)S(1)}, bf16[2,2,128,128]{3,2,1,0:T(8,128)(2,1)S(1)}, bf16[2,2,128,128]{3,2,1,0:T(8,128)(2,1)S(1)}, bf16[2,2,128,128]{3,2,1,0:T(8,128)(2,1)S(1)}) custom-call(s32[3,32]{1,0:T(4,128)} %get-tuple-element.15.info_hbm, bf16[1,8,128,128]{3,2,1,0:T(8,128)(2,1)} %get-tuple-element.16.theta_hbm, ...), custom_call_target="tpu_custom_call" | custom-call | bytes 33554432 | tf_op jit(solution)/shard_map/cond/branch_1_fun/pick/pallas_call | solution.py:462
  8.2 1.3 %collective-permute-start.5 = (bf16[2,2,128,128]{3,2,1,0:T(8,128)(2,1)S(1)}, bf16[2,2,128,128]{3,2,1,0:T(8,128)(2,1)S(1)}, u32[]{:S(2)}, u32[]{:S(2)}) collective-permute-start(bf16[2,2,128,128]{3,2,1,0:T(8,128)(2,1)S(1)} %get-tuple-element.44), channel_id=1, source_target_pairs={{0,2},{1,3},{2,0},{3,1},{4,6},{5,7},{6,4},{7,5},{8,10},{9,11},{10,... | collective-permute-start | bytes 393224 | tf_op jit(solution)/shard_map/ppermute | solution.py:434
  9.5 0.0 collective-permute-start.6
  9.5 1.4 %collective-permute-start.7 = (bf16[2,2,128,128]{3,2,1,0:T(8,128)(2,1)S(1)}, bf16[2,2,128,128]{3,2,1,0:T(8,128)(2,1)S(1)}, u32[]{:S(2)}, u32[]{:S(2)}) collective-permute-start(bf16[2,2,128,128]{3,2,1,0:T(8,128)(2,1)S(1)} %get-tuple-element.46), channel_id=1, source_target_pairs={{0,6},{1,7},{2,4},{3,5},{4,2},{5,3},{6,0},{7,1},{8,14},{9,15},{10,... | collective-permute-start | bytes 393224 | tf_op jit(solution)/shard_map/ppermute | solution.py:434
  10.9 2.3 %prepare.1 = (bf16[2,128,128]{2,1,0:T(8,128)(2,1)S(1)}, f32[2,128,128]{2,1,0:T(8,128)S(1)}, f32[8,128]{1,0:T(8,128)S(1)}, s32[24]{0:T(128)S(1)}, s32[16]{0:T(128)S(1)}) custom-call(s32[3,32]{1,0:T(4,128)} %info_hbm.1, s32[16]{0:T(128)} %count_hbm.1, s32[8]{0:T(128)} %size_hbm.1, f32[1,128]{1,0:T(1,128)} %fields_hbm.1, bf16[1024,128]{1,0:T(8,128)(2,1)} %trial_ref.1, ...), custom_call_target="tpu_custom_call" | custom-call | bytes 33554432 | tf_op jit(solution)/shard_map/prepare/pallas_call | solution.py:466
  13.2 0.0 collective-permute-done.4.theta_ref
  13.2 0.0 slice-start.1
  13.2 0.6 spread.1
  13.8 0.0 collective-permute-done.5.refs_1_
  13.8 0.7 collective-permute-done.6.refs_2_
  14.5 3.6 %collective-permute-done.7.refs_3_ = bf16[2,2,128,128]{3,2,1,0:T(8,128)(2,1)S(1)} collective-permute-done((bf16[2,2,128,128]{3,2,1,0:T(8,128)(2,1)S(1)}, bf16[2,2,128,128]{3,2,1,0:T(8,128)(2,1)S(1)}, u32[]{:S(2)}, u32[]{:S(2)}) %collective-permute-start.7) | collective-permute-done | bytes 131104 | tf_op jit(solution)/shard_map/ppermute | solution.py:434
  18.1 12.1 %all_to_all.15.far_ref = bf16[8,2,128,128]{3,2,1,0:T(8,128)(2,1)S(1)} all-to-all(bf16[8,2,128,128]{3,2,1,0:T(8,128)(2,1)S(1)} %spread.1), channel_id=1, replica_groups={{1,0,3,2,5,4,7,6},{9,8,11,10,13,12,15,14},{17,16,19,18,21,20,23,22},{25..., dimensions={0} | all-to-all | bytes 1048576 | tf_op jit(solution)/shard_map/all_to_all | solution.py:437
  30.2 0.0 slice-done
  30.2 0.0 slice-done.1
  30.2 2.6 %bias.1 = f32[16,16,128]{2,1,0:T(8,128)S(1)} custom-call(bf16[2,128,128]{2,1,0:T(8,128)(2,1)S(1)} %get-tuple-element.39.rows_ref, f32[2,128,128]{2,1,0:T(8,128)S(1)} %get-tuple-element.40.mask_ref, f32[8,128]{1,0:T(8,128)S(1)} %get-tuple-element.41.draws_ref.fields_ref, bf16[2,128,16384]{2,1,0:T(8,128)(2,1)S(1)} %bitcast.3, ...), custom_call_target="tpu_custom_call" | custom-call | tf_op jit(solution)/shard_map/bias/pallas_call | solution.py:502
  32.8 10.7 %all_to_all.16.shift_ref = f32[16,16,128]{2,1,0:T(8,128)S(1)} all-to-all(f32[16,16,128]{2,1,0:T(8,128)S(1)} %bias.1), channel_id=1, replica_groups={{3,2,7,6,11,10,15,14,13,12,9,8,5,4,1,0},{19,18,23,22,27,26,31,30,29,28,..., dimensions={0} | all-to-all | bytes 262144 | tf_op jit(solution)/shard_map/all_to_all | solution.py:437
  43.4 1.4 %operator.1 = (bf16[16,1,2,128,128]{4,3,2,1,0:T(8,128)(2,1)S(1)}, f32[8,128]{1,0:T(8,128)S(1)}) custom-call(f32[16,16,128]{2,1,0:T(8,128)S(1)} %all_to_all.16.shift_ref, f32[8,128]{1,0:T(8,128)S(1)} %get-tuple-element.41.draws_ref.fields_ref, f32[2,128,128]{2,1,0:T(8,128)S(1)} %get-tuple-element.40.mask_ref, bf16[2,128,16384]{2,1,0:T(8,128)(2,1)S(1)} %bitcast.3), custom_call_target="tpu_custom_call" | custom-call | tf_op jit(solution)/shard_map/operator/pallas_call | solution.py:512
  44.8 27.8 %all_to_all.17.oper_ref = bf16[16,1,2,128,128]{4,3,2,1,0:T(8,128)(2,1)S(1)} all-to-all(bf16[16,1,2,128,128]{4,3,2,1,0:T(8,128)(2,1)S(1)} %get-tuple-element.52), channel_id=1, replica_groups={{3,12,7,8,11,4,15,0,13,2,9,6,5,10,1,14},{19,28,23,24,27,20,31,16,29,18,..., dimensions={0} | all-to-all | bytes 2097152 | tf_op jit(solution)/shard_map/all_to_all | solution.py:437
  72.6 0.0 copy-done
  72.6 1.6 %update.1 = (bf16[1,8,128,128]{3,2,1,0:T(8,128)(2,1)}, f32[1,128]{1,0:T(1,128)}) custom-call(s32[24]{0:T(128)S(1)} %get-tuple-element.38.where_ref, bf16[1,8,128,128]{3,2,1,0:T(8,128)(2,1)S(1)} %bitcast.7, bf16[16,1,2,128,128]{4,3,2,1,0:T(8,128)(2,1)S(1)} %all_to_all.17.oper_ref, f32[8,128]{1,0:T(8,128)S(1)} %get-tuple-element.53.bias_ref), custom_call_target="tpu_custom_call" | custom-call | tf_op jit(solution)/shard_map/update/pallas_call | solution.py:525
  (3 shorter events, 0.0 us)
Async XLA Ops:
  0.6 12.5 %collective-permute-start.4 = (bf16[1,8,128,128]{3,2,1,0:T(8,128)(2,1)}, bf16[1,8,128,128]{3,2,1,0:T(8,128)(2,1)S(1)}, u32[]{:S(2)}, u32[]{:S(2)}) collective-permute-start(bf16[1,8,128,128]{3,2,1,0:T(8,128)(2,1)} %bitcast.4), channel_id=1, source_target_pairs={{0,12},{1,13},{2,14},{3,15},{4,8},{5,9},{6,10},{7,11},{8,4},{9,5},... | collective-permute-start | bytes 786440 | tf_op jit(solution)/shard_map/ppermute | solution.py:434
  4.8 2.3 %collective-permute-start.3 = (bf16[1,8,128,128]{3,2,1,0:T(8,128)(2,1)}, bf16[1,8,128,128]{3,2,1,0:T(8,128)(2,1)S(1)}, u32[]{:S(2)}, u32[]{:S(2)}) collective-permute-start(bf16[1,8,128,128]{3,2,1,0:T(8,128)(2,1)} %get-tuple-element.16.theta_hbm), channel_id=1, source_target_pairs={{0,1},{1,0},{2,3},{3,2},{4,5},{5,4},{6,7},{7,6},{8,9},{9,8},{10,11... | collective-permute-start | bytes 786440 | tf_op jit(solution)/shard_map/cond/branch_1_fun/ppermute | solution.py:434
  8.2 5.6 %collective-permute-start.5 = (bf16[2,2,128,128]{3,2,1,0:T(8,128)(2,1)S(1)}, bf16[2,2,128,128]{3,2,1,0:T(8,128)(2,1)S(1)}, u32[]{:S(2)}, u32[]{:S(2)}) collective-permute-start(bf16[2,2,128,128]{3,2,1,0:T(8,128)(2,1)S(1)} %get-tuple-element.44), channel_id=1, source_target_pairs={{0,2},{1,3},{2,0},{3,1},{4,6},{5,7},{6,4},{7,5},{8,10},{9,11},{10,... | collective-permute-start | bytes 393224 | tf_op jit(solution)/shard_map/ppermute | solution.py:434
  9.5 5.0 %collective-permute-start.6 = (bf16[2,2,128,128]{3,2,1,0:T(8,128)(2,1)S(1)}, bf16[2,2,128,128]{3,2,1,0:T(8,128)(2,1)S(1)}, u32[]{:S(2)}, u32[]{:S(2)}) collective-permute-start(bf16[2,2,128,128]{3,2,1,0:T(8,128)(2,1)S(1)} %get-tuple-element.45), channel_id=1, source_target_pairs={{0,4},{1,5},{2,6},{3,7},{4,0},{5,1},{6,2},{7,3},{8,12},{9,13},{10,... | collective-permute-start | bytes 393224 | tf_op jit(solution)/shard_map/ppermute | solution.py:434
  9.5 20.7 %slice-start = ((s8[8388608]{0:T(1024)(128)(4,1)}), s8[4194304]{0:T(1024)(128)(4,1)S(1)}, s32[]{:S(2)}) async-start(s8[8388608]{0:T(1024)(128)(4,1)} %bitcast.2), calls=%async_computation.3 | async-start | bytes 8388608
  9.5 8.6 %collective-permute-start.7 = (bf16[2,2,128,128]{3,2,1,0:T(8,128)(2,1)S(1)}, bf16[2,2,128,128]{3,2,1,0:T(8,128)(2,1)S(1)}, u32[]{:S(2)}, u32[]{:S(2)}) collective-permute-start(bf16[2,2,128,128]{3,2,1,0:T(8,128)(2,1)S(1)} %get-tuple-element.46), channel_id=1, source_target_pairs={{0,6},{1,7},{2,4},{3,5},{4,2},{5,3},{6,0},{7,1},{8,14},{9,15},{10,... | collective-permute-start | bytes 393224 | tf_op jit(solution)/shard_map/ppermute | solution.py:434
  13.2 17.0 %slice-start.1 = ((s8[8388608]{0:T(1024)(128)(4,1)}), s8[4194304]{0:T(1024)(128)(4,1)S(1)}, s32[]{:S(2)}) async-start(s8[8388608]{0:T(1024)(128)(4,1)} %bitcast.2), calls=%async_computation.4 | async-start | bytes 8388608
  30.2 42.5 %copy-start = (bf16[1,1024,128]{2,1,0:T(8,128)(2,1)S(1)}, bf16[1,1024,128]{2,1,0:T(8,128)(2,1)}, u32[]{:S(2)}) copy-start(bf16[1,1024,128]{2,1,0:T(8,128)(2,1)} %param.9) | copy-start | bytes 786436
